TPU v7x, 32 devices: a whole 2x2x4 slice. The times are simulated.
32 devices in a mesh: dp: 4 (over y, x), shard: 8 (over z, core).
Axes of the slice: x: 2, y: 2, z: 4, core: 2. Of those that a mesh axis runs over, the one named last changes fastest.
Arguments:
- tokens: bfloat16 [8192, 1600], P(('dp', 'shard')), may hold values from -6 to 6
- cotangent: bfloat16 [8192, 1600], P(('dp', 'shard')), may hold values from -6 to 6
- lengths: int32 [32, 2], P(('dp', 'shard')), may hold values from 0 to 256, as said below
- step_count: int32 [1], replicated, may hold values from 1 to 20
- norm_gains: bfloat16 [1600, 4], P('shard'), may hold values from 0.5 to 1.5
- qkv_weight: bfloat16 [1600, 2240], P('shard', 'dp'), may hold values from -0.15625 to 0.15625
- attn_weight: bfloat16 [1600, 1600], P('shard', 'dp'), may hold values from -0.15625 to 0.15625
- mixer_in: bfloat16 [1600, 6400], P('shard', 'dp'), may hold values from -0.15625 to 0.15625
- mixer_table: bfloat16 [3200, 255], P('shard'), may hold values from -7 to 3
- mixer_out: bfloat16 [3200, 1600], P('shard', 'dp'), may hold values from -0.109375 to 0.109375
- ffn_in: bfloat16 [1600, 11008], P('shard', 'dp'), may hold values from -0.15625 to 0.15625
- ffn_out: bfloat16 [5504, 1600], P('shard', 'dp'), may hold values from -0.078125 to 0.078125
- first_gains: float32 [1600, 4], P('shard'), may hold values from -16 to 16
- first_qkv: float32 [1600, 2240], P('shard', 'dp'), may hold values from -16 to 16
- first_attn: float32 [1600, 1600], P('shard', 'dp'), may hold values from -16 to 16
- first_mixin: float32 [1600, 6400], P('shard', 'dp'), may hold values from -16 to 16
- first_table: float32 [3200, 255], P('shard'), may hold values from -16 to 16
- first_mixout: float32 [3200, 1600], P('shard', 'dp'), may hold values from -16 to 16
- first_ffnin: float32 [1600, 11008], P('shard', 'dp'), may hold values from -16 to 16
- first_ffnout: float32 [5504, 1600], P('shard', 'dp'), may hold values from -16 to 16
- second_gains: float32 [1600, 4], P('shard'), may hold values from 20 to 500
- second_qkv: float32 [1600, 2240], P('shard', 'dp'), may hold values from 20 to 500
- second_attn: float32 [1600, 1600], P('shard', 'dp'), may hold values from 20 to 500
- second_mixin: float32 [1600, 6400], P('shard', 'dp'), may hold values from 20 to 500
- second_table: float32 [3200, 255], P('shard'), may hold values from 20 to 500
- second_mixout: float32 [3200, 1600], P('shard', 'dp'), may hold values from 20 to 500
- second_ffnin: float32 [1600, 11008], P('shard', 'dp'), may hold values from 20 to 500
- second_ffnout: float32 [5504, 1600], P('shard', 'dp'), may hold values from 20 to 500
Outputs:
- output: bfloat16 [8192, 1600], P(('dp', 'shard'))
- grad_tokens: float32 [8192, 1600], P(('dp', 'shard'))
- grad_gains: float32 [1600, 4], P('shard')
- grad_qkv: float32 [1600, 2240], P('shard', 'dp')
- grad_attn: float32 [1600, 1600], P('shard', 'dp')
- grad_mixin: float32 [1600, 6400], P('shard', 'dp')
- grad_table: float32 [3200, 255], P('shard')
- grad_mixout: float32 [3200, 1600], P('shard', 'dp')
- grad_ffnin: float32 [1600, 11008], P('shard', 'dp')
- grad_ffnout: float32 [5504, 1600], P('shard', 'dp')
- mean_gains: float32 [1600, 4], P('shard')
- mean_qkv: float32 [1600, 2240], P('shard', 'dp')
- mean_attn: float32 [1600, 1600], P('shard', 'dp')
- mean_mixin: float32 [1600, 6400], P('shard', 'dp')
- mean_table: float32 [3200, 255], P('shard')
- mean_mixout: float32 [3200, 1600], P('shard', 'dp')
- mean_ffnin: float32 [1600, 11008], P('shard', 'dp')
- mean_ffnout: float32 [5504, 1600], P('shard', 'dp')
- square_gains: float32 [1600, 4], P('shard')
- square_qkv: float32 [1600, 2240], P('shard', 'dp')
- square_attn: float32 [1600, 1600], P('shard', 'dp')
- square_mixin: float32 [1600, 6400], P('shard', 'dp')
- square_table: float32 [3200, 255], P('shard')
- square_mixout: float32 [3200, 1600], P('shard', 'dp')
- square_ffnin: float32 [1600, 11008], P('shard', 'dp')
- square_ffnout: float32 [5504, 1600], P('shard', 'dp')
- delta_gains: float32 [1600, 4], P('shard')
- delta_qkv: float32 [1600, 2240], P('shard', 'dp')
- delta_attn: float32 [1600, 1600], P('shard', 'dp')
- delta_mixin: float32 [1600, 6400], P('shard', 'dp')
- delta_table: float32 [3200, 255], P('shard')
- delta_mixout: float32 [3200, 1600], P('shard', 'dp')
- delta_ffnin: float32 [1600, 11008], P('shard', 'dp')
- delta_ffnout: float32 [5504, 1600], P('shard', 'dp')
Inputs may be any that keep to these rules, and one draw needn't show every extreme that they name: Row i lists the lengths of buffer i's sequences in order, zeros after the last; each sequence is padded to whole blocks of 128 rows and a row's blocks add up to at most 2. In every draw some row holds one sequence of 256 rows.
All inputs are finite; a program needn't handle non-finite values.
Results may differ from a plain program's by a relative error of at most 0.014.
Values may be sent and summed in bfloat16 or wider, within the bound.
A program may use at most 512 MiB of HBM per device.

v0:
```python
import jax
import jax.numpy as jnp
from jax import lax
from jax.sharding import PartitionSpec as P

KV = 5
HEAD = 64
GROUP = 5
INNER = 3200
STATE = 16
CONV = 4
RANK = 100
FF = 5504
BLOCK = 128
SUB = 16


epsilon = 1e-06
beta_first = 0.9
beta_second = 0.95
adam_floor = 1e-08
learn_rate = 0.01
weight_decay = 0.1
masked_score = -1e30


def product(left, right):
    return jnp.dot(left, right, preferred_element_type=jnp.float32)


def product_tn(left, right):
    return lax.dot_general(
        left, right, (((0,), (0,)), ((), ())), preferred_element_type=jnp.float32
    )


def product_nt(left, right):
    return lax.dot_general(
        left, right, (((1,), (1,)), ((), ())), preferred_element_type=jnp.float32
    )


def sigmoid(values):
    return 1.0 / (1.0 + jnp.exp(-values))


def silu_act(values):
    return values / (1.0 + jnp.exp(-values))


def silu_slope(values):
    gate_sig = sigmoid(values)
    return gate_sig * (1.0 + values * (1.0 - gate_sig))


def rms_scale(values):
    return lax.rsqrt(jnp.mean(values * values, axis=-1, keepdims=True) + epsilon)


def rms_back(values, scale, gain, incoming):
    weighted = incoming * gain
    inner_mean = jnp.mean(weighted * values, axis=-1, keepdims=True)
    return (
        scale * weighted - values * (scale * scale * scale) * inner_mean,
        jnp.sum(incoming * values * scale, axis=0),
    )


def shift_rows(values, lag):
    if lag == 0:
        return values
    return jnp.concatenate(
        [jnp.zeros((lag, values.shape[1]), values.dtype), values[: values.shape[0] - lag]], axis=0
    )


def unshift_rows(values, lag):
    if lag == 0:
        return values
    return jnp.concatenate([values[lag:], jnp.zeros((lag, values.shape[1]), values.dtype)], axis=0)


def layout(row, buffer_rows):
    index = jnp.arange(row.shape[0], dtype=jnp.int32)
    count_blocks = (row + (BLOCK - 1)) // BLOCK
    first_block = jnp.cumsum(count_blocks) - count_blocks
    places = jnp.arange(buffer_rows, dtype=jnp.int32)
    owner = (
        jnp.sum((first_block[None, :] <= (places // BLOCK)[:, None]).astype(jnp.int32), axis=1) - 1
    )
    pick = (owner[:, None] == index[None, :]).astype(jnp.int32)
    seq_length = jnp.sum(pick * row[None, :], axis=1)
    offset = places - BLOCK * jnp.sum(pick * first_block[None, :], axis=1)
    live = offset < seq_length
    begins = live & (offset == 0)
    allowed = (owner[:, None] == owner[None, :]) & (places[None, :] <= places[:, None]) & live[
        None, :
    ] | (places[:, None] == places[None, :])
    return (offset, live.astype(jnp.float32), 1.0 - begins.astype(jnp.float32), allowed)


def combine(early, late):
    return (early[0] * late[0], late[0] * early[1] + late[1])


def states(decay, drive, start):
    cum_decay, cum_drive = lax.associative_scan(combine, (decay, drive), axis=0)
    return cum_decay * start[None] + cum_drive


def adam_update(weight, gradient, first_old, second_old, step_float):
    mean_new = beta_first * first_old + (1.0 - beta_first) * gradient
    square_new = beta_second * second_old + (1.0 - beta_second) * gradient * gradient
    fix_first = 1.0 - jnp.power(beta_first, step_float)
    fix_second = 1.0 - jnp.power(beta_second, step_float)
    delta_new = -learn_rate * (
        mean_new / fix_first / (jnp.sqrt(square_new / fix_second) + adam_floor)
        + weight_decay * weight.astype(jnp.float32)
    )
    return (mean_new, square_new, delta_new)


def shards(
    tokens,
    cotangent,
    lengths,
    step_count,
    norm_gains,
    qkv_weight,
    attn_weight,
    mixer_in,
    mixer_table,
    mixer_out,
    ffn_in,
    ffn_out,
    first_gains,
    first_qkv,
    first_attn,
    first_mixin,
    first_table,
    first_mixout,
    first_ffnin,
    first_ffnout,
    second_gains,
    second_qkv,
    second_attn,
    second_mixin,
    second_table,
    second_mixout,
    second_ffnin,
    second_ffnout,
):
    wide = (
        lax.all_gather(qkv_weight, "dp", axis=1, tiled=True),
        lax.all_gather(attn_weight, "dp", axis=1, tiled=True),
        lax.all_gather(mixer_in, "dp", axis=1, tiled=True),
        lax.all_gather(mixer_out, "dp", axis=1, tiled=True),
        lax.all_gather(ffn_in, "dp", axis=1, tiled=True),
        lax.all_gather(ffn_out, "dp", axis=1, tiled=True),
    )
    gathered = (
        lax.all_gather(norm_gains, "shard", axis=0, tiled=True),
        lax.all_gather(wide[0], "shard", axis=0, tiled=True),
        lax.all_gather(wide[1], "shard", axis=0, tiled=True),
        lax.all_gather(wide[2], "shard", axis=0, tiled=True),
        lax.all_gather(mixer_table, "shard", axis=0, tiled=True),
        lax.all_gather(wide[3], "shard", axis=0, tiled=True),
        lax.all_gather(wide[4], "shard", axis=0, tiled=True),
        lax.all_gather(wide[5], "shard", axis=0, tiled=True),
    )
    gain_low, weight_qkv, weight_attn, weight_in, table_low, weight_mix, weight_up, weight_down = (
        gathered
    )
    buffer_rows = tokens.shape[0]
    model_width = tokens.shape[1]
    offset, live_rows, keep_rows, allowed = layout(lengths[0], buffer_rows)
    gain_cols = gain_low.astype(jnp.float32)
    inputs = tokens.astype(jnp.float32)
    scale_in = rms_scale(inputs)
    normed = (inputs * scale_in * gain_cols[:, 0]).astype(jnp.bfloat16)
    heads_low = product(normed, weight_qkv).astype(jnp.bfloat16)
    kv_width = KV * HEAD
    query = heads_low[:, :model_width].reshape(buffer_rows, KV, GROUP, HEAD)
    key_rows = heads_low[:, model_width : model_width + kv_width].reshape(buffer_rows, KV, HEAD)
    value_rows = heads_low[:, model_width + kv_width :].reshape(buffer_rows, KV, HEAD)
    factor = HEAD ** (-0.5)

    def masked_scores():
        raw_scores = (
            jnp.einsum("qkgd,skd->kgqs", query, key_rows, preferred_element_type=jnp.float32)
            * factor
        )
        return jnp.where(allowed, raw_scores, masked_score)

    scores = masked_scores()
    top_score = jnp.max(scores, axis=-1, keepdims=True)
    log_total = top_score + jnp.log(jnp.sum(jnp.exp(scores - top_score), axis=-1, keepdims=True))
    probs_low = jnp.exp(scores - log_total).astype(jnp.bfloat16)
    context = (
        jnp.einsum("kgqs,skd->qkgd", probs_low, value_rows, preferred_element_type=jnp.float32)
        .reshape(buffer_rows, model_width)
        .astype(jnp.bfloat16)
    )
    attn_raw = product(context, weight_attn)
    scale_attn = rms_scale(attn_raw)
    mixed = product(normed, weight_in)
    xin = mixed[:, :INNER]
    gate_z = mixed[:, INNER:]
    table = table_low.astype(jnp.float32)
    tap_masks = [(offset >= lag).astype(jnp.float32)[:, None] for lag in range(CONV)]
    taps = [shift_rows(xin, lag) * tap_masks[lag] for lag in range(CONV)]
    conv_pre = table[:, CONV]
    for lag in range(CONV):
        conv_pre = conv_pre + table[:, lag] * taps[lag]
    conv_low = silu_act(conv_pre).astype(jnp.bfloat16)
    conv_out = conv_low.astype(jnp.float32)
    proj_start = CONV + 3 + STATE
    input_proj = table_low[:, proj_start : proj_start + RANK + 2 * STATE]
    step_proj = table_low[:, proj_start + RANK + 2 * STATE :]
    double = product(conv_low, input_proj)
    rank_part = double[:, :RANK].astype(jnp.bfloat16)
    inject = double[:, RANK : RANK + STATE]
    readout = double[:, RANK + STATE :]
    dt_pre = product_nt(rank_part, step_proj) + table[:, CONV + 1]
    step_size = jnp.log1p(jnp.exp(dt_pre))
    rates = -jnp.exp(table[:, CONV + 3 : CONV + 3 + STATE]).T
    block_count = buffer_rows // SUB

    def split(values):
        return values.reshape((block_count, SUB) + values.shape[1:])

    live_blocks = jnp.max(split(live_rows), axis=1) > 0.0
    scan_items = (
        split(step_size),
        split(conv_out),
        split(inject),
        split(readout),
        split(keep_rows),
        live_blocks,
    )

    def block_inputs(item):
        decay = jnp.exp(item[0][:, None, :] * rates[None]) * item[4][:, None, None]
        drive = (item[0] * item[1])[:, None, :] * item[2][:, :, None]
        return (decay, drive)

    def run_block(start, item):
        decay, drive = block_inputs(item)
        history = states(decay, drive, start)
        return (history[-1], (jnp.sum(history * item[3][:, :, None], axis=1), start))

    def forward_step(start, item):
        return run_block(start, item)

    final_state, (block_out, block_starts) = lax.scan(
        forward_step, jnp.zeros((STATE, INNER), jnp.float32), scan_items
    )
    skip_weight = table[:, CONV + 2]
    scanned = block_out.reshape(buffer_rows, INNER) + skip_weight * conv_out
    silu_z = silu_act(gate_z)
    gated_low = (scanned * silu_z).astype(jnp.bfloat16)
    mamba_raw = product(gated_low, weight_mix)
    scale_mamba = rms_scale(mamba_raw)
    hidden = inputs + 0.5 * (
        attn_raw * scale_attn * gain_cols[:, 1] + mamba_raw * scale_mamba * gain_cols[:, 2]
    )
    scale_hidden = rms_scale(hidden)
    normed_two = (hidden * scale_hidden * gain_cols[:, 3]).astype(jnp.bfloat16)
    both = product(normed_two, weight_up)
    gate_ffn = both[:, :FF]
    up_ffn = both[:, FF:]
    act_low = (silu_act(gate_ffn) * up_ffn).astype(jnp.bfloat16)
    ffn_raw = product(act_low, weight_down)
    output = (live_rows[:, None] * (hidden + ffn_raw)).astype(jnp.bfloat16)
    grad_out = cotangent.astype(jnp.float32) * live_rows[:, None]
    grad_ffn = grad_out.astype(jnp.bfloat16)
    grad_down_w = product_tn(act_low, grad_ffn)
    grad_act = product_nt(grad_ffn, weight_down)
    gate_sig = sigmoid(gate_ffn)
    grad_gate = grad_act * up_ffn * gate_sig * (1.0 + gate_ffn * (1.0 - gate_sig))
    grad_up = grad_act * silu_act(gate_ffn)
    grad_both = jnp.concatenate([grad_gate, grad_up], axis=1).astype(jnp.bfloat16)
    grad_up_w = product_tn(normed_two, grad_both)
    grad_second = product_nt(grad_both, weight_up)
    back_hidden, gain_three = rms_back(hidden, scale_hidden, gain_cols[:, 3], grad_second)
    grad_hidden = grad_out + back_hidden
    ffn_part = (
        lax.psum_scatter(grad_up_w, "shard", scatter_dimension=0, tiled=True),
        lax.psum_scatter(grad_down_w, "shard", scatter_dimension=0, tiled=True),
    )
    ffn_done = (
        lax.psum_scatter(ffn_part[0], "dp", scatter_dimension=1, tiled=True),
        lax.psum_scatter(ffn_part[1], "dp", scatter_dimension=1, tiled=True),
    )
    half_grad = 0.5 * grad_hidden
    grad_attn_full, gain_one = rms_back(attn_raw, scale_attn, gain_cols[:, 1], half_grad)
    grad_attn_low = grad_attn_full.astype(jnp.bfloat16)
    grad_attn_w = product_tn(context, grad_attn_low)
    grad_context = (
        product_nt(grad_attn_low, weight_attn)
        .astype(jnp.bfloat16)
        .reshape(buffer_rows, KV, GROUP, HEAD)
    )
    probs_again = jnp.exp(masked_scores() - log_total)
    grad_probs = jnp.einsum(
        "qkgd,skd->kgqs", grad_context, value_rows, preferred_element_type=jnp.float32
    )
    grad_values = jnp.einsum(
        "kgqs,qkgd->skd",
        probs_again.astype(jnp.bfloat16),
        grad_context,
        preferred_element_type=jnp.float32,
    )
    grad_scores = (
        probs_again * (grad_probs - jnp.sum(probs_again * grad_probs, axis=-1, keepdims=True))
    ).astype(jnp.bfloat16)
    grad_query = (
        jnp.einsum("kgqs,skd->qkgd", grad_scores, key_rows, preferred_element_type=jnp.float32)
        * factor
    )
    grad_keys = (
        jnp.einsum("kgqs,qkgd->skd", grad_scores, query, preferred_element_type=jnp.float32)
        * factor
    )
    grad_heads = jnp.concatenate(
        [
            grad_query.reshape(buffer_rows, model_width),
            grad_keys.reshape(buffer_rows, kv_width),
            grad_values.reshape(buffer_rows, kv_width),
        ],
        axis=1,
    ).astype(jnp.bfloat16)
    grad_qkv_w = product_tn(normed, grad_heads)
    grad_normed = product_nt(grad_heads, weight_qkv)
    grad_mamba_full, gain_two = rms_back(mamba_raw, scale_mamba, gain_cols[:, 2], half_grad)
    grad_mamba_low = grad_mamba_full.astype(jnp.bfloat16)
    grad_mix_w = product_tn(gated_low, grad_mamba_low)
    grad_gated = product_nt(grad_mamba_low, weight_mix)
    grad_scanned = grad_gated * silu_z
    grad_gate_z = grad_gated * scanned * silu_slope(gate_z)
    grad_skip = jnp.sum(grad_scanned * conv_out, axis=0)
    back_items = scan_items + (block_starts, split(grad_scanned))

    def back_block(carry, item):
        later, rate_total = carry
        decay, drive = block_inputs(item)
        history = states(decay, drive, item[6])
        before = jnp.concatenate([item[6][None], history[:-1]], axis=0)
        seed = item[3][:, :, None] * item[7][:, None, :]
        seed = seed.at[-1].add(later)
        onward = jnp.concatenate([decay[1:], jnp.zeros_like(decay[:1])], axis=0)
        total = lax.associative_scan(combine, (onward[::-1], seed[::-1]), axis=0)[1][::-1]
        pull = total * before * decay
        drive_sum = jnp.sum(total * item[2][:, :, None], axis=1)
        grad_step_b = jnp.sum(pull * rates[None], axis=1) + drive_sum * item[1]
        grad_input_b = drive_sum * item[0]
        grad_inject_b = jnp.sum(total * (item[0] * item[1])[:, None, :], axis=2)
        grad_readout_b = jnp.sum(history * item[7][:, None, :], axis=2)
        rate_total = rate_total + jnp.sum(pull * item[0][:, None, :], axis=0)
        return (
            (decay[0] * total[0], rate_total),
            (grad_step_b, grad_input_b, grad_inject_b, grad_readout_b),
        )

    def backward_step(carry, item):
        return back_block(carry, item)

    zero_states = jnp.zeros((STATE, INNER), jnp.float32)
    carry_end, back_out = lax.scan(
        backward_step, (zero_states, zero_states), back_items, reverse=True
    )
    grad_step = back_out[0].reshape(buffer_rows, INNER)
    grad_conv_scan = back_out[1].reshape(buffer_rows, INNER)
    grad_inject = back_out[2].reshape(buffer_rows, STATE)
    grad_readout = back_out[3].reshape(buffer_rows, STATE)
    grad_pre = grad_step * sigmoid(dt_pre)
    grad_step_bias = jnp.sum(grad_pre, axis=0)
    grad_pre_low = grad_pre.astype(jnp.bfloat16)
    grad_step_proj = product_tn(grad_pre_low, rank_part)
    grad_rank = product(grad_pre_low, step_proj)
    grad_double = jnp.concatenate([grad_rank, grad_inject, grad_readout], axis=1).astype(
        jnp.bfloat16
    )
    grad_input_proj = product_tn(conv_low, grad_double)
    grad_conv_out = (
        product_nt(grad_double, input_proj) + grad_conv_scan + skip_weight * grad_scanned
    )
    grad_conv = grad_conv_out * silu_slope(conv_pre)
    grad_conv_bias = jnp.sum(grad_conv, axis=0)
    grad_taps = jnp.stack([jnp.sum(grad_conv * taps[lag], axis=0) for lag in range(CONV)], axis=1)
    grad_xin = unshift_rows(grad_conv * tap_masks[0] * table[:, 0], 0)
    for lag in range(1, CONV):
        grad_xin = grad_xin + unshift_rows(grad_conv * tap_masks[lag] * table[:, lag], lag)
    grad_mixed = jnp.concatenate([grad_xin, grad_gate_z], axis=1).astype(jnp.bfloat16)
    grad_in_w = product_tn(normed, grad_mixed)
    grad_normed = grad_normed + product_nt(grad_mixed, weight_in)
    grad_log_rates = (carry_end[1] * rates).T
    grad_table = jnp.concatenate(
        [
            grad_taps,
            grad_conv_bias[:, None],
            grad_step_bias[:, None],
            grad_skip[:, None],
            grad_log_rates,
            grad_input_proj,
            grad_step_proj,
        ],
        axis=1,
    )
    back_inputs, gain_zero = rms_back(inputs, scale_in, gain_cols[:, 0], grad_normed)
    grad_tokens = grad_hidden + back_inputs
    grad_gains = jnp.stack([gain_zero, gain_one, gain_two, gain_three], axis=1)
    mixer_part = (
        lax.psum_scatter(grad_gains, "shard", scatter_dimension=0, tiled=True),
        lax.psum_scatter(grad_qkv_w, "shard", scatter_dimension=0, tiled=True),
        lax.psum_scatter(grad_attn_w, "shard", scatter_dimension=0, tiled=True),
        lax.psum_scatter(grad_in_w, "shard", scatter_dimension=0, tiled=True),
        lax.psum_scatter(grad_table, "shard", scatter_dimension=0, tiled=True),
        lax.psum_scatter(grad_mix_w, "shard", scatter_dimension=0, tiled=True),
    )
    mixer_done = (
        lax.psum_scatter(mixer_part[1], "dp", scatter_dimension=1, tiled=True),
        lax.psum_scatter(mixer_part[2], "dp", scatter_dimension=1, tiled=True),
        lax.psum_scatter(mixer_part[3], "dp", scatter_dimension=1, tiled=True),
        lax.psum_scatter(mixer_part[5], "dp", scatter_dimension=1, tiled=True),
    )
    small_pair = (mixer_part[0], mixer_part[4])
    small_done = lax.psum((small_pair[0], small_pair[1]), "dp")
    owned = (norm_gains, qkv_weight, attn_weight, mixer_in, mixer_table, mixer_out, ffn_in, ffn_out)
    grads_owned = (
        small_done[0],
        mixer_done[0],
        mixer_done[1],
        mixer_done[2],
        small_done[1],
        mixer_done[3],
        ffn_done[0],
        ffn_done[1],
    )
    firsts = (
        first_gains,
        first_qkv,
        first_attn,
        first_mixin,
        first_table,
        first_mixout,
        first_ffnin,
        first_ffnout,
    )
    seconds = (
        second_gains,
        second_qkv,
        second_attn,
        second_mixin,
        second_table,
        second_mixout,
        second_ffnin,
        second_ffnout,
    )
    step_float = step_count[0].astype(jnp.float32)
    updates = [
        adam_update(owned[slot], grads_owned[slot], firsts[slot], seconds[slot], step_float)
        for slot in range(8)
    ]
    means = tuple((entry[0] for entry in updates))
    squares = tuple((entry[1] for entry in updates))
    deltas = tuple((entry[2] for entry in updates))
    return (output, grad_tokens) + grads_owned + means + squares + deltas


def solution(mesh):
    in_specs = (
        P(("dp", "shard"), None),
        P(("dp", "shard"), None),
        P(("dp", "shard"), None),
        P(),
        P("shard", None),
        P("shard", "dp"),
        P("shard", "dp"),
        P("shard", "dp"),
        P("shard", None),
        P("shard", "dp"),
        P("shard", "dp"),
        P("shard", "dp"),
        P("shard", None),
        P("shard", "dp"),
        P("shard", "dp"),
        P("shard", "dp"),
        P("shard", None),
        P("shard", "dp"),
        P("shard", "dp"),
        P("shard", "dp"),
        P("shard", None),
        P("shard", "dp"),
        P("shard", "dp"),
        P("shard", "dp"),
        P("shard", None),
        P("shard", "dp"),
        P("shard", "dp"),
        P("shard", "dp"),
    )
    out_specs = (
        P(("dp", "shard"), None),
        P(("dp", "shard"), None),
        P("shard", None),
        P("shard", "dp"),
        P("shard", "dp"),
        P("shard", "dp"),
        P("shard", None),
        P("shard", "dp"),
        P("shard", "dp"),
        P("shard", "dp"),
        P("shard", None),
        P("shard", "dp"),
        P("shard", "dp"),
        P("shard", "dp"),
        P("shard", None),
        P("shard", "dp"),
        P("shard", "dp"),
        P("shard", "dp"),
        P("shard", None),
        P("shard", "dp"),
        P("shard", "dp"),
        P("shard", "dp"),
        P("shard", None),
        P("shard", "dp"),
        P("shard", "dp"),
        P("shard", "dp"),
        P("shard", None),
        P("shard", "dp"),
        P("shard", "dp"),
        P("shard", "dp"),
        P("shard", None),
        P("shard", "dp"),
        P("shard", "dp"),
        P("shard", "dp"),
    )
    return jax.shard_map(shards, mesh=mesh, in_specs=in_specs, out_specs=out_specs, check_vma=False)
```

profile of v0, /device:TPU:0, one launch (start us, length us, event | category | flops | bytes accessed | tf_op | source)
XLA Modules:
  0.0 7639.2 jit_solution(7139245037745438816)
XLA Ops:
  11.9 20.5 all-gather.1
  66.2 27.8 all-gather.24.cloned.1.call-done
  97.6 53.6 all-gather.36.cloned.1.call-done
  190.9 26.9 all-gather.30.cloned.1.call-done
  222.8 70.8 all-gather.16.cloned.1.call-done
  305.7 45.4 all-gather.18.cloned.1.call-done
  357.6 175.4 %all-gather.22.cloned.1.call-done = bf16[1600,6400]{1,0:T(8,128)(2,1)} async-done(((bf16[200,6400]{1,0:T(8,128)(2,1)}), bf16[1600,6400]{1,0:T(8,128)(2,1)}) %all-gather.22.cloned.1.call-update) | async-done | bytes 20480016 | tf_op jit(solution)/shard_map/all_gather | solution.py:165
  568.9 1689.0 %while.40 = (s32[]{:T(128)}, f32[16,3200]{1,0:T(8,128)}, f32[16,16,3200]{2,1,0:T(8,128)}, f32[16,16,3200]{2,1,0:T(8,128)}, f32[16,16,3200]{2,1,0:T(8,128)}, /*in...) while((s32[]{:T(128)}, f32[16,3200]{1,0:T(8,128)}, ...), condition=%wide.region_10.11_spmd, body=%wide.region_8.10_spmd.sunk | while | flops 15360002 | bytes 184531664 | solution.py:255
  2272.7 20.2 fusion.102
  2307.8 20.1 multiply_reduce_fusion.11
  2354.8 2719.3 %while.41 = (s32[]{:T(128)}, f32[16,3200]{1,0:T(8,128)}, f32[16,3200]{1,0:T(8,128)}, f32[16,16,3200]{2,1,0:T(8,128)}, f32[16,16,3200]{2,1,0:T(8,128)}, /*index=5...) while((s32[]{:T(128)}, f32[16,3200]{1,0:T(8,128)}, ...), condition=%wide.region_23.24_spmd.clone, body=%wide.region_17.23_spmd.clone.sunk | while | flops 33279492 | bytes 415763008 | solution.py:369
  5210.1 28.8 fusion.34
  5241.1 33.6 reduce-scatter.55.cloned.1.call-done
  5277.7 147.2 %reduce-scatter.35.cloned.1.call-done = f32[200,2240]{1,0:T(8,128)} async-done(((f32[1600,2240]{1,0:T(8,128)}), f32[200,2240]{1,0:T(8,128)}) %reduce-scatter.35.cloned.1.call-update) | async-done | bytes 1792016 | tf_op jit(solution)/shard_map/reduce_scatter | solution.py:415
  5428.0 209.0 %reduce-scatter.37.cloned.1.call-done = f32[400,1600]{1,0:T(8,128)} async-done(((f32[3200,1600]{1,0:T(8,128)}), f32[400,1600]{1,0:T(8,128)}) %reduce-scatter.37.cloned.1.call-update) | async-done | bytes 2560016 | tf_op jit(solution)/shard_map/reduce_scatter | solution.py:419
  5641.5 351.9 %reduce-scatter.39.cloned.1.call-done = f32[688,1600]{1,0:T(8,128)} async-done(((f32[5504,1600]{1,0:T(8,128)}), f32[688,1600]{1,0:T(8,128)}) %reduce-scatter.39.cloned.1.call-update) | async-done | bytes 4403216 | tf_op jit(solution)/shard_map/reduce_scatter | solution.py:289
  5999.3 391.0 %reduce-scatter.57.cloned.1.call-done = f32[200,6400]{1,0:T(8,128)} async-done(((f32[1600,6400]{1,0:T(8,128)}), f32[200,6400]{1,0:T(8,128)}) %reduce-scatter.57.cloned.1.call-update) | async-done | bytes 5120016
  6397.2 782.1 %reduce-scatter.59.cloned.1.call-done = f32[200,11008]{1,0:T(8,128)} async-done(((f32[1600,11008]{1,0:T(8,128)}), f32[200,11008]{1,0:T(8,128)}) %reduce-scatter.59.cloned.1.call-update) | async-done | bytes 8806416
  7224.8 34.7 all-reduce.47
  7301.1 21.7 reduce-scatter.41.cloned.1.call-done
  7325.5 45.7 reduce-scatter.49.cloned.1.call-done
  7377.3 56.5 reduce-scatter.53.cloned.1.call-done
  7448.4 61.0 reduce-scatter.45.cloned.1.call-done
  7515.7 107.2 %reduce-scatter.51.cloned.1.call-done = f32[2752,200]{1,0:T(8,128)} async-done(((f32[11008,200]{1,0:T(8,128)}), f32[2752,200]{1,0:T(8,128)}) %reduce-scatter.51.cloned.1.call-update) | async-done | bytes 2201616
  (3959 shorter events, 4882.2 us)
Async XLA Ops:
  8.0 86.1 %all-gather.24.cloned.1.call-start = ((), (), s32[]{:S(2)}) async-start(), calls=%async_computation.17 | async-start | bytes 2048000 | tf_op jit(solution)/shard_map/all_gather | solution.py:157
  10.0 141.3 %all-gather.36.cloned.1.call-start = ((), (), s32[]{:S(2)}) async-start(), calls=%async_computation.27 | async-start | bytes 5632000 | tf_op jit(solution)/shard_map/all_gather | solution.py:158
  10.7 175.3 %all-gather.20.cloned.1.call-start = ((), (), s32[]{:S(2)}) async-start(), calls=%async_computation.15 | async-start | bytes 1843200 | tf_op jit(solution)/shard_map/all_gather | solution.py:166
  11.3 206.5 %all-gather.30.cloned.1.call-start = ((), (), s32[]{:S(2)}) async-start(), calls=%async_computation.20 | async-start | bytes 3072000 | tf_op jit(solution)/shard_map/all_gather | solution.py:159
  11.9 281.7 %all-gather.16.cloned.1.call-start = ((), (), s32[]{:S(2)}) async-start(), calls=%async_computation.13 | async-start | bytes 8294400 | tf_op jit(solution)/shard_map/all_gather | solution.py:163
  34.5 316.7 %all-gather.18.cloned.1.call-start = ((), (), s32[]{:S(2)}) async-start(), calls=%async_computation.14 | async-start | bytes 5990400 | tf_op jit(solution)/shard_map/all_gather | solution.py:164
  54.9 478.1 %all-gather.22.cloned.1.call-start = ((), (), s32[]{:S(2)}) async-start(), calls=%async_computation.16 | async-start | bytes 23040000 | tf_op jit(solution)/shard_map/all_gather | solution.py:165
  66.2 2196.2 %all-gather.26.cloned.1.call-start = ((), (), s32[]{:S(2)}) async-start(), calls=%async_computation.18 | async-start | bytes 11980800 | tf_op jit(solution)/shard_map/all_gather | solution.py:167
  97.5 2175.2 %all-gather.28.cloned.1.call-start = ((), (), s32[]{:S(2)}) async-start(), calls=%async_computation.19 | async-start | bytes 39628800 | tf_op jit(solution)/shard_map/all_gather | solution.py:168
  167.2 2125.8 %all-gather.32.cloned.1.call-start = ((), (), s32[]{:S(2)}) async-start(), calls=%async_computation.21 | async-start | bytes 20606976 | tf_op jit(solution)/shard_map/all_gather | solution.py:169
  222.2 5016.8 %reduce-scatter.47.cloned.1.call-start = ((), (), s32[]{:S(2)}) async-start(), calls=%async_computation.31 | async-start | bytes 3686400
  5122.2 152.4 %reduce-scatter.55.cloned.1.call-start = ((), (), s32[]{:S(2)}) async-start(), calls=%async_computation.35 | async-start | bytes 11980800
  5129.4 295.6 %reduce-scatter.35.cloned.1.call-start = ((), (), s32[]{:S(2)}) async-start(), calls=%async_computation.22 | async-start | bytes 16588800 | tf_op jit(solution)/shard_map/reduce_scatter | solution.py:415
  5158.0 479.0 %reduce-scatter.37.cloned.1.call-start = ((), (), s32[]{:S(2)}) async-start(), calls=%async_computation.24 | async-start | bytes 23961600 | tf_op jit(solution)/shard_map/reduce_scatter | solution.py:419
  5170.9 822.5 %reduce-scatter.39.cloned.1.call-start = ((), (), s32[]{:S(2)}) async-start(), calls=%async_computation.25 | async-start | bytes 41213952 | tf_op jit(solution)/shard_map/reduce_scatter | solution.py:289
  5189.3 1201.0 %reduce-scatter.57.cloned.1.call-start = ((), (), s32[]{:S(2)}) async-start(), calls=%async_computation.36 | async-start | bytes 46080000
  5208.6 1970.7 %reduce-scatter.59.cloned.1.call-start = ((), (), s32[]{:S(2)}) async-start(), calls=%async_computation.37 | async-start | bytes 79257600
  5238.9 2054.3 %all-reduce.53.cloned.1.call-start = ((), (), s32[]{:S(2)}) async-start(), calls=%async_computation.23 | async-start | bytes 1048576 | tf_op jit(solution)/shard_map/psum | solution.py:428
  5241.0 2057.5 %reduce-scatter.43.cloned.1.call-start = ((), (), s32[]{:S(2)}) async-start(), calls=%async_computation.29 | async-start | bytes 2048000
  5277.7 2045.1 %reduce-scatter.41.cloned.1.call-start = ((), (), s32[]{:S(2)}) async-start(), calls=%async_computation.28 | async-start | bytes 2867200
  5427.9 1943.2 %reduce-scatter.49.cloned.1.call-start = ((), (), s32[]{:S(2)}) async-start(), calls=%async_computation.32 | async-start | bytes 4096000
  5641.4 1792.4 %reduce-scatter.53.cloned.1.call-start = ((), (), s32[]{:S(2)}) async-start(), calls=%async_computation.34 | async-start | bytes 6144000
  5999.3 1510.2 %reduce-scatter.45.cloned.1.call-start = ((), (), s32[]{:S(2)}) async-start(), calls=%async_computation.30 | async-start | bytes 8192000
  6396.7 1226.2 %reduce-scatter.51.cloned.1.call-start = ((), (), s32[]{:S(2)}) async-start(), calls=%async_computation.33 | async-start | bytes 14090240
  (903 other events, 9322.6 us)
Sparse Core Ops, SparseCore 0:
  9.9 49.9 all-gather.33
  62.3 31.7 all-gather.23
  95.9 55.2 all-gather.35
  179.9 37.7 all-gather.29
  219.8 73.6 all-gather.15
  295.7 55.3 all-gather.17
  352.7 180.2 all-gather.21
  535.2 98.9 all-gather.25
  635.7 302.2 all-gather.27
  939.6 162.7 all-gather.31
  5122.4 39.7 reduce-scatter.46
  5164.6 110.0 reduce-scatter.54
  5276.9 147.9 reduce-scatter.34
  5427.3 209.6 reduce-scatter.36
  5639.4 353.9 reduce-scatter.38
  5995.6 394.6 reduce-scatter.56
  6392.6 786.6 reduce-scatter.58
  7183.1 64.1 all-reduce.52
  7251.1 31.4 reduce-scatter.42
  7285.9 36.8 reduce-scatter.40
  7326.1 45.0 reduce-scatter.48
  7375.1 58.7 reduce-scatter.52
  7437.0 72.3 reduce-scatter.44
  7512.9 109.9 reduce-scatter.50
  (1 shorter events, 25.4 us)
where the time goes:
time: 7700 us; the launch traced here: 7640 us
  local copies, waits for them, and re-layouts  3030 us (39%)
  waiting for transfers between devices  2610 us (34%)
  other arithmetic  1610 us (21%)
  matrix products  255 us (3%)
  blocking collectives  104 us (1%)
    pad x384, local copies, waits for them, and re-layouts, states(): cum_decay, cum_drive = lax.associative_scan(combine, (decay, drive), axis=0)  1860 us
    unnamed x35, waiting for transfers between devices  1500 us
    pad x96, local copies, waits for them, and re-layouts, back_block(): lax.associative_scan(combine, (onward[::-1], seed[::-1]), axis=0)[1][::-1]  455 us
    add x192, other arithmetic, states(): cum_decay, cum_drive = lax.associative_scan(combine, (decay, drive), axis=0)  385 us
    reduce_scatter x1, waiting for transfers between devices, shards(): lax.psum_scatter(grad_down_w, 'shard', scatter_dimension=0, tiled=True)  352 us
    concatenate x192, other arithmetic, states(): cum_decay, cum_drive = lax.associative_scan(combine, (decay, drive), axis=0)  287 us
    mul x192, other arithmetic, combine(): return (early[0] * late[0], late[0] * early[1] + late[1])  275 us
    while x1472, local copies, waits for them, and re-layouts  262 us
  transfers between devices with their start and end apart: 25, of which 18 were waited for; matrix products, arithmetic and copies ran while one was open for 26% of the time, Pallas kernels for 0%

commit v1 on v0

v1 whole, which is shorter than its diff:
```python
import functools

import jax
import jax.numpy as jnp
from jax import lax
from jax.experimental import pallas as pl
from jax.experimental.pallas import tpu as pltpu
from jax.sharding import PartitionSpec as P

KV = 5
HEAD = 64
GROUP = 5
INNER = 3200
STATE = 16
CONV = 4
RANK = 100
FF = 5504
BLOCK = 128
CHUNK = 32


epsilon = 1e-06
beta_first = 0.9
beta_second = 0.95
adam_floor = 1e-08
learn_rate = 0.01
weight_decay = 0.1
masked_score = -1e30


def product(left, right):
    return jnp.dot(left, right, preferred_element_type=jnp.float32)


def product_tn(left, right):
    return lax.dot_general(
        left, right, (((0,), (0,)), ((), ())), preferred_element_type=jnp.float32
    )


def product_nt(left, right):
    return lax.dot_general(
        left, right, (((1,), (1,)), ((), ())), preferred_element_type=jnp.float32
    )


def sigmoid(values):
    return 1.0 / (1.0 + jnp.exp(-values))


def silu_act(values):
    return values / (1.0 + jnp.exp(-values))


def silu_slope(values):
    gate_sig = sigmoid(values)
    return gate_sig * (1.0 + values * (1.0 - gate_sig))


def rms_scale(values):
    return lax.rsqrt(jnp.mean(values * values, axis=-1, keepdims=True) + epsilon)


def rms_back(values, scale, gain, incoming):
    weighted = incoming * gain
    inner_mean = jnp.mean(weighted * values, axis=-1, keepdims=True)
    return (
        scale * weighted - values * (scale * scale * scale) * inner_mean,
        jnp.sum(incoming * values * scale, axis=0),
    )


def shift_rows(values, lag):
    if lag == 0:
        return values
    return jnp.concatenate(
        [jnp.zeros((lag, values.shape[1]), values.dtype), values[: values.shape[0] - lag]], axis=0
    )


def unshift_rows(values, lag):
    if lag == 0:
        return values
    return jnp.concatenate([values[lag:], jnp.zeros((lag, values.shape[1]), values.dtype)], axis=0)


LANES=128

def row_sums(parts):
    rows = lax.broadcasted_iota(jnp.int32, (8, LANES), 0)
    quads = []
    low = rows < 4
    for i in range(4):
        a, b = parts[i], parts[i + 4]
        quads.append(jnp.where(low, a, b) + pltpu.roll(jnp.where(low, b, a), 4, 0))
    pairs = []
    low = (rows & 3) < 2
    for i in range(2):
        a, b = quads[i], quads[i + 2]
        pairs.append(jnp.where(low, a + pltpu.roll(a, 6, 0), b + pltpu.roll(b, 2, 0)))
    a, b = pairs
    return jnp.where((rows & 1) < 1, a + pltpu.roll(a, 7, 0), b + pltpu.roll(b, 1, 0))

def fold(values):
    return values[:8] + values[8:]

def scan_kernel(per_block, keep_ref, step_ref, conv_ref, inj_ref, read_ref, rates_ref, out_ref, start_ref, state_ref):
    chunk, tiles = step_ref.shape[0], step_ref.shape[1] // LANES
    at = pl.program_id(0)
    @pl.when(at % per_block == 0)
    def _():
        state_ref[...] = state_ref[...] * keep_ref[at // per_block]
    @pl.when(at == 0)
    def _():
        state_ref[...] = jnp.zeros_like(state_ref)
    start_ref[0] = state_ref[...]
    rates = [rates_ref[:, k*LANES:(k+1)*LANES] for k in range(tiles)]
    def group(g, state):
        base = pl.multiple_of(g * 8, 8)
        state = list(state)
        steps = [step_ref[pl.ds(base, 8), k*LANES:(k+1)*LANES] for k in range(tiles)]
        pushes = [steps[k] * conv_ref[pl.ds(base, 8), k*LANES:(k+1)*LANES] for k in range(tiles)]
        parts = [[] for _ in range(tiles)]
        for i in range(8):
            inject, read = inj_ref[base + i], read_ref[base + i]
            for k in range(tiles):
                decay = jnp.exp(steps[k][i:i+1] * rates[k])
                state[k] = decay * state[k] + pushes[k][i:i+1] * inject
                parts[k].append(fold(state[k] * read))
        for k in range(tiles):
            out_ref[pl.ds(base, 8), k*LANES:(k+1)*LANES] = row_sums(parts[k])
        return tuple(state)
    state = tuple(state_ref[:, k*LANES:(k+1)*LANES] for k in range(tiles))
    state = lax.fori_loop(0, chunk // 8, group, state)
    for k in range(tiles):
        state_ref[:, k*LANES:(k+1)*LANES] = state[k]

def scan_forward(keep, step, conv, inject, read, rates, chunk, block):
    rows, width = step.shape
    grid = rows // chunk
    row_spec = pl.BlockSpec((chunk, width), lambda i, *_: (i, 0))
    wide_spec = pl.BlockSpec((chunk, STATE, LANES), lambda i, *_: (i, 0, 0))
    return pl.pallas_call(
        functools.partial(scan_kernel, block // chunk),
        grid_spec=pltpu.PrefetchScalarGridSpec(num_scalar_prefetch=1, grid=(grid,),
            in_specs=[row_spec, row_spec, wide_spec, wide_spec, pl.BlockSpec((STATE, width), lambda i, *_: (0, 0))],
            out_specs=[row_spec, pl.BlockSpec((1, STATE, width), lambda i, *_: (i, 0, 0))],
            scratch_shapes=[pltpu.VMEM((STATE, width), jnp.float32)]),
        out_shape=[jax.ShapeDtypeStruct((rows, width), jnp.float32), jax.ShapeDtypeStruct((grid, STATE, width), jnp.float32)],
        compiler_params=pltpu.CompilerParams(vmem_limit_bytes=40<<20),
        name="state_scan",
    )(keep, step, conv, inject, read, rates)

def back_kernel(per_block, keep_ref, step_ref, conv_ref, inj_ref, read_ref, rates_ref, grad_ref, start_ref,
                gstep_ref, gconv_ref, ginj_ref, gread_ref, grate_ref, later_ref, hist_ref, decay_ref):
    chunk, tiles = step_ref.shape[0], step_ref.shape[1] // LANES
    at = pl.num_programs(0) - 1 - pl.program_id(0)
    lanes = [slice(k*LANES, (k+1)*LANES) for k in range(tiles)]
    @pl.when(pl.program_id(0) == 0)
    def _():
        later_ref[...] = jnp.zeros_like(later_ref)
        grate_ref[...] = jnp.zeros_like(grate_ref)
    def forward(g, state):
        base = pl.multiple_of(g * 8, 8)
        state = list(state)
        steps = [step_ref[pl.ds(base, 8), lanes[k]] for k in range(tiles)]
        pushes = [steps[k] * conv_ref[pl.ds(base, 8), lanes[k]] for k in range(tiles)]
        for i in range(8):
            inject = inj_ref[base + i]
            for k in range(tiles):
                decay = jnp.exp(steps[k][i:i+1] * rates_ref[:, lanes[k]])
                decay_ref[base + i, :, lanes[k]] = decay
                hist_ref[base + i, :, lanes[k]] = state[k]
                state[k] = decay * state[k] + pushes[k][i:i+1] * inject
        return tuple(state)
    state = lax.fori_loop(0, chunk // 8, forward, tuple(start_ref[0, :, lanes[k]] for k in range(tiles)))
    for k in range(tiles):
        hist_ref[chunk, :, lanes[k]] = state[k]
    def backward(j, later):
        base = pl.multiple_of((chunk // 8 - 1 - j) * 8, 8)
        later = list(later)
        steps = [step_ref[pl.ds(base, 8), lanes[k]] for k in range(tiles)]
        convs = [conv_ref[pl.ds(base, 8), lanes[k]] for k in range(tiles)]
        grads = [grad_ref[pl.ds(base, 8), lanes[k]] for k in range(tiles)]
        pushes = [steps[k] * convs[k] for k in range(tiles)]
        pulls = [[None] * 8 for _ in range(tiles)]
        drives = [[None] * 8 for _ in range(tiles)]
        rate_sums = [None] * tiles
        for i in range(7, -1, -1):
            inject, read = inj_ref[base + i], read_ref[base + i]
            ginj = gread = None
            for k in range(tiles):
                grad = grads[k][i:i+1]
                total = read * grad + later[k]
                later[k] = decay_ref[base + i, :, lanes[k]] * total
                pull = later[k] * hist_ref[base + i, :, lanes[k]]
                term = pull * steps[k][i:i+1]
                rate_sums[k] = term if rate_sums[k] is None else rate_sums[k] + term
                pulls[k][i] = fold(pull * rates_ref[:, lanes[k]])
                drives[k][i] = fold(total * inject)
                term = total * pushes[k][i:i+1]
                ginj = term if ginj is None else ginj + term
                term = hist_ref[base + i + 1, :, lanes[k]] * grad
                gread = term if gread is None else gread + term
            ginj_ref[base + i] = ginj
            gread_ref[base + i] = gread
        for k in range(tiles):
            grate_ref[:, lanes[k]] += rate_sums[k]
            drive = row_sums(drives[k])
            gstep_ref[pl.ds(base, 8), lanes[k]] = row_sums(pulls[k]) + drive * convs[k]
            gconv_ref[pl.ds(base, 8), lanes[k]] = drive * steps[k]
        return tuple(later)
    later = lax.fori_loop(0, chunk // 8, backward, tuple(later_ref[:, lanes[k]] for k in range(tiles)))
    factor = jnp.where(at % per_block == 0, keep_ref[at // per_block], 1.0)
    for k in range(tiles):
        later_ref[:, lanes[k]] = later[k] * factor

def scan_backward(keep, step, conv, inject, read, rates, grad, starts, chunk, block):
    rows, width = step.shape
    grid = rows // chunk
    row_spec = pl.BlockSpec((chunk, width), lambda i, *_: (grid - 1 - i, 0))
    wide_spec = pl.BlockSpec((chunk, STATE, LANES), lambda i, *_: (grid - 1 - i, 0, 0))
    all_spec = pl.BlockSpec((STATE, width), lambda i, *_: (0, 0))
    return pl.pallas_call(
        functools.partial(back_kernel, block // chunk),
        grid_spec=pltpu.PrefetchScalarGridSpec(num_scalar_prefetch=1, grid=(grid,),
            in_specs=[row_spec, row_spec, wide_spec, wide_spec, all_spec, row_spec, pl.BlockSpec((1, STATE, width), lambda i, *_: (grid - 1 - i, 0, 0))],
            out_specs=[row_spec, row_spec, wide_spec, wide_spec, all_spec],
            scratch_shapes=[pltpu.VMEM((STATE, width), jnp.float32), pltpu.VMEM((chunk + 1, STATE, width), jnp.float32), pltpu.VMEM((chunk, STATE, width), jnp.float32)]),
        out_shape=[jax.ShapeDtypeStruct((rows, width), jnp.float32)] * 2 + [jax.ShapeDtypeStruct((rows, STATE, LANES), jnp.float32)] * 2 + [jax.ShapeDtypeStruct((STATE, width), jnp.float32)],
        compiler_params=pltpu.CompilerParams(vmem_limit_bytes=50<<20),
        name="state_back",
    )(keep, step, conv, inject, read, rates, grad, starts)


def adam_update(weight, gradient, first_old, second_old, step_float):
    mean_new = beta_first * first_old + (1.0 - beta_first) * gradient
    square_new = beta_second * second_old + (1.0 - beta_second) * gradient * gradient
    fix_first = 1.0 - jnp.power(beta_first, step_float)
    fix_second = 1.0 - jnp.power(beta_second, step_float)
    delta_new = -learn_rate * (
        mean_new / fix_first / (jnp.sqrt(square_new / fix_second) + adam_floor)
        + weight_decay * weight.astype(jnp.float32)
    )
    return (mean_new, square_new, delta_new)


def layout(lengths, buffer_rows):
    index = jnp.arange(lengths.shape[0], dtype=jnp.int32)
    count_blocks = (lengths + (BLOCK - 1)) // BLOCK
    earlier = (index[None, :] < index[:, None]).astype(jnp.int32)
    first_block = jnp.sum(earlier * count_blocks[None, :], axis=1)
    places = jnp.arange(buffer_rows, dtype=jnp.int32)
    owner = (
        jnp.sum((first_block[None, :] <= (places // BLOCK)[:, None]).astype(jnp.int32), axis=1) - 1
    )
    pick = (owner[:, None] == index[None, :]).astype(jnp.int32)
    seq_length = jnp.sum(pick * lengths[None, :], axis=1)
    offset = places - BLOCK * jnp.sum(pick * first_block[None, :], axis=1)
    live = offset < seq_length
    begins = live & (offset == 0)
    return (owner, offset, live, begins)


def trade(pieces):
    return lax.all_to_all(pieces, "dp", 0, 0)


def spread(rows, groups):
    got = trade(jnp.broadcast_to(rows[None], (groups,) + rows.shape))
    return got.reshape((groups * rows.shape[0],) + rows.shape[1:])


def collect(partial, groups, kind=jnp.bfloat16):
    pieces = partial.astype(kind).reshape((groups, partial.shape[0] // groups) + partial.shape[1:])
    return jnp.sum(trade(pieces).astype(jnp.float32), axis=0)


def padded_part(part, ranks):
    unit = max(8, LANES // ranks)
    return -(-part // unit) * unit


def deal_columns(shard, groups, part, wide_part):
    rows, width = shard.shape
    runs = width // (groups * part)
    pieces = shard.reshape(rows, runs, groups, part).transpose(2, 0, 1, 3)
    got = trade(pieces.reshape(groups, rows, runs * part)).transpose(1, 0, 2)
    got = jnp.pad(got.reshape(rows, groups * runs, part), ((0, 0), (0, 0), (0, wide_part - part)))
    return got.reshape(rows, groups * runs * wide_part)


def return_columns(dealt, groups, part, wide_part):
    rows, width = dealt.shape
    runs = width // (groups * wide_part)
    pieces = dealt.reshape(rows, groups * runs, wide_part)[:, :, :part]
    got = trade(pieces.reshape(rows, groups, runs * part).transpose(1, 0, 2))
    return got.reshape(groups, rows, runs, part).transpose(1, 2, 0, 3).reshape(rows, -1)


def deal_rows(shard, groups, wide_part):
    rows, width = shard.shape
    part = rows // groups
    got = trade(shard.reshape(groups, part, width))
    got = got.transpose(1, 0, 2).reshape(part, groups * width)
    return jnp.pad(got, ((0, wide_part - part), (0, 0)))


def return_rows(dealt, groups, part):
    width = dealt.shape[1]
    got = trade(dealt[:part].reshape(part, groups, width // groups).transpose(1, 0, 2))
    return got.reshape(groups * part, width // groups)


def whole(shard):
    return lax.all_gather(shard, "shard", axis=0, tiled=True)


def owned_sum(partial):
    return lax.psum_scatter(partial, "shard", scatter_dimension=0, tiled=True)


def lane_copies(values):
    return jnp.broadcast_to(values[:, :, None], values.shape + (LANES,))


def shards(
    groups,
    ranks,
    tokens,
    cotangent,
    lengths,
    step_count,
    norm_gains,
    qkv_weight,
    attn_weight,
    mixer_in,
    mixer_table,
    mixer_out,
    ffn_in,
    ffn_out,
    first_gains,
    first_qkv,
    first_attn,
    first_mixin,
    first_table,
    first_mixout,
    first_ffnin,
    first_ffnout,
    second_gains,
    second_qkv,
    second_attn,
    second_mixin,
    second_table,
    second_mixout,
    second_ffnin,
    second_ffnout,
):
    low = jnp.bfloat16
    buffer_rows = tokens.shape[0]
    model_width = tokens.shape[1]
    here = lax.axis_index("dp")
    part_inner = INNER // groups // ranks
    part_hidden = FF // groups // ranks
    wide_inner = padded_part(part_inner, ranks)
    wide_hidden = padded_part(part_hidden, ranks)
    inner = wide_inner * ranks
    hidden_units = wide_hidden * ranks
    part_model = model_width // ranks
    table_width = mixer_table.shape[1]
    gain_count = norm_gains.shape[1]

    table_part = lax.dynamic_slice_in_dim(mixer_table, here * part_inner, part_inner, axis=0)
    table_part = jnp.pad(table_part, ((0, 0), (0, 2 * LANES - table_width)))
    fold_rows = part_inner * 2 * LANES // part_model
    first_pack = jnp.concatenate(
        [qkv_weight, table_part.reshape(part_model, fold_rows), norm_gains], axis=1
    )
    first_full = whole(first_pack)
    weight_in = whole(deal_columns(mixer_in, groups, part_inner, wide_inner))
    weight_mix = whole(deal_rows(mixer_out, groups, wide_inner))
    weight_attn = whole(spread(attn_weight, groups).reshape(groups, part_model, -1).transpose(1, 0, 2).reshape(part_model, model_width))
    weight_up = whole(deal_columns(ffn_in, groups, part_hidden, wide_hidden))
    weight_down = whole(deal_rows(ffn_out, groups, wide_hidden))

    qkv_width = qkv_weight.shape[1]
    weight_qkv = first_full[:, :qkv_width]
    table_low = first_full[:, qkv_width : qkv_width + fold_rows].reshape(
        ranks, part_inner, 2 * LANES
    )
    table_low = jnp.pad(
        table_low[:, :, :table_width], ((0, 0), (0, wide_inner - part_inner), (0, 0))
    ).reshape(inner, table_width)
    gain_cols = first_full[:, qkv_width + fold_rows :].astype(jnp.float32)

    lengths_all = lax.all_gather(lengths, "dp", axis=0, tiled=True)
    owner, offset, live, _ = layout(lengths[0], buffer_rows)
    live_rows = live.astype(jnp.float32)
    places = jnp.arange(buffer_rows, dtype=jnp.int32)
    allowed = (owner[:, None] == owner[None, :]) & (places[None, :] <= places[:, None]) & live[
        None, :
    ] | (places[:, None] == places[None, :])
    _, offset_all, _, begins_all = jax.vmap(lambda row: layout(row, buffer_rows))(lengths_all)
    offset_all = offset_all.reshape(-1)
    block_starts = begins_all[:, ::BLOCK] | (jnp.arange(buffer_rows // BLOCK) == 0)[None, :]
    block_keep = 1.0 - block_starts.reshape(-1).astype(jnp.float32)

    inputs = tokens.astype(jnp.float32)
    scale_in = rms_scale(inputs)
    normed = (inputs * scale_in * gain_cols[:, 0]).astype(low)
    normed_all = spread(normed, groups)
    grad_out = cotangent.astype(jnp.float32) * live_rows[:, None]
    grad_ffn_all = spread(grad_out.astype(low), groups)

    heads_part = product(normed_all, weight_qkv).astype(low)
    heads_low = (
        trade(heads_part.reshape(groups, buffer_rows, qkv_width))
        .transpose(1, 0, 2)
        .reshape(buffer_rows, groups * qkv_width)
    )
    kv_width = KV * HEAD
    query = heads_low[:, :model_width].reshape(buffer_rows, KV, GROUP, HEAD)
    key_rows = heads_low[:, model_width : model_width + kv_width].reshape(buffer_rows, KV, HEAD)
    value_rows = heads_low[:, model_width + kv_width :].reshape(buffer_rows, KV, HEAD)
    factor = HEAD ** (-0.5)

    def masked_scores():
        raw_scores = (
            jnp.einsum("qkgd,skd->kgqs", query, key_rows, preferred_element_type=jnp.float32)
            * factor
        )
        return jnp.where(allowed, raw_scores, masked_score)

    scores = masked_scores()
    top_score = jnp.max(scores, axis=-1, keepdims=True)
    log_total = top_score + jnp.log(jnp.sum(jnp.exp(scores - top_score), axis=-1, keepdims=True))
    probs_low = jnp.exp(scores - log_total).astype(low)
    context = (
        jnp.einsum("kgqs,skd->qkgd", probs_low, value_rows, preferred_element_type=jnp.float32)
        .reshape(buffer_rows, model_width)
        .astype(low)
    )
    attn_raw = product(context, weight_attn)
    scale_attn = rms_scale(attn_raw)

    mixed = product(normed_all, weight_in)
    xin = mixed[:, :inner]
    gate_z = mixed[:, inner:]
    table = table_low.astype(jnp.float32)
    tap_masks = [(offset_all >= lag).astype(jnp.float32)[:, None] for lag in range(CONV)]
    taps = [shift_rows(xin, lag) * tap_masks[lag] for lag in range(CONV)]
    conv_pre = table[:, CONV]
    for lag in range(CONV):
        conv_pre = conv_pre + table[:, lag] * taps[lag]
    conv_low = silu_act(conv_pre).astype(low)
    conv_out = conv_low.astype(jnp.float32)
    proj_start = CONV + 3 + STATE
    input_proj = table_low[:, proj_start : proj_start + RANK + 2 * STATE]
    step_proj = table_low[:, proj_start + RANK + 2 * STATE :]
    double = spread(
        collect(product(conv_low, input_proj), groups, jnp.float32), groups
    )
    rank_part = double[:, :RANK].astype(low)
    inject = lane_copies(double[:, RANK : RANK + STATE])
    readout = lane_copies(double[:, RANK + STATE :])
    dt_pre = product_nt(rank_part, step_proj) + table[:, CONV + 1]
    step_size = jnp.log1p(jnp.exp(dt_pre))
    rates = -jnp.exp(table[:, CONV + 3 : CONV + 3 + STATE]).T
    states_out, chunk_starts = scan_forward(
        block_keep, step_size, conv_out, inject, readout, rates, CHUNK, BLOCK
    )
    skip_weight = table[:, CONV + 2]
    scanned = states_out + skip_weight * conv_out
    silu_z = silu_act(gate_z)
    gated_low = (scanned * silu_z).astype(low)
    mamba_raw = collect(product(gated_low, weight_mix), groups)
    scale_mamba = rms_scale(mamba_raw)
    hidden = inputs + 0.5 * (
        attn_raw * scale_attn * gain_cols[:, 1] + mamba_raw * scale_mamba * gain_cols[:, 2]
    )
    scale_hidden = rms_scale(hidden)
    normed_two = (hidden * scale_hidden * gain_cols[:, 3]).astype(low)

    normed_two_all = spread(normed_two, groups)
    both = product(normed_two_all, weight_up)
    gate_ffn = both[:, :hidden_units]
    up_ffn = both[:, hidden_units:]
    act_low = (silu_act(gate_ffn) * up_ffn).astype(low)
    ffn_raw = collect(product(act_low, weight_down), groups)
    output = (live_rows[:, None] * (hidden + ffn_raw)).astype(low)
    grad_down_w = product_tn(act_low, grad_ffn_all).astype(low)
    grad_act = product_nt(grad_ffn_all, weight_down)
    gate_sig = sigmoid(gate_ffn)
    grad_gate = grad_act * up_ffn * gate_sig * (1.0 + gate_ffn * (1.0 - gate_sig))
    grad_up = grad_act * silu_act(gate_ffn)
    grad_both = jnp.concatenate([grad_gate, grad_up], axis=1).astype(low)
    grad_up_w = product_tn(normed_two_all, grad_both).astype(low)
    grad_second = collect(product_nt(grad_both, weight_up), groups)
    back_hidden, gain_three = rms_back(hidden, scale_hidden, gain_cols[:, 3], grad_second)
    grad_hidden = grad_out + back_hidden
    ffn_done = (
        return_columns(owned_sum(grad_up_w), groups, part_hidden, wide_hidden),
        return_rows(owned_sum(grad_down_w), groups, part_hidden),
    )

    half_grad = 0.5 * grad_hidden
    grad_mamba_full, gain_two = rms_back(mamba_raw, scale_mamba, gain_cols[:, 2], half_grad)
    grad_mamba_all = spread(grad_mamba_full.astype(low), groups)
    grad_attn_full, gain_one = rms_back(attn_raw, scale_attn, gain_cols[:, 1], half_grad)
    grad_attn_low = grad_attn_full.astype(low)
    grad_attn_w = product_tn(context, grad_attn_low).astype(low)
    grad_attn_own = owned_sum(grad_attn_w)
    grad_attn_done = collect(
        grad_attn_own.reshape(part_model, groups, -1).transpose(1, 0, 2).reshape(groups * part_model, -1),
        groups,
    )
    grad_context = (
        product_nt(grad_attn_low, weight_attn).astype(low).reshape(buffer_rows, KV, GROUP, HEAD)
    )
    probs_again = jnp.exp(masked_scores() - log_total)
    grad_probs = jnp.einsum(
        "qkgd,skd->kgqs", grad_context, value_rows, preferred_element_type=jnp.float32
    )
    grad_values = jnp.einsum(
        "kgqs,qkgd->skd",
        probs_again.astype(low),
        grad_context,
        preferred_element_type=jnp.float32,
    )
    grad_scores = (
        probs_again * (grad_probs - jnp.sum(probs_again * grad_probs, axis=-1, keepdims=True))
    ).astype(low)
    grad_query = (
        jnp.einsum("kgqs,skd->qkgd", grad_scores, key_rows, preferred_element_type=jnp.float32)
        * factor
    )
    grad_keys = (
        jnp.einsum("kgqs,qkgd->skd", grad_scores, query, preferred_element_type=jnp.float32)
        * factor
    )
    grad_heads = jnp.concatenate(
        [
            grad_query.reshape(buffer_rows, model_width),
            grad_keys.reshape(buffer_rows, kv_width),
            grad_values.reshape(buffer_rows, kv_width),
        ],
        axis=1,
    ).astype(low)
    grad_heads_part = trade(
        grad_heads.reshape(buffer_rows, groups, qkv_width).transpose(1, 0, 2)
    ).reshape(groups * buffer_rows, qkv_width)
    grad_qkv_w = product_tn(normed_all, grad_heads_part).astype(low)

    grad_mix_w = product_tn(gated_low, grad_mamba_all).astype(low)
    grad_mix_done = return_rows(owned_sum(grad_mix_w), groups, part_inner)
    grad_gated = product_nt(grad_mamba_all, weight_mix)
    grad_scanned = grad_gated * silu_z
    grad_gate_z = grad_gated * scanned * silu_slope(gate_z)
    grad_skip = jnp.sum(grad_scanned * conv_out, axis=0)
    grad_step, grad_conv_scan, grad_inject, grad_readout, grad_rates = scan_backward(
        block_keep,
        step_size,
        conv_out,
        inject,
        readout,
        rates,
        grad_scanned,
        chunk_starts,
        CHUNK,
        BLOCK,
    )
    grad_pre = grad_step * sigmoid(dt_pre)
    grad_step_bias = jnp.sum(grad_pre, axis=0)
    grad_pre_low = grad_pre.astype(low)
    grad_step_proj = product_tn(grad_pre_low, rank_part)
    grad_rank = product(grad_pre_low, step_proj)
    grad_double = spread(
        collect(
            jnp.concatenate(
                [grad_rank, jnp.sum(grad_inject, axis=2), jnp.sum(grad_readout, axis=2)], axis=1
            ),
            groups,
            jnp.float32,
        ).astype(low),
        groups,
    )
    grad_input_proj = product_tn(conv_low, grad_double)
    grad_conv_out = (
        product_nt(grad_double, input_proj) + grad_conv_scan + skip_weight * grad_scanned
    )
    grad_conv = grad_conv_out * silu_slope(conv_pre)
    grad_conv_bias = jnp.sum(grad_conv, axis=0)
    grad_taps = jnp.stack([jnp.sum(grad_conv * taps[lag], axis=0) for lag in range(CONV)], axis=1)
    grad_xin = unshift_rows(grad_conv * tap_masks[0] * table[:, 0], 0)
    for lag in range(1, CONV):
        grad_xin = grad_xin + unshift_rows(grad_conv * tap_masks[lag] * table[:, lag], lag)
    grad_mixed = jnp.concatenate([grad_xin, grad_gate_z], axis=1).astype(low)
    grad_in_w = product_tn(normed_all, grad_mixed).astype(low)
    grad_normed = collect(
        product_nt(grad_heads_part, weight_qkv) + product_nt(grad_mixed, weight_in), groups
    )
    grad_log_rates = (grad_rates * rates).T
    grad_table = jnp.concatenate(
        [
            grad_taps,
            grad_conv_bias[:, None],
            grad_step_bias[:, None],
            grad_skip[:, None],
            grad_log_rates,
            grad_input_proj,
            grad_step_proj,
        ],
        axis=1,
    ).reshape(ranks, wide_inner, table_width)[:, :part_inner]
    back_inputs, gain_zero = rms_back(inputs, scale_in, gain_cols[:, 0], grad_normed)
    grad_tokens = grad_hidden + back_inputs
    grad_gains = jnp.stack([gain_zero, gain_one, gain_two, gain_three], axis=1)

    grad_qkv_done = owned_sum(grad_qkv_w).astype(jnp.float32)
    grad_in_done = return_columns(owned_sum(grad_in_w), groups, part_inner, wide_inner)
    small = jnp.concatenate(
        [
            jnp.pad(grad_table, ((0, 0), (0, 0), (0, 2 * LANES - table_width))).reshape(
                model_width, fold_rows
            ),
            grad_gains,
        ],
        axis=1,
    )
    small_all = spread(owned_sum(small), groups).reshape(groups, part_model, fold_rows + gain_count)
    grad_table_done = small_all[:, :, :fold_rows].reshape(groups * part_inner, 2 * LANES)[
        :, :table_width
    ]
    grad_gains_done = jnp.sum(small_all[:, :, fold_rows:], axis=0)

    owned = (norm_gains, qkv_weight, attn_weight, mixer_in, mixer_table, mixer_out, ffn_in, ffn_out)
    grads_owned = (
        grad_gains_done,
        grad_qkv_done,
        grad_attn_done,
        grad_in_done.astype(jnp.float32),
        grad_table_done,
        grad_mix_done.astype(jnp.float32),
        ffn_done[0].astype(jnp.float32),
        ffn_done[1].astype(jnp.float32),
    )
    firsts = (
        first_gains,
        first_qkv,
        first_attn,
        first_mixin,
        first_table,
        first_mixout,
        first_ffnin,
        first_ffnout,
    )
    seconds = (
        second_gains,
        second_qkv,
        second_attn,
        second_mixin,
        second_table,
        second_mixout,
        second_ffnin,
        second_ffnout,
    )
    step_float = step_count[0].astype(jnp.float32)
    updates = [
        adam_update(owned[slot], grads_owned[slot], firsts[slot], seconds[slot], step_float)
        for slot in range(8)
    ]
    means = tuple((entry[0] for entry in updates))
    squares = tuple((entry[1] for entry in updates))
    deltas = tuple((entry[2] for entry in updates))
    return (output, grad_tokens) + grads_owned + means + squares + deltas


def solution(mesh):
    in_specs = (
        P(("dp", "shard"), None),
        P(("dp", "shard"), None),
        P(("dp", "shard"), None),
        P(),
        P("shard", None),
        P("shard", "dp"),
        P("shard", "dp"),
        P("shard", "dp"),
        P("shard", None),
        P("shard", "dp"),
        P("shard", "dp"),
        P("shard", "dp"),
        P("shard", None),
        P("shard", "dp"),
        P("shard", "dp"),
        P("shard", "dp"),
        P("shard", None),
        P("shard", "dp"),
        P("shard", "dp"),
        P("shard", "dp"),
        P("shard", None),
        P("shard", "dp"),
        P("shard", "dp"),
        P("shard", "dp"),
        P("shard", None),
        P("shard", "dp"),
        P("shard", "dp"),
        P("shard", "dp"),
    )
    out_specs = (
        P(("dp", "shard"), None),
        P(("dp", "shard"), None),
        P("shard", None),
        P("shard", "dp"),
        P("shard", "dp"),
        P("shard", "dp"),
        P("shard", None),
        P("shard", "dp"),
        P("shard", "dp"),
        P("shard", "dp"),
        P("shard", None),
        P("shard", "dp"),
        P("shard", "dp"),
        P("shard", "dp"),
        P("shard", None),
        P("shard", "dp"),
        P("shard", "dp"),
        P("shard", "dp"),
        P("shard", None),
        P("shard", "dp"),
        P("shard", "dp"),
        P("shard", "dp"),
        P("shard", None),
        P("shard", "dp"),
        P("shard", "dp"),
        P("shard", "dp"),
        P("shard", None),
        P("shard", "dp"),
        P("shard", "dp"),
        P("shard", "dp"),
        P("shard", None),
        P("shard", "dp"),
        P("shard", "dp"),
        P("shard", "dp"),
    )
    return jax.shard_map(functools.partial(shards, mesh.shape["dp"], mesh.shape["shard"]), mesh=mesh, in_specs=in_specs, out_specs=out_specs, check_vma=False)
```

time: 7700 us -> 1190 us (0.15)
  local copies, waits for them, and re-layouts: 3030 us -> 212 us
  waiting for transfers between devices: 2610 us -> 393 us
  other arithmetic: 1610 us -> 108 us
  starting transfers between devices: 2.35 us -> 97.6 us
  Pallas kernels: 0 us -> 87 us
    pad x480 -> x7, local copies, waits for them, and re-layouts: 2310 us -> 4.34 us  [the longest x2 2.7 us: deal_rows(): return jnp.pad(got, ((0, wide_part - part), (0, 0)))]
    unnamed x35 -> x15, waiting for transfers between devices: 1500 us -> 31.3 us
    reduce_scatter x3 -> x5, waiting for transfers between devices: 708 us -> 141 us  [owned_sum(): return lax.psum_scatter(partial, 'shard', scatter_dimension=0, tiled=True)]
    add x320 -> x0, other arithmetic: 530 us -> none  [the longest x192 385 us: states(): cum_decay, cum_drive = lax.associative_scan(combine, (decay, drive), axis=0)]
    all_gather x11 -> x6, waiting for transfers between devices: 405 us -> 0.03 us  [whole(): return lax.all_gather(shard, 'shard', axis=0, tiled=True)]
    mul x305 -> x1, other arithmetic: 342 us -> 0.01 us  [layout(): first_block = jnp.sum(earlier * count_blocks[None, :], axis=1)]
    concatenate x240 -> x3, other arithmetic: 335 us -> 2.92 us  [the longest x1 1.79 us: shards(): jnp.concatenate([qkv_weight, table_part.reshape(part_model, fold_rows), n...]
    while x1474 -> x0, local copies, waits for them, and re-layouts: 263 us -> none
  transfers between devices with their start and end apart: 25 -> 34, of which waited for: 18 -> 18; matrix products, arithmetic and copies ran while one was open for 26% -> 37% of each run, Pallas kernels for 0% -> 7%
where the time goes in v1:
time: 1190 us; the launch traced here: 1170 us
  waiting for transfers between devices  393 us (33%)
  local copies, waits for them, and re-layouts  212 us (18%)
  matrix products  197 us (17%)
  other arithmetic  108 us (9%)
  starting transfers between devices  97.6 us (8%)
  Pallas kernels  87 us (7%)
  blocking collectives  62.1 us (5%)
  between operations  17.2 us (1%)
    all_to_all x21, waiting for transfers between devices, trade(): return lax.all_to_all(pieces, 'dp', 0, 0)  221 us
    reduce_scatter x5, waiting for transfers between devices, owned_sum(): return lax.psum_scatter(partial, 'shard', scatter_dimension=0, tiled=True)  141 us
    all_to_all x21, starting transfers between devices, trade(): return lax.all_to_all(pieces, 'dp', 0, 0)  96.1 us
    dot_general x8, matrix products, product_nt(): lax.dot_general(left, right, (((1,), (1,)), ((), ())), preferred_element_...  66.1 us
    dot_general x8, matrix products, product_tn(): lax.dot_general(left, right, (((0,), (0,)), ((), ())), preferred_element_...  61.4 us
    pallas_call x1, Pallas kernels, scan_backward(): pl.pallas_call(functools.partial(back_kernel, block // chunk), grid_spec=...  57.7 us
    unnamed x264, local copies, waits for them, and re-layouts  56.5 us
    all_to_all x4, blocking collectives, trade(): return lax.all_to_all(pieces, 'dp', 0, 0)  54.7 us
  transfers between devices with their start and end apart: 34, of which 18 were waited for; matrix products, arithmetic and copies ran while one was open for 37% of the time, Pallas kernels for 7%

profile of v1, /device:TPU:0, one launch (start us, length us, event | category | flops | bytes accessed | tf_op | source)
XLA Modules:
  0.0 1173.2 jit_solution(9987253427435820992)
XLA Ops:
  16.4 16.9 %all_to_all.125 = bf16[4,200,400]{1,2,0:T(8,128)(2,1)S(1)} all-to-all(bf16[4,200,400]{1,2,0:T(8,128)(2,1)S(1)} %reshape.518), channel_id=1, replica_groups=mesh['dp'=4,'shard'=8] {'dp'}, dimensions={0} | all-to-all | bytes 1280000 | tf_op jit(solution)/shard_map/all_to_all | solution.py:266
  45.8 12.8 %all_to_all.127 = bf16[4,200,400]{2,1,0:T(8,128)(2,1)S(1)} all-to-all(bf16[4,200,400]{2,1,0:T(8,128)(2,1)S(1)} %broadcast_in_dim.31), channel_id=1, replica_groups=mesh['dp'=4,'shard'=8] {'dp'}, dimensions={0} | all-to-all | bytes 1280000 | tf_op jit(solution)/shard_map/all_to_all | solution.py:266
  68.1 15.8 %all_to_all.128 = bf16[4,200,688]{2,1,0:T(8,128)(2,1)S(1)} all-to-all(bf16[4,200,688]{2,1,0:T(8,128)(2,1)S(1)} %copy.446), channel_id=1, replica_groups=mesh['dp'=4,'shard'=8] {'dp'}, dimensions={0} | all-to-all | bytes 2201600 | tf_op jit(solution)/shard_map/all_to_all | solution.py:266
  115.6 27.5 %all-to-all-done = bf16[4,256,1600]{1,2,0:T(8,128)(2,1)} async-done(((bf16[4,256,1600]{1,2,0:T(8,128)(2,1)}), bf16[4,256,1600]{1,2,0:T(8,128)(2,1)}, u32[]{:S(2)}, u32[]{:S(2)}) %all-to-all-start) | async-done | bytes 3276832 | tf_op jit(solution)/shard_map/all_to_all | solution.py:266
  185.7 12.0 %all-to-all-start.5 = ((f32[4,256,132]{1,2,0:T(8,128)}), f32[4,256,132]{1,2,0:T(8,128)S(1)}, u32[]{:S(2)}, u32[]{:S(2)}) async-start(f32[4,256,132]{1,2,0:T(8,128)} %broadcast_in_dim.32), calls=%async_computation.5 | async-start | bytes 1114112 | tf_op jit(solution)/shard_map/all_to_all | solution.py:266
  224.8 29.4 %state_scan.1 = (f32[1024,896]{1,0:T(8,128)S(1)}, f32[32,16,896]{2,1,0:T(8,128)S(1)}) custom-call(f32[8]{0:T(128)S(1)} %sub.155.keep_ref, f32[1024,896]{1,0:T(8,128)S(1)} %get-tuple-element.345.step_ref, f32[1024,896]{1,0:T(8,128)S(1)} %copy-done, f32[1024,16,128]{2,1,0:T(8,128)} %broadcast_in_dim.33.inj_ref, f32[1024,16,128]{2,1,0:T(8,128)} %broadcast_in_dim.34.read_ref, ...), custom_call_target="tpu_custom_call" | custom-call | tf_op jit(solution)/shard_map/state_scan/pallas_call | solution.py:143
  296.1 18.5 %all-to-all-done.7 = bf16[4,256,1600]{1,2,0:T(8,128)(2,1)} async-done(((bf16[4,256,1600]{1,2,0:T(8,128)(2,1)}), bf16[4,256,1600]{1,2,0:T(8,128)(2,1)}, u32[]{:S(2)}, u32[]{:S(2)}) %all-to-all-start.7) | async-done | bytes 3276832 | tf_op jit(solution)/shard_map/all_to_all | solution.py:266
  333.8 24.4 %all-to-all-done.12 = bf16[4,256,1600]{1,2,0:T(8,128)(2,1)} async-done(((bf16[4,256,1600]{1,2,0:T(8,128)(2,1)}), bf16[4,256,1600]{1,2,0:T(8,128)(2,1)}, u32[]{:S(2)}, u32[]{:S(2)}) %all-to-all-start.12) | async-done | bytes 3276832 | tf_op jit(solution)/shard_map/all_to_all | solution.py:266
  371.9 31.5 %all-to-all-done.8 = bf16[4,256,1600]{1,2,0:T(8,128)(2,1)} async-done(((bf16[4,256,1600]{1,2,0:T(8,128)(2,1)}), bf16[4,256,1600]{1,2,0:T(8,128)(2,1)}, u32[]{:S(2)}, u32[]{:S(2)}) %all-to-all-start.8) | async-done | bytes 3276832 | tf_op jit(solution)/shard_map/all_to_all | solution.py:266
  408.9 16.9 %fusion.83 = f32[1024,2816]{1,0:T(8,128)} fusion(bf16[1024,1600]{1,0:T(8,128)(2,1)} %bitcast.279, bf16[1600,2816]{1,0:T(8,128)(2,1)} %all-gather.16.cloned.1.call-done), kind=kOutput, calls=%fused_computation.249 | convolution fusion | flops 9227468800 | bytes 23822336 | tf_op jit(solution)/shard_map/dot_general | solution.py:32
  425.8 14.8 %multiply_convert_fusion.1 = (bf16[1024,1408]{1,0:T(8,128)(2,1)}, bf16[1024,1408]{1,0:T(8,128)(2,1)}, bf16[1024,1408]{1,0:T(8,128)(2,1)}) fusion(f32[1024,2816]{1,0:T(8,128)} %fusion.83, bf16[1024,1600]{1,0:T(8,128)(2,1)} %bitcast.283, bf16[1408,1600]{1,0:T(8,128)(2,1)} %all-gather.18.cloned.1.call-done), kind=kOutput, calls=%fused_computation.19 | convolution fusion | flops 4635361280 | bytes 27967488 | tf_op jit(solution)/shard_map/dot_general | solution.py:42
  440.6 11.6 convolution_convert_fusion.4
  469.4 26.7 %all-to-all-done.13 = bf16[4,256,1600]{1,2,0:T(8,128)(2,1)} async-done(((bf16[4,256,1600]{1,2,0:T(8,128)(2,1)}), bf16[4,256,1600]{1,2,0:T(8,128)(2,1)}, u32[]{:S(2)}, u32[]{:S(2)}) %all-to-all-start.13) | async-done | bytes 3276832 | tf_op jit(solution)/shard_map/all_to_all | solution.py:266
  516.4 21.4 %all-to-all-done.11 = bf16[4,256,1600]{1,2,0:T(8,128)(2,1)} async-done(((bf16[4,256,1600]{1,2,0:T(8,128)(2,1)}), bf16[4,256,1600]{1,2,0:T(8,128)(2,1)}, u32[]{:S(2)}, u32[]{:S(2)}) %all-to-all-start.11) | async-done | bytes 3276832 | tf_op jit(solution)/shard_map/all_to_all | solution.py:266
  575.6 16.0 %all-to-all-done.15 = bf16[4,256,1600]{1,2,0:T(8,128)(2,1)} async-done(((bf16[4,256,1600]{1,2,0:T(8,128)(2,1)}), bf16[4,256,1600]{1,2,0:T(8,128)(2,1)}, u32[]{:S(2)}, u32[]{:S(2)}) %all-to-all-start.15) | async-done | bytes 3276832 | tf_op jit(solution)/shard_map/all_to_all | solution.py:266
  597.3 13.5 %multiply_reduce_fusion = (f32[896]{0:T(1024)S(1)}, f32[1024,896]{1,0:T(8,128)}, bf16[1024,896]{1,0:T(8,128)(2,1)}) fusion(bf16[1024,896]{1,0:T(8,128)(2,1)} %copy-done.14, f32[1024,1792]{1,0:T(8,128)} %copy-done.6, f32[1024,896]{1,0:T(8,128)} %copy-done.2, f32[896]{0:T(1024)S(1)} %copy-done.96, bf16[1024,1600]{1,0:T(8,128)(2,1)} %bitcast.281, ...), kind=kOutput, calls=%fused_computation.43 | convolution fusion | flops 2951609344 | bytes 20831232 | tf_op jit(solution)/shard_map/dot_general | solution.py:42
  610.7 57.7 %state_back.1 = (f32[1024,896]{1,0:T(8,128)}, f32[1024,896]{1,0:T(8,128)}, f32[1024,16,128]{2,1,0:T(8,128)}, f32[1024,16,128]{2,1,0:T(8,128)}, f32[16,896]{1,0:T(8,128)S(1)}) custom-call(f32[8]{0:T(128)S(1)} %copy-done.4, f32[1024,896]{1,0:T(8,128)} %copy-done.1, f32[1024,896]{1,0:T(8,128)} %get-tuple-element.317.conv_ref, ...), custom_call_target="tpu_custom_call" | custom-call | tf_op jit(solution)/shard_map/state_back/pallas_call | solution.py:224
  702.6 13.0 %all-to-all-done.14 = bf16[4,256,560]{1,2,0:T(8,128)(2,1)S(1)} async-done(((bf16[4,256,560]{1,2,0:T(8,128)(2,1)}), bf16[4,256,560]{1,2,0:T(8,128)(2,1)S(1)}, u32[]{:S(2)}, u32[]{:S(2)}) %all-to-all-start.14) | async-done | bytes 1146912 | tf_op jit(solution)/shard_map/all_to_all | solution.py:266
  786.6 18.2 %all-to-all-done.18 = bf16[4,256,1600]{1,2,0:T(8,128)(2,1)} async-done(((bf16[4,256,1600]{1,2,0:T(8,128)(2,1)}), bf16[4,256,1600]{1,2,0:T(8,128)(2,1)}, u32[]{:S(2)}, u32[]{:S(2)}) %all-to-all-start.18) | async-done | bytes 3276832 | tf_op jit(solution)/shard_map/all_to_all | solution.py:266
  827.7 11.8 %convolution_convert_fusion.2 = bf16[1600,1792]{1,0:T(8,128)(2,1)} fusion(bf16[1024,1600]{1,0:T(8,128)(2,1)} %bitcast.278, bf16[1024,896]{1,0:T(8,128)(2,1)} %get-tuple-element.322, bf16[1024,896]{1,0:T(8,128)(2,1)} %copy-done.50), kind=kOutput, calls=%fused_computation.2 | convolution fusion | flops 5882232832 | bytes 12681216 | tf_op jit(solution)/shard_map/dot_general | solution.py:36
  839.8 15.8 %convolution_convert_fusion = bf16[1600,2816]{1,0:T(8,128)(2,1)} fusion(bf16[1024,1600]{1,0:T(8,128)(2,1)} %bitcast.280, bf16[1024,1408]{1,0:T(8,128)(2,1)} %get-tuple-element.321, bf16[1024,1408]{1,0:T(8,128)(2,1)} %get-tuple-element.320), kind=kOutput, calls=%fused_computation | convolution fusion | flops 9243508736 | bytes 18055168 | tf_op jit(solution)/shard_map/dot_general | solution.py:36
  920.0 31.1 %reduce-scatter.24.cloned.1.call-done = bf16[200,1600]{1,0:T(8,128)(2,1)} async-done(((bf16[1600,1600]{1,0:T(8,128)(2,1)}), bf16[200,1600]{1,0:T(8,128)(2,1)}) %reduce-scatter.24.cloned.1.call-update) | async-done | bytes 640016
  962.1 54.8 %reduce-scatter.14.cloned.1.call-done = bf16[200,1792]{1,0:T(8,128)(2,1)} async-done(((bf16[1600,1792]{1,0:T(8,128)(2,1)}), bf16[200,1792]{1,0:T(8,128)(2,1)}) %reduce-scatter.14.cloned.1.call-update) | async-done | bytes 716816 | tf_op jit(solution)/shard_map/reduce_scatter | solution.py:320
  1027.6 85.9 %reduce-scatter.18.cloned.1.call-done = bf16[200,2816]{1,0:T(8,128)(2,1)} async-done(((bf16[1600,2816]{1,0:T(8,128)(2,1)}), bf16[200,2816]{1,0:T(8,128)(2,1)}) %reduce-scatter.18.cloned.1.call-update) | async-done | bytes 1126416 | tf_op jit(solution)/shard_map/reduce_scatter | solution.py:320
  (555 shorter events, 558.2 us)
Async XLA Ops:
  7.2 92.8 %all-gather.8.cloned.1.call-start = ((), (), s32[]{:S(2)}) async-start(), calls=%async_computation.32 | async-start | bytes 2764800 | tf_op jit(solution)/shard_map/all_gather | solution.py:316
  10.8 137.8 %all-gather.12.cloned.1.call-start = ((), (), s32[]{:S(2)}) async-start(), calls=%async_computation.34 | async-start | bytes 6451200 | tf_op jit(solution)/shard_map/all_gather | solution.py:316
  35.0 232.1 %all-gather.14.cloned.1.call-start = ((), (), s32[]{:S(2)}) async-start(), calls=%async_computation.35 | async-start | bytes 3354624 | tf_op jit(solution)/shard_map/all_gather | solution.py:316
  45.7 275.6 %all-gather.10.cloned.1.call-start = ((), (), s32[]{:S(2)}) async-start(), calls=%async_computation.33 | async-start | bytes 5990400 | tf_op jit(solution)/shard_map/all_gather | solution.py:316
  60.6 348.3 %all-gather.16.cloned.1.call-start = ((), (), s32[]{:S(2)}) async-start(), calls=%async_computation.36 | async-start | bytes 10137600 | tf_op jit(solution)/shard_map/all_gather | solution.py:316
  204.5 51.4 %all-to-all-start.10 = ((bf16[4,172,400]{2,1,0:T(8,128)(2,1)}), bf16[4,172,400]{2,1,0:T(8,128)(2,1)S(1)}, u32[]{:S(2)}, u32[]{:S(2)}) async-start(bf16[4,172,400]{2,1,0:T(8,128)(2,1)} %copy.515), calls=%async_computation.10 | async-start | bytes 1441792 | tf_op jit(solution)/shard_map/all_to_all | solution.py:266
  275.1 39.5 %all-to-all-start.7 = ((bf16[4,256,1600]{1,2,0:T(8,128)(2,1)}), bf16[4,256,1600]{1,2,0:T(8,128)(2,1)}, u32[]{:S(2)}, u32[]{:S(2)}) async-start(bf16[4,256,1600]{1,2,0:T(8,128)(2,1)} %bitcast.249), calls=%async_computation.7 | async-start | bytes 6553600 | tf_op jit(solution)/shard_map/all_to_all | solution.py:266
  279.8 146.0 %all-gather.18.cloned.1.call-start = ((), (), s32[]{:S(2)}) async-start(), calls=%async_computation.37 | async-start | bytes 5271552 | tf_op jit(solution)/shard_map/all_gather | solution.py:316
  316.5 41.7 %all-to-all-start.12 = ((bf16[4,256,1600]{1,2,0:T(8,128)(2,1)}), bf16[4,256,1600]{1,2,0:T(8,128)(2,1)}, u32[]{:S(2)}, u32[]{:S(2)}) async-start(bf16[4,256,1600]{1,2,0:T(8,128)(2,1)} %broadcast_in_dim.36), calls=%async_computation.12 | async-start | bytes 6553600 | tf_op jit(solution)/shard_map/all_to_all | solution.py:266
  361.3 42.1 %all-to-all-start.8 = ((bf16[4,256,1600]{1,2,0:T(8,128)(2,1)}), bf16[4,256,1600]{1,2,0:T(8,128)(2,1)}, u32[]{:S(2)}, u32[]{:S(2)}) async-start(bf16[4,256,1600]{1,2,0:T(8,128)(2,1)} %broadcast_in_dim.35), calls=%async_computation.8 | async-start | bytes 6553600 | tf_op jit(solution)/shard_map/all_to_all | solution.py:266
  454.1 41.9 %all-to-all-start.13 = ((bf16[4,256,1600]{1,2,0:T(8,128)(2,1)}), bf16[4,256,1600]{1,2,0:T(8,128)(2,1)}, u32[]{:S(2)}, u32[]{:S(2)}) async-start(bf16[4,256,1600]{1,2,0:T(8,128)(2,1)} %bitcast.251), calls=%async_computation.13 | async-start | bytes 6553600 | tf_op jit(solution)/shard_map/all_to_all | solution.py:266
  496.0 41.8 %all-to-all-start.11 = ((bf16[4,256,1600]{1,2,0:T(8,128)(2,1)}), bf16[4,256,1600]{1,2,0:T(8,128)(2,1)}, u32[]{:S(2)}, u32[]{:S(2)}) async-start(bf16[4,256,1600]{1,2,0:T(8,128)(2,1)} %bitcast.250), calls=%async_computation.11 | async-start | bytes 6553600 | tf_op jit(solution)/shard_map/all_to_all | solution.py:266
  500.8 371.5 %reduce-scatter.20.cloned.1.call-start = ((), (), s32[]{:S(2)}) async-start(), calls=%async_computation.42 | async-start | bytes 5271552 | tf_op jit(solution)/shard_map/reduce_scatter | solution.py:320
  549.5 42.1 %all-to-all-start.15 = ((bf16[4,256,1600]{1,2,0:T(8,128)(2,1)}), bf16[4,256,1600]{1,2,0:T(8,128)(2,1)}, u32[]{:S(2)}, u32[]{:S(2)}) async-start(bf16[4,256,1600]{1,2,0:T(8,128)(2,1)} %broadcast_in_dim.37), calls=%async_computation.15 | async-start | bytes 6553600 | tf_op jit(solution)/shard_map/all_to_all | solution.py:266
  719.8 160.0 %reduce-scatter.22.cloned.1.call-start = ((), (), s32[]{:S(2)}) async-start(), calls=%async_computation.43 | async-start | bytes 2304000
  763.0 41.7 %all-to-all-start.18 = ((bf16[4,256,1600]{1,2,0:T(8,128)(2,1)}), bf16[4,256,1600]{1,2,0:T(8,128)(2,1)}, u32[]{:S(2)}, u32[]{:S(2)}) async-start(bf16[4,256,1600]{1,2,0:T(8,128)(2,1)} %bitcast.248), calls=%async_computation.18 | async-start | bytes 6553600 | tf_op jit(solution)/shard_map/all_to_all | solution.py:266
  767.9 114.7 %reduce-scatter.12.cloned.1.call-start = ((), (), s32[]{:S(2)}) async-start(), calls=%async_computation.38 | async-start | bytes 1843200 | tf_op jit(solution)/shard_map/reduce_scatter | solution.py:320
  813.5 84.3 %reduce-scatter.16.cloned.1.call-start = ((), (), s32[]{:S(2)}) async-start(), calls=%async_computation.40 | async-start | bytes 3354624 | tf_op jit(solution)/shard_map/reduce_scatter | solution.py:320
  821.3 129.7 %reduce-scatter.24.cloned.1.call-start = ((), (), s32[]{:S(2)}) async-start(), calls=%async_computation.44 | async-start | bytes 5990400
  827.7 189.3 %reduce-scatter.14.cloned.1.call-start = ((), (), s32[]{:S(2)}) async-start(), calls=%async_computation.39 | async-start | bytes 6451200 | tf_op jit(solution)/shard_map/reduce_scatter | solution.py:320
  839.5 273.9 %reduce-scatter.18.cloned.1.call-start = ((), (), s32[]{:S(2)}) async-start(), calls=%async_computation.41 | async-start | bytes 10137600 | tf_op jit(solution)/shard_map/reduce_scatter | solution.py:320
  902.3 52.9 %all-to-all-start.22 = ((bf16[4,100,400]{1,2,0:T(8,128)(2,1)}), bf16[4,100,400]{1,2,0:T(8,128)(2,1)S(1)}, u32[]{:S(2)}, u32[]{:S(2)}) async-start(bf16[4,100,400]{1,2,0:T(8,128)(2,1)} %bitcast.300), calls=%async_computation.25 | async-start | bytes 819200 | tf_op jit(solution)/shard_map/all_to_all | solution.py:266
  955.2 64.5 %all-to-all-start.20 = ((bf16[4,200,400]{2,1,0:T(8,128)(2,1)}), bf16[4,200,400]{2,1,0:T(8,128)(2,1)S(1)}, u32[]{:S(2)}, u32[]{:S(2)}) async-start(bf16[4,200,400]{2,1,0:T(8,128)(2,1)} %bitcast.235), calls=%async_computation.21 | async-start | bytes 1638400 | tf_op jit(solution)/shard_map/all_to_all | solution.py:266
  1019.7 101.7 %all-to-all-start.21 = ((bf16[4,200,400]{1,2,0:T(8,128)(2,1)}), bf16[4,200,400]{1,2,0:T(8,128)(2,1)}, u32[]{:S(2)}, u32[]{:S(2)}) async-start(bf16[4,200,400]{1,2,0:T(8,128)(2,1)} %bitcast.59), calls=%async_computation.23 | async-start | bytes 1638400 | tf_op jit(solution)/shard_map/all_to_all | solution.py:266
  (130 other events, 2205.1 us)
Sparse Core Ops, SparseCore 0:
  10.9 35.1 all-gather.7
  48.3 59.2 all-gather.11
  109.8 35.6 all-gather.13
  147.5 55.5 all-gather.9
  205.2 86.0 all-gather.15
  293.4 49.8 all-gather.17
  512.1 56.4 reduce-scatter.19
  727.3 40.2 reduce-scatter.21
  813.6 34.4 reduce-scatter.11
  850.4 37.3 reduce-scatter.15
  890.2 60.8 reduce-scatter.23
  953.2 63.7 reduce-scatter.13
  1019.3 94.1 reduce-scatter.17

commit v2 on v1

v2 whole, which is shorter than its diff:
```python
import functools

import jax
import jax.numpy as jnp
from jax import lax
from jax.experimental import pallas as pl
from jax.experimental.pallas import tpu as pltpu
from jax.sharding import PartitionSpec as P

KV = 5
HEAD = 64
GROUP = 5
INNER = 3200
STATE = 16
CONV = 4
RANK = 100
FF = 5504
BLOCK = 128
LANES = 128


epsilon = 1e-06
beta_first = 0.9
beta_second = 0.95
adam_floor = 1e-08
learn_rate = 0.01
weight_decay = 0.1
masked_score = -1e30


def product(left, right):
    return jnp.dot(left, right, preferred_element_type=jnp.float32)


def product_tn(left, right):
    return lax.dot_general(
        left, right, (((0,), (0,)), ((), ())), preferred_element_type=jnp.float32
    )


def product_nt(left, right):
    return lax.dot_general(
        left, right, (((1,), (1,)), ((), ())), preferred_element_type=jnp.float32
    )


def sigmoid(values):
    return 1.0 / (1.0 + jnp.exp(-values))


def silu_act(values):
    return values / (1.0 + jnp.exp(-values))


def silu_slope(values):
    gate_sig = sigmoid(values)
    return gate_sig * (1.0 + values * (1.0 - gate_sig))


def rms_scale(values):
    return lax.rsqrt(jnp.mean(values * values, axis=-1, keepdims=True) + epsilon)


def rms_back(values, scale, gain, incoming):
    weighted = incoming * gain
    inner_mean = jnp.mean(weighted * values, axis=-1, keepdims=True)
    return (
        scale * weighted - values * (scale * scale * scale) * inner_mean,
        jnp.sum(incoming * values * scale, axis=0),
    )


def shift_rows(values, lag):
    if lag == 0:
        return values
    return jnp.concatenate(
        [jnp.zeros((lag, values.shape[1]), values.dtype), values[: values.shape[0] - lag]], axis=0
    )


def unshift_rows(values, lag):
    if lag == 0:
        return values
    return jnp.concatenate([values[lag:], jnp.zeros((lag, values.shape[1]), values.dtype)], axis=0)


def row_sums(parts):
    rows = lax.broadcasted_iota(jnp.int32, (8, LANES), 0)
    quads = []
    low = rows < 4
    for i in range(4):
        a, b = parts[i], parts[i + 4]
        quads.append(jnp.where(low, a, b) + pltpu.roll(jnp.where(low, b, a), 4, 0))
    pairs = []
    low = (rows & 3) < 2
    for i in range(2):
        a, b = quads[i], quads[i + 2]
        pairs.append(jnp.where(low, a + pltpu.roll(a, 6, 0), b + pltpu.roll(b, 2, 0)))
    a, b = pairs
    return jnp.where((rows & 1) < 1, a + pltpu.roll(a, 7, 0), b + pltpu.roll(b, 1, 0))


def fold_rows_in(values):
    return values[:8] + values[8:]


def lane_tiles(width):
    return [slice(k * LANES, (k + 1) * LANES) for k in range(width // LANES)]


def scan_kernel(
    keep_ref,
    step_ref,
    conv_ref,
    inject_ref,
    read_ref,
    rates_ref,
    out_ref,
    start_ref,
    inject_wide_ref,
    read_wide_ref,
    state_ref,
):
    at = pl.program_id(0)
    tiles = lane_tiles(step_ref.shape[1])

    @pl.when(at == 0)
    def _():
        state_ref[...] = jnp.zeros_like(state_ref)

    state_ref[...] = state_ref[...] * keep_ref[at]
    start_ref[0] = state_ref[...]
    rates = [rates_ref[:, tile] for tile in tiles]

    def group(turn, state):
        base = pl.multiple_of(turn * 8, 8)
        state = list(state)
        steps = [step_ref[pl.ds(base, 8), tile] for tile in tiles]
        pushes = [
            steps[k] * conv_ref[pl.ds(base, 8), tile] for k, tile in enumerate(tiles)
        ]
        parts = [[] for _ in tiles]
        turned = [pltpu.roll(ref[...], BLOCK - base, 1) for ref in (inject_ref, read_ref)]
        for i in range(8):
            inject, read = [
                jnp.broadcast_to(values[:, i : i + 1], (STATE, LANES)) for values in turned
            ]
            inject_wide_ref[base + i], read_wide_ref[base + i] = inject, read
            for k in range(len(tiles)):
                decay = jnp.exp(steps[k][i : i + 1] * rates[k])
                state[k] = decay * state[k] + pushes[k][i : i + 1] * inject
                parts[k].append(fold_rows_in(state[k] * read))
        for k, tile in enumerate(tiles):
            out_ref[pl.ds(base, 8), tile] = row_sums(parts[k])
        return tuple(state)

    state = lax.fori_loop(0, BLOCK // 8, group, tuple(state_ref[:, tile] for tile in tiles))
    for k, tile in enumerate(tiles):
        state_ref[:, tile] = state[k]


def scan_forward(keep, step, conv, inject, read, rates):
    rows, width = step.shape
    blocks = rows // BLOCK
    row_spec = pl.BlockSpec((BLOCK, width), lambda i, *_: (i, 0))
    state_spec = pl.BlockSpec((STATE, BLOCK), lambda i, *_: (0, i))
    wide_spec = pl.BlockSpec((BLOCK, STATE, LANES), lambda i, *_: (i, 0, 0))
    return pl.pallas_call(
        scan_kernel,
        grid_spec=pltpu.PrefetchScalarGridSpec(
            num_scalar_prefetch=1,
            grid=(blocks,),
            in_specs=[
                row_spec,
                row_spec,
                state_spec,
                state_spec,
                pl.BlockSpec((STATE, width), lambda i, *_: (0, 0)),
            ],
            out_specs=[
                row_spec,
                pl.BlockSpec((1, STATE, width), lambda i, *_: (i, 0, 0)),
                wide_spec,
                wide_spec,
            ],
            scratch_shapes=[pltpu.VMEM((STATE, width), jnp.float32)],
        ),
        out_shape=[
            jax.ShapeDtypeStruct((rows, width), jnp.float32),
            jax.ShapeDtypeStruct((blocks, STATE, width), jnp.float32),
        ]
        + [jax.ShapeDtypeStruct((rows, STATE, LANES), jnp.float32)] * 2,
        cost_estimate=pl.CostEstimate(
            flops=30 * rows * STATE * width,
            bytes_accessed=140 * rows * width,
            transcendentals=rows * STATE * width,
        ),
        compiler_params=pltpu.CompilerParams(vmem_limit_bytes=24 * 2**20),
        name="state_scan",
    )(keep, step, conv, inject, read, rates)


def back_kernel(
    keep_ref,
    step_ref,
    conv_ref,
    inject_ref,
    read_ref,
    rates_ref,
    grad_ref,
    start_ref,
    gstep_ref,
    gconv_ref,
    ginject_ref,
    gread_ref,
    grate_ref,
    later_ref,
    history_ref,
    decay_ref,
    sums_ref,
):
    tiles = lane_tiles(step_ref.shape[1])
    at = pl.num_programs(0) - 1 - pl.program_id(0)

    @pl.when(pl.program_id(0) == 0)
    def _():
        later_ref[...] = jnp.zeros_like(later_ref)
        grate_ref[...] = jnp.zeros_like(grate_ref)

    def forward(turn, state):
        base = pl.multiple_of(turn * 8, 8)
        state = list(state)
        steps = [step_ref[pl.ds(base, 8), tile] for tile in tiles]
        pushes = [
            steps[k] * conv_ref[pl.ds(base, 8), tile] for k, tile in enumerate(tiles)
        ]
        for i in range(8):
            inject = inject_ref[base + i]
            for k, tile in enumerate(tiles):
                decay = jnp.exp(steps[k][i : i + 1] * rates_ref[:, tile])
                decay_ref[base + i, :, tile] = decay
                history_ref[base + i, :, tile] = state[k]
                state[k] = decay * state[k] + pushes[k][i : i + 1] * inject
        return tuple(state)

    state = lax.fori_loop(
        0, BLOCK // 8, forward, tuple(start_ref[0, :, tile] for tile in tiles)
    )
    for k, tile in enumerate(tiles):
        history_ref[BLOCK, :, tile] = state[k]

    def backward(turn, later):
        base = pl.multiple_of((BLOCK // 8 - 1 - turn) * 8, 8)
        later = list(later)
        steps = [step_ref[pl.ds(base, 8), tile] for tile in tiles]
        convs = [conv_ref[pl.ds(base, 8), tile] for tile in tiles]
        grads = [grad_ref[pl.ds(base, 8), tile] for tile in tiles]
        pushes = [steps[k] * convs[k] for k in range(len(tiles))]
        pulls = [[None] * 8 for _ in tiles]
        drives = [[None] * 8 for _ in tiles]
        rate_sums = [None for _ in tiles]
        for i in range(7, -1, -1):
            sums = [None, None]
            inject, read = inject_ref[base + i], read_ref[base + i]
            for k, tile in enumerate(tiles):
                grad = grads[k][i : i + 1]
                total = read * grad + later[k]
                later[k] = decay_ref[base + i, :, tile] * total
                pull = later[k] * history_ref[base + i, :, tile]
                pulls[k][i] = fold_rows_in(pull * rates_ref[:, tile])
                drives[k][i] = fold_rows_in(total * inject)
                terms = [total * pushes[k][i : i + 1], history_ref[base + i + 1, :, tile] * grad]
                sums = [term if old is None else old + term for old, term in zip(sums, terms)]
                term = pull * steps[k][i : i + 1]
                rate_sums[k] = term if rate_sums[k] is None else rate_sums[k] + term
            sums_ref[0, base + i], sums_ref[1, base + i] = sums
        for k, tile in enumerate(tiles):
            grate_ref[:, tile] += rate_sums[k]
            drive = row_sums(drives[k])
            gstep_ref[pl.ds(base, 8), tile] = row_sums(pulls[k]) + drive * convs[k]
            gconv_ref[pl.ds(base, 8), tile] = drive * steps[k]
        return tuple(later)

    later = lax.fori_loop(
        0, BLOCK // 8, backward, tuple(later_ref[:, tile] for tile in tiles)
    )
    ones = jnp.ones((LANES, LANES), jnp.bfloat16)
    lane = lax.broadcasted_iota(jnp.int32, (STATE, BLOCK), 1)
    ginject_ref[...] = jnp.zeros_like(ginject_ref)
    gread_ref[...] = jnp.zeros_like(gread_ref)

    def lane_sums(turn, none):
        base = pl.multiple_of(turn * 32, 32)
        for which, ref in enumerate((ginject_ref, gread_ref)):
            values = sums_ref[which, pl.ds(base, 32)].reshape(32 * STATE, LANES)
            high = values.astype(jnp.bfloat16)
            rest = (values - high.astype(jnp.float32)).astype(jnp.bfloat16)
            totals = jnp.dot(high, ones, preferred_element_type=jnp.float32) + jnp.dot(
                rest, ones, preferred_element_type=jnp.float32
            )
            kept = ref[...]
            for i in range(32):
                kept = jnp.where(lane == base + i, totals[i * STATE : (i + 1) * STATE], kept)
            ref[...] = kept
        return none

    lax.fori_loop(0, BLOCK // 32, lane_sums, 0)
    for k, tile in enumerate(tiles):
        later_ref[:, tile] = later[k] * keep_ref[at]


def scan_backward(keep, step, conv, inject, read, rates, grad, starts):
    rows, width = step.shape
    blocks = rows // BLOCK
    row_spec = pl.BlockSpec((BLOCK, width), lambda i, *_: (blocks - 1 - i, 0))
    wide_spec = pl.BlockSpec((BLOCK, STATE, LANES), lambda i, *_: (blocks - 1 - i, 0, 0))
    all_spec = pl.BlockSpec((STATE, width), lambda i, *_: (0, 0))
    flat_spec = pl.BlockSpec((STATE, BLOCK), lambda i, *_: (0, blocks - 1 - i))
    return pl.pallas_call(
        back_kernel,
        grid_spec=pltpu.PrefetchScalarGridSpec(
            num_scalar_prefetch=1,
            grid=(blocks,),
            in_specs=[
                row_spec,
                row_spec,
                wide_spec,
                wide_spec,
                all_spec,
                row_spec,
                pl.BlockSpec((1, STATE, width), lambda i, *_: (blocks - 1 - i, 0, 0)),
            ],
            out_specs=[row_spec, row_spec, flat_spec, flat_spec, all_spec],
            scratch_shapes=[
                pltpu.VMEM((STATE, width), jnp.float32),
                pltpu.VMEM((BLOCK + 1, STATE, width), jnp.float32),
                pltpu.VMEM((BLOCK, STATE, width), jnp.float32),
                pltpu.VMEM((2, BLOCK, STATE, LANES), jnp.float32),
            ],
        ),
        out_shape=[jax.ShapeDtypeStruct((rows, width), jnp.float32)] * 2
        + [jax.ShapeDtypeStruct((STATE, rows), jnp.float32)] * 2
        + [jax.ShapeDtypeStruct((STATE, width), jnp.float32)],
        cost_estimate=pl.CostEstimate(
            flops=60 * rows * STATE * width,
            bytes_accessed=260 * rows * width,
            transcendentals=rows * STATE * width,
        ),
        compiler_params=pltpu.CompilerParams(vmem_limit_bytes=40 * 2**20),
        name="state_back",
    )(keep, step, conv, inject, read, rates, grad, starts)


def adam_kernel(
    fix_ref, weight_ref, grad_ref, first_ref, second_ref, out_ref, mean_ref, square_ref, delta_ref
):
    gradient = grad_ref[...].astype(jnp.float32)
    out_ref[...] = gradient
    mean_new = beta_first * first_ref[...] + (1.0 - beta_first) * gradient
    square_new = beta_second * second_ref[...] + (1.0 - beta_second) * gradient * gradient
    mean_ref[...] = mean_new
    square_ref[...] = square_new
    delta_ref[...] = -learn_rate * (
        mean_new / fix_ref[0] / (jnp.sqrt(square_new / fix_ref[1]) + adam_floor)
        + weight_decay * weight_ref[...].astype(jnp.float32)
    )


def adam_rows(weight, gradient, first_old, second_old, step_float):
    rows, width = weight.shape
    across = -(-rows // LANES) * LANES * width < -(-width // LANES) * LANES * rows
    operands = (weight, gradient, first_old, second_old)
    if across:
        operands = tuple(values.T for values in operands)
        rows, width = width, rows
    sizes = [n for n in range(8, rows, 8) if rows % n == 0 and n * width <= 2**17]
    size = max(sizes, default=rows)
    fixes = jnp.stack(
        [1.0 - jnp.power(beta_first, step_float), 1.0 - jnp.power(beta_second, step_float)]
    )
    spec = pl.BlockSpec((size, width), lambda i, *_: (i, 0))
    results = pl.pallas_call(
        adam_kernel,
        grid_spec=pltpu.PrefetchScalarGridSpec(
            num_scalar_prefetch=1, grid=(rows // size,), in_specs=[spec] * 4, out_specs=[spec] * 4
        ),
        out_shape=[jax.ShapeDtypeStruct((rows, width), jnp.float32)] * 4,
        cost_estimate=pl.CostEstimate(
            flops=20 * rows * width, bytes_accessed=28 * rows * width, transcendentals=rows * width
        ),
        compiler_params=pltpu.CompilerParams(vmem_limit_bytes=16 * 2**20),
        name="adam_rows",
    )(fixes, *operands)
    return [values.T for values in results] if across else results


def by_place(body):
    def kernel(here_ref, *refs):
        for here in range(4):
            pl.when(here_ref[0] == here)(functools.partial(body, here, *refs))

    return kernel


def column_runs(values, starts, width, padding=0):
    parts = []
    for start in starts:
        parts.append(values[:, start : start + width])
        if padding:
            parts.append(jnp.zeros((values.shape[0], padding), values.dtype))
    return jnp.concatenate(parts, axis=1)


def place_call(body, here, operands, shapes, name):
    return pl.pallas_call(
        by_place(body),
        grid_spec=pltpu.PrefetchScalarGridSpec(
            num_scalar_prefetch=1,
            in_specs=[pl.BlockSpec(memory_space=pltpu.VMEM)] * len(operands),
            out_specs=[pl.BlockSpec(memory_space=pltpu.VMEM)] * len(shapes),
        ),
        out_shape=shapes,
        compiler_params=pltpu.CompilerParams(vmem_limit_bytes=24 * 2**20),
        name=name,
    )(here, *operands)


def split_columns(shard, here, starts_of, width):
    count = len(starts_of(0)) * width

    def body(here, shard_ref, *piece_refs):
        values = shard_ref[...].astype(jnp.float32)
        for j, ref in enumerate(piece_refs):
            ref[...] = column_runs(values, starts_of(here ^ j), width).astype(ref.dtype)

    shapes = [jax.ShapeDtypeStruct((shard.shape[0], count), shard.dtype)] * 4
    return place_call(body, here, [shard], shapes, "split_columns")


def join_columns(pieces, here, width, wide):
    rows, count = pieces[0].shape
    runs = count // width

    def body(here, *refs):
        values = [ref[...].astype(jnp.float32) for ref in refs[:4]]
        refs[4][...] = jnp.concatenate(
            [
                column_runs(values[here ^ i], [r * width for r in range(runs)], width, wide - width)
                for i in range(4)
            ],
            axis=1,
        ).astype(refs[4].dtype)

    shape = jax.ShapeDtypeStruct((rows, 4 * runs * wide), pieces[0].dtype)
    return place_call(body, here, pieces, [shape], "join_columns")[0]


def split_rows(shard, here):
    part = shard.shape[0] // 4

    def body(here, shard_ref, *piece_refs):
        values = shard_ref[...].astype(jnp.float32)
        for j, ref in enumerate(piece_refs):
            i = here ^ j
            ref[...] = values[i * part : (i + 1) * part].astype(ref.dtype)

    shapes = [jax.ShapeDtypeStruct((part, shard.shape[1]), shard.dtype)] * 4
    return place_call(body, here, [shard], shapes, "split_rows")


def join_side(pieces, here, wide):
    part, width = pieces[0].shape

    def body(here, *refs):
        values = jnp.concatenate(
            [refs[here ^ i][...].astype(jnp.float32) for i in range(4)], axis=1
        )
        refs[4][:part] = values.astype(refs[4].dtype)
        if wide > part:
            refs[4][part:] = jnp.zeros((wide - part, 4 * width), refs[4].dtype)

    shape = jax.ShapeDtypeStruct((wide, 4 * width), pieces[0].dtype)
    return place_call(body, here, pieces, [shape], "join_side")[0]


def split_side(dealt, here, part):
    width = dealt.shape[1] // 4

    def body(here, dealt_ref, *piece_refs):
        values = dealt_ref[:part].astype(jnp.float32)
        for j, ref in enumerate(piece_refs):
            i = here ^ j
            ref[...] = values[:, i * width : (i + 1) * width].astype(ref.dtype)

    shapes = [jax.ShapeDtypeStruct((part, width), dealt.dtype)] * 4
    return place_call(body, here, [dealt], shapes, "split_side")


def join_rows(pieces, here):
    part, width = pieces[0].shape

    def body(here, *refs):
        refs[4][...] = jnp.concatenate(
            [refs[here ^ i][...].astype(jnp.float32) for i in range(4)], axis=0
        ).astype(refs[4].dtype)

    shape = jax.ShapeDtypeStruct((4 * part, width), pieces[0].dtype)
    return place_call(body, here, pieces, [shape], "join_rows")[0]


def join_back(pieces, here, part):
    rows, count = pieces[0].shape
    runs = count // part

    def body(here, *refs):
        values = [ref[...].astype(jnp.float32) for ref in refs[:4]]
        refs[4][...] = jnp.concatenate(
            [
                values[here ^ i][:, r * part : (r + 1) * part]
                for r in range(runs)
                for i in range(4)
            ],
            axis=1,
        ).astype(refs[4].dtype)

    shape = jax.ShapeDtypeStruct((rows, 4 * count), pieces[0].dtype)
    return place_call(body, here, pieces, [shape], "join_back")[0]


def layout(lengths, buffer_rows):
    index = jnp.arange(lengths.shape[0], dtype=jnp.int32)
    count_blocks = (lengths + (BLOCK - 1)) // BLOCK
    earlier = (index[None, :] < index[:, None]).astype(jnp.int32)
    first_block = jnp.sum(earlier * count_blocks[None, :], axis=1)
    places = jnp.arange(buffer_rows, dtype=jnp.int32)
    owner = (
        jnp.sum((first_block[None, :] <= (places // BLOCK)[:, None]).astype(jnp.int32), axis=1) - 1
    )
    pick = (owner[:, None] == index[None, :]).astype(jnp.int32)
    seq_length = jnp.sum(pick * lengths[None, :], axis=1)
    offset = places - BLOCK * jnp.sum(pick * first_block[None, :], axis=1)
    live = offset < seq_length
    begins = live & (offset == 0)
    return (owner, offset, live, begins)


def product_tt(left, right):
    return lax.dot_general(
        left, right, (((0,), (1,)), ((), ())), preferred_element_type=jnp.float32
    )


def after(values, *others):
    return lax.optimization_barrier((values, others))[0]


def swap(values, bit):
    return lax.ppermute(values, "dp", [(i, i ^ bit) for i in range(4)])


def exchange(pieces):
    if len(pieces) != 4:
        return list(lax.all_to_all(jnp.stack(pieces), "dp", 0, 0))
    return [pieces[0]] + [swap(pieces[j], j) for j in (1, 2, 3)]


def trade(pieces):
    return lax.all_to_all(pieces, "dp", 0, 0)


def spread_direct(rows, groups):
    if groups != 4:
        return list(lax.all_gather(rows, "dp", axis=0))
    return [rows] + [swap(rows, j) for j in (1, 2, 3)]


def spread(rows, groups):
    if groups != 4:
        got = lax.all_gather(rows, "dp", axis=0, tiled=True)
        return got, got
    half = rows.shape[0] // 2
    one, two = swap(rows, 1), swap(rows, 2)
    far = [swap(one[:half], 2), swap(two[half:], 1)]
    return jnp.concatenate([rows, one, two] + far, axis=0), (one, two)


def first_hop(pieces):
    if len(pieces) != 4:
        return lax.all_to_all(jnp.stack(pieces), "dp", 0, 0)
    half = pieces[0].shape[0] // 2
    return (
        swap(pieces[3][:half], 1),
        swap(pieces[3][half:], 2),
        swap(pieces[1][:half], 1),
        swap(pieces[2][half:], 2),
    )


def second_hop(pieces, hops):
    wide, kind = jnp.float32, pieces[0].dtype
    if len(pieces) != 4:
        return jnp.sum(hops.astype(wide), axis=0)
    half = pieces[0].shape[0] // 2
    one_far, two_far, one, two = hops
    top = swap((pieces[2][:half].astype(wide) + one_far.astype(wide)).astype(kind), 2)
    bottom = swap((pieces[1][half:].astype(wide) + two_far.astype(wide)).astype(kind), 1)
    own = pieces[0].astype(wide)
    return jnp.concatenate(
        [
            own[:half] + one.astype(wide) + top.astype(wide),
            own[half:] + two.astype(wide) + bottom.astype(wide),
        ],
        axis=0,
    )


def collect(pieces):
    return second_hop(pieces, first_hop(pieces))


def whole_small(values, ranks):
    if ranks != 8:
        return lax.all_gather(values, "shard", axis=1, tiled=True)
    width = values.shape[1]
    slots = jnp.zeros((values.shape[0], ranks * width), values.dtype)
    slots = lax.dynamic_update_slice_in_dim(
        slots, values, lax.axis_index("shard") * width, axis=1
    )
    for step in (1, 2, 4):
        slots = slots + lax.ppermute(slots, "shard", [(i, i ^ step) for i in range(ranks)])
    return slots


def everyone(values, groups, ranks):
    if groups != 4:
        return lax.psum(values, ("dp", "shard"))
    values = values + swap(values, 1)
    values = values + swap(values, 2)
    step = 1
    while step < ranks:
        values = values + lax.ppermute(values, "shard", [(i, i ^ step) for i in range(ranks)])
        step *= 2
    return values


def row_pieces(partial, groups):
    rows = partial.shape[0] // groups
    return [partial[j * rows : (j + 1) * rows] for j in range(groups)]


def everywhere(partial, groups):
    if groups != 4:
        return lax.psum(partial, "dp")
    rows, width = partial.shape
    part = width // 4

    def turn(values, bit):
        return jnp.concatenate(
            [values[:, (j ^ bit) * part : ((j ^ bit) + 1) * part] for j in range(4)], axis=1
        )

    half = rows // 16 * 8
    top, bottom = partial[:half], partial[half:]
    top = top + swap(turn(top, 1), 1)
    bottom = bottom + swap(turn(bottom, 2), 2)
    top = top + swap(turn(top, 2), 2)
    bottom = bottom + swap(turn(bottom, 1), 1)
    return jnp.concatenate([top, bottom], axis=0)


def padded_part(part, ranks):
    unit = max(8, LANES // ranks)
    return -(-part // unit) * unit


def deal_columns(shard, here, groups, part, wide_part):
    rows, width = shard.shape
    runs = width // (groups * part)
    if groups == 4:
        starts = lambda i: [(r * groups + i) * part for r in range(runs)]
        pieces = exchange(split_columns(shard, here, starts, part))
        return join_columns(pieces, here, part, wide_part)
    pieces = shard.reshape(rows, runs, groups, part).transpose(2, 0, 1, 3)
    got = trade(pieces.reshape(groups, rows, runs * part)).transpose(1, 0, 2)
    got = jnp.pad(got.reshape(rows, groups * runs, part), ((0, 0), (0, 0), (0, wide_part - part)))
    return got.reshape(rows, groups * runs * wide_part)


def return_columns(dealt, here, groups, part, wide_part):
    rows, width = dealt.shape
    runs = width // (groups * wide_part)
    if groups == 4:
        starts = lambda i: [(i * runs + r) * wide_part for r in range(runs)]
        return join_back(exchange(split_columns(dealt, here, starts, part)), here, part)
    pieces = dealt.reshape(rows, groups * runs, wide_part)[:, :, :part]
    got = trade(pieces.reshape(rows, groups, runs * part).transpose(1, 0, 2))
    return got.reshape(groups, rows, runs, part).transpose(1, 2, 0, 3).reshape(rows, -1)


def deal_rows(shard, here, groups, wide_part):
    rows, width = shard.shape
    part = rows // groups
    if groups == 4:
        return join_side(exchange(split_rows(shard, here)), here, wide_part)
    got = trade(shard.reshape(groups, part, width))
    got = got.transpose(1, 0, 2).reshape(part, groups * width)
    return jnp.pad(got, ((0, wide_part - part), (0, 0)))


def return_rows(dealt, here, groups, part):
    width = dealt.shape[1]
    if groups == 4:
        return join_rows(exchange(split_side(dealt, here, part)), here)
    got = trade(dealt[:part].reshape(part, groups, width // groups).transpose(1, 0, 2))
    return got.reshape(groups * part, width // groups)


def beside(pieces, here):
    if len(pieces) != 4:
        return jnp.concatenate(pieces, axis=1)
    return join_side(pieces, here, pieces[0].shape[0])


def apart(values, here, groups):
    if groups != 4:
        return jnp.split(values, groups, axis=1)
    return split_side(values, here, values.shape[0])


def whole(shard):
    return lax.all_gather(shard, "shard", axis=0, tiled=True)


def owned_sum(partial):
    return lax.psum_scatter(partial, "shard", scatter_dimension=0, tiled=True)


def shards(
    groups,
    ranks,
    tokens,
    cotangent,
    lengths,
    step_count,
    norm_gains,
    qkv_weight,
    attn_weight,
    mixer_in,
    mixer_table,
    mixer_out,
    ffn_in,
    ffn_out,
    first_gains,
    first_qkv,
    first_attn,
    first_mixin,
    first_table,
    first_mixout,
    first_ffnin,
    first_ffnout,
    second_gains,
    second_qkv,
    second_attn,
    second_mixin,
    second_table,
    second_mixout,
    second_ffnin,
    second_ffnout,
):
    low = jnp.bfloat16
    buffer_rows = tokens.shape[0]
    model_width = tokens.shape[1]
    at = lax.axis_index("dp")
    here = at.reshape(1)
    part_inner = INNER // groups // ranks
    part_hidden = FF // groups // ranks
    wide_inner = padded_part(part_inner, ranks)
    wide_hidden = padded_part(part_hidden, ranks)
    inner = wide_inner * ranks
    hidden_units = wide_hidden * ranks
    part_model = model_width // ranks
    table_width = mixer_table.shape[1]
    gain_count = norm_gains.shape[1]

    qkv_width = qkv_weight.shape[1]
    attn_width = attn_weight.shape[1]
    table_part = lax.dynamic_slice_in_dim(mixer_table, at * part_inner, part_inner, axis=0)
    table_part = jnp.pad(
        table_part, ((0, part_model - part_inner), (0, 2 * LANES - table_width))
    )
    gain_cols = whole_small(norm_gains.astype(jnp.float32).T, ranks)
    mixer_pack = jnp.concatenate(
        [deal_columns(mixer_in, here, groups, part_inner, wide_inner), table_part], axis=1
    )
    mixer_early = whole(mixer_pack)
    lengths_all = jnp.concatenate(spread_direct(lengths, groups), axis=0)
    owner, offset, live, _ = layout(lengths[0], buffer_rows)
    live_rows = live.astype(jnp.float32)
    places = jnp.arange(buffer_rows, dtype=jnp.int32)
    allowed = (owner[:, None] == owner[None, :]) & (places[None, :] <= places[:, None]) & live[
        None, :
    ] | (places[:, None] == places[None, :])
    _, offset_all, _, begins_all = jax.vmap(lambda row: layout(row, buffer_rows))(lengths_all)
    offset_all = offset_all.reshape(-1)
    block_starts = begins_all[:, ::BLOCK] | (jnp.arange(buffer_rows // BLOCK) == 0)[None, :]
    block_keep = 1.0 - block_starts.reshape(-1).astype(jnp.float32)

    inputs = tokens.astype(jnp.float32)
    scale_in = rms_scale(inputs)
    normed = (inputs * scale_in * gain_cols[0]).astype(low)
    normed_all, near_rows = spread(after(normed, mixer_pack), groups)
    attn_rows = beside(spread_direct(attn_weight, groups), here)
    dealt_mix = deal_rows(after(mixer_out, near_rows), here, groups, wide_inner)
    dealt_up = deal_columns(after(ffn_in, near_rows), here, groups, part_hidden, wide_hidden)
    mixer_full = after(mixer_early, normed_all, dealt_mix, dealt_up)
    weight_in = mixer_full[:, : 2 * inner]
    table_low = mixer_full[:, 2 * inner :].reshape(ranks, part_model, 2 * LANES)[:, :part_inner]
    table_low = jnp.pad(
        table_low[:, :, :table_width], ((0, 0), (0, wide_inner - part_inner), (0, 0))
    ).reshape(inner, table_width)

    heads_full = whole(jnp.concatenate([after(qkv_weight, mixer_full), attn_rows], axis=1))
    weight_qkv, weight_attn = heads_full[:, :qkv_width], heads_full[:, qkv_width:]
    grad_out = cotangent.astype(jnp.float32) * live_rows[:, None]

    mixed = product(normed_all, weight_in)
    weight_mix, weight_up = whole(after(dealt_mix, mixed)), whole(after(dealt_up, mixed))
    xin = mixed[:, :inner]
    gate_z = mixed[:, inner:]
    table = table_low.astype(jnp.float32)
    tap_masks = [(offset_all >= lag).astype(jnp.float32)[:, None] for lag in range(CONV)]
    taps = [shift_rows(xin, lag) * tap_masks[lag] for lag in range(CONV)]
    conv_pre = table[:, CONV]
    for lag in range(CONV):
        conv_pre = conv_pre + table[:, lag] * taps[lag]
    conv_low = silu_act(conv_pre).astype(low)
    conv_out = conv_low.astype(jnp.float32)
    proj_start = CONV + 3 + STATE
    input_proj = table_low[:, proj_start : proj_start + RANK + 2 * STATE]
    step_proj = table_low[:, proj_start + RANK + 2 * STATE :]
    double_part = product_tt(input_proj, conv_low)
    double = everywhere(double_part, groups)
    dealt_down = deal_rows(after(ffn_out, double), here, groups, wide_hidden)
    weight_down = whole(dealt_down)

    heads_part = product(after(normed_all, double_part), weight_qkv).astype(low)
    heads_part = after(heads_part, double)
    heads_low = beside(exchange(row_pieces(heads_part, groups)), here)
    kv_width = KV * HEAD
    query = heads_low[:, :model_width].reshape(buffer_rows, KV, GROUP, HEAD)
    key_rows = heads_low[:, model_width : model_width + kv_width].reshape(buffer_rows, KV, HEAD)
    value_rows = heads_low[:, model_width + kv_width :].reshape(buffer_rows, KV, HEAD)
    factor = HEAD ** (-0.5)

    def masked_scores():
        raw_scores = (
            jnp.einsum("qkgd,skd->kgqs", query, key_rows, preferred_element_type=jnp.float32)
            * factor
        )
        return jnp.where(allowed, raw_scores, masked_score)

    scores = masked_scores()
    top_score = jnp.max(scores, axis=-1, keepdims=True)
    log_total = top_score + jnp.log(jnp.sum(jnp.exp(scores - top_score), axis=-1, keepdims=True))
    probs_low = jnp.exp(scores - log_total).astype(low)
    context = (
        jnp.einsum("kgqs,skd->qkgd", probs_low, value_rows, preferred_element_type=jnp.float32)
        .reshape(buffer_rows, model_width)
        .astype(low)
    )
    attn_raw = product(context, weight_attn)
    scale_attn = rms_scale(attn_raw)

    rank_part = double[:RANK].astype(low)
    inject = double[RANK : RANK + STATE]
    readout = double[RANK + STATE :]
    dt_pre = product_tt(rank_part, step_proj) + table[:, CONV + 1]
    step_size = jnp.log1p(jnp.exp(dt_pre))
    rates = -jnp.exp(table[:, CONV + 3 : CONV + 3 + STATE]).T
    states_out, block_begins, inject_wide, readout_wide = scan_forward(
        block_keep, step_size, conv_out, inject, readout, rates
    )
    skip_weight = table[:, CONV + 2]
    scanned = states_out + skip_weight * conv_out
    silu_z = silu_act(gate_z)
    gated_low = (scanned * silu_z).astype(low)
    gated_low = after(gated_low, heads_low, dealt_down)
    mamba_raw = collect(row_pieces(product(gated_low, weight_mix).astype(low), groups))
    mamba_raw = after(mamba_raw, attn_raw)
    scale_mamba = rms_scale(mamba_raw)
    hidden = inputs + 0.5 * (
        attn_raw * scale_attn * gain_cols[1] + mamba_raw * scale_mamba * gain_cols[2]
    )
    scale_hidden = rms_scale(hidden)
    normed_two = (hidden * scale_hidden * gain_cols[3]).astype(low)

    normed_two_all, _ = spread(normed_two, groups)
    grad_ffn_pieces = spread_direct(after(grad_out.astype(low), normed_two_all), groups)
    both = product(normed_two_all, weight_up)
    both, grad_ffn_pieces = lax.optimization_barrier((both, grad_ffn_pieces))
    grad_ffn_all = jnp.concatenate(grad_ffn_pieces, axis=0)
    gate_ffn = both[:, :hidden_units]
    up_ffn = both[:, hidden_units:]
    act_low = (silu_act(gate_ffn) * up_ffn).astype(low)
    grad_act = product_nt(grad_ffn_all, weight_down)
    gate_sig = sigmoid(gate_ffn)
    grad_gate = grad_act * up_ffn * gate_sig * (1.0 + gate_ffn * (1.0 - gate_sig))
    grad_up = grad_act * silu_act(gate_ffn)
    grad_both = jnp.concatenate([grad_gate, grad_up], axis=1).astype(low)
    grad_second = product_nt(grad_both, weight_up).astype(low)
    grad_up_w = product_tn(after(normed_two_all, grad_second), grad_both).astype(low)
    grad_down_w = product_tn(act_low, after(grad_ffn_all, grad_up_w)).astype(low)
    grad_second = collect(row_pieces(grad_second, groups))
    grad_second = after(grad_second, grad_up_w, grad_down_w)
    back_hidden, gain_three = rms_back(hidden, scale_hidden, gain_cols[3], grad_second)
    grad_hidden = grad_out + back_hidden
    half_grad = 0.5 * grad_hidden
    grad_mamba_full, gain_two = rms_back(mamba_raw, scale_mamba, gain_cols[2], half_grad)
    grad_mamba_all, _ = spread(grad_mamba_full.astype(low), groups)
    up_own, down_own = owned_sum(grad_up_w), owned_sum(grad_down_w)

    grad_attn_full, gain_one = rms_back(attn_raw, scale_attn, gain_cols[1], half_grad)
    grad_attn_low = grad_attn_full.astype(low)
    grad_context = (
        product_nt(grad_attn_low, weight_attn).astype(low).reshape(buffer_rows, KV, GROUP, HEAD)
    )
    probs_again = jnp.exp(masked_scores() - log_total)
    grad_probs = jnp.einsum(
        "qkgd,skd->kgqs", grad_context, value_rows, preferred_element_type=jnp.float32
    )
    grad_values = jnp.einsum(
        "kgqs,qkgd->skd",
        probs_again.astype(low),
        grad_context,
        preferred_element_type=jnp.float32,
    )
    grad_scores = (
        probs_again * (grad_probs - jnp.sum(probs_again * grad_probs, axis=-1, keepdims=True))
    ).astype(low)
    grad_query = (
        jnp.einsum("kgqs,skd->qkgd", grad_scores, key_rows, preferred_element_type=jnp.float32)
        * factor
    )
    grad_keys = (
        jnp.einsum("kgqs,qkgd->skd", grad_scores, query, preferred_element_type=jnp.float32)
        * factor
    )
    grad_heads = jnp.concatenate(
        [
            grad_query.reshape(buffer_rows, model_width),
            grad_keys.reshape(buffer_rows, kv_width),
            grad_values.reshape(buffer_rows, kv_width),
        ],
        axis=1,
    ).astype(low)
    grad_heads_part = jnp.concatenate(exchange(apart(grad_heads, here, groups)), axis=0)

    grad_mamba_all = after(grad_mamba_all, grad_heads)
    grad_gated = product_nt(grad_mamba_all, weight_mix)
    grad_scanned = grad_gated * silu_z
    grad_gate_low = (grad_gated * scanned * silu_slope(gate_z)).astype(low)
    grad_mix_w = product_tn(gated_low, grad_mamba_all).astype(low)
    grad_gate_w = product_tn(normed_all, grad_gate_low).astype(low)
    mix_own, gate_own = owned_sum(grad_mix_w), owned_sum(grad_gate_w)
    heads_pack = jnp.concatenate(
        [
            product_tn(normed_all, grad_heads_part).astype(low),
            product_tn(context, grad_attn_low).astype(low),
        ],
        axis=1,
    )
    heads_own = owned_sum(heads_pack)
    raw_pieces = row_pieces(product(after(act_low, grad_gate_w), weight_down).astype(low), groups)
    grad_scanned, raw_pieces = after(
        (grad_scanned, raw_pieces), grad_mix_w, grad_gate_w, heads_pack
    )
    raw_hops = first_hop(raw_pieces)
    grad_skip = jnp.sum(grad_scanned * conv_out, axis=0)
    grad_step, grad_conv_scan, grad_inject, grad_readout, grad_rates = scan_backward(
        block_keep,
        step_size,
        conv_out,
        inject_wide,
        readout_wide,
        rates,
        grad_scanned,
        block_begins,
    )
    grad_step = after(grad_step, up_own, raw_hops)
    grad_pre = grad_step * sigmoid(dt_pre)
    grad_step_bias = jnp.sum(grad_pre, axis=0)
    grad_pre_low = grad_pre.astype(low)
    grad_rank = product_tt(step_proj, grad_pre_low)
    grad_double = everywhere(
        jnp.concatenate([grad_rank, grad_inject, grad_readout], axis=0), groups
    ).astype(low)

    raw_hops = after(raw_hops, grad_double)
    ffn_raw = second_hop(raw_pieces, raw_hops)
    output = (live_rows[:, None] * (hidden + ffn_raw)).astype(low)
    grad_conv_out = (
        product_tt(grad_double, input_proj) + grad_conv_scan + skip_weight * grad_scanned
    )
    grad_conv_out = after(grad_conv_out, down_own, mix_own)
    grad_conv = grad_conv_out * silu_slope(conv_pre)
    grad_xin = unshift_rows(grad_conv * tap_masks[0] * table[:, 0], 0)
    for lag in range(1, CONV):
        grad_xin = grad_xin + unshift_rows(grad_conv * tap_masks[lag] * table[:, lag], lag)
    grad_xin_low = grad_xin.astype(low)
    grad_table = jnp.concatenate(
        [
            jnp.stack(
                [jnp.sum(grad_conv * taps[lag], axis=0) for lag in range(CONV)]
                + [jnp.sum(grad_conv, axis=0), grad_step_bias, grad_skip]
            ),
            grad_rates * rates,
            product(grad_double, conv_low),
            product(rank_part, grad_pre_low),
            jnp.zeros((2 * LANES - table_width, inner), jnp.float32),
        ],
        axis=0,
    ).astype(low)
    grad_table = jnp.pad(
        grad_table.T.reshape(ranks, wide_inner, 2 * LANES),
        ((0, 0), (0, part_model - wide_inner), (0, 0)),
    ).reshape(model_width, 2 * LANES)
    xin_pack = jnp.concatenate(
        [product_tn(normed_all, grad_xin_low).astype(low), grad_table], axis=1
    )
    xin_pack = after(xin_pack, gate_own)
    last_own = owned_sum(xin_pack)
    normed_part = (
        product_nt(grad_heads_part, weight_qkv)
        + product_nt(grad_gate_low, weight_in[:, inner:])
        + product_nt(after(grad_xin_low, xin_pack), weight_in[:, :inner])
    ).astype(low)
    grad_normed = collect(row_pieces(normed_part, groups))
    back_inputs, gain_zero = rms_back(inputs, scale_in, gain_cols[0], grad_normed)
    grad_tokens = grad_hidden + back_inputs
    grad_gains = everyone(jnp.stack([gain_zero, gain_one, gain_two, gain_three], axis=0), groups, ranks)
    grad_gains_done = lax.dynamic_slice_in_dim(
        grad_gains, lax.axis_index("shard") * part_model, part_model, axis=1
    ).T

    last_own = lax.optimization_barrier(last_own)
    heads_own = lax.optimization_barrier(heads_own)
    grad_in_done = return_columns(
        jnp.concatenate([last_own[:, :inner], gate_own], axis=1),
        here,
        groups,
        part_inner,
        wide_inner,
    )
    table_pieces = spread_direct(last_own[:part_inner, inner : inner + 2 * LANES], groups)
    if groups == 4:
        grad_table_done = join_rows(table_pieces, here)[:, :table_width]
    else:
        grad_table_done = jnp.concatenate(table_pieces, axis=0)[:, :table_width]
    grad_qkv_done = heads_own[:, :qkv_width]
    grad_attn_done = sum(
        piece.astype(jnp.float32)
        for piece in exchange(apart(heads_own[:, qkv_width:], here, groups))
    )
    grad_mix_done = return_rows(after(mix_own, normed_part), here, groups, part_inner)
    ffn_done = (
        return_columns(after(up_own, normed_part), here, groups, part_hidden, wide_hidden),
        return_rows(after(down_own, normed_part), here, groups, part_hidden),
    )

    owned = (norm_gains, qkv_weight, attn_weight, mixer_in, mixer_table, mixer_out, ffn_in, ffn_out)
    grads_owned = (
        grad_gains_done,
        grad_qkv_done,
        grad_attn_done,
        grad_in_done,
        grad_table_done,
        grad_mix_done,
        ffn_done[0],
        ffn_done[1],
    )
    firsts = (
        first_gains,
        first_qkv,
        first_attn,
        first_mixin,
        first_table,
        first_mixout,
        first_ffnin,
        first_ffnout,
    )
    seconds = (
        second_gains,
        second_qkv,
        second_attn,
        second_mixin,
        second_table,
        second_mixout,
        second_ffnin,
        second_ffnout,
    )
    step_float = step_count[0].astype(jnp.float32)
    updates = [
        adam_rows(owned[slot], grads_owned[slot], firsts[slot], seconds[slot], step_float)
        for slot in range(8)
    ]
    return (output, grad_tokens) + tuple(entry[kind] for kind in range(4) for entry in updates)


def solution(mesh):
    in_specs = (
        P(("dp", "shard"), None),
        P(("dp", "shard"), None),
        P(("dp", "shard"), None),
        P(),
        P("shard", None),
        P("shard", "dp"),
        P("shard", "dp"),
        P("shard", "dp"),
        P("shard", None),
        P("shard", "dp"),
        P("shard", "dp"),
        P("shard", "dp"),
        P("shard", None),
        P("shard", "dp"),
        P("shard", "dp"),
        P("shard", "dp"),
        P("shard", None),
        P("shard", "dp"),
        P("shard", "dp"),
        P("shard", "dp"),
        P("shard", None),
        P("shard", "dp"),
        P("shard", "dp"),
        P("shard", "dp"),
        P("shard", None),
        P("shard", "dp"),
        P("shard", "dp"),
        P("shard", "dp"),
    )
    out_specs = (
        P(("dp", "shard"), None),
        P(("dp", "shard"), None),
        P("shard", None),
        P("shard", "dp"),
        P("shard", "dp"),
        P("shard", "dp"),
        P("shard", None),
        P("shard", "dp"),
        P("shard", "dp"),
        P("shard", "dp"),
        P("shard", None),
        P("shard", "dp"),
        P("shard", "dp"),
        P("shard", "dp"),
        P("shard", None),
        P("shard", "dp"),
        P("shard", "dp"),
        P("shard", "dp"),
        P("shard", None),
        P("shard", "dp"),
        P("shard", "dp"),
        P("shard", "dp"),
        P("shard", None),
        P("shard", "dp"),
        P("shard", "dp"),
        P("shard", "dp"),
        P("shard", None),
        P("shard", "dp"),
        P("shard", "dp"),
        P("shard", "dp"),
        P("shard", None),
        P("shard", "dp"),
        P("shard", "dp"),
        P("shard", "dp"),
    )
    return jax.shard_map(functools.partial(shards, mesh.shape["dp"], mesh.shape["shard"]), mesh=mesh, in_specs=in_specs, out_specs=out_specs, check_vma=False)
```

time: 1190 us -> 805 us (0.68)
  waiting for transfers between devices: 393 us -> 172 us
  local copies, waits for them, and re-layouts: 212 us -> 86.8 us
  blocking collectives: 62.1 us -> 0 us
  Pallas kernels: 87 us -> 135 us
  other arithmetic: 108 us -> 84.7 us
  starting transfers between devices: 97.6 us -> 111 us
    all_to_all x21 -> x0, waiting for transfers between devices: 221 us -> none  [trade(): return lax.all_to_all(pieces, 'dp', 0, 0)]
    ppermute x0 -> x97, waiting for transfers between devices: none -> 165 us  [the longest x91 157 us: swap(): return lax.ppermute(values, 'dp', [(i, i ^ bit) for i in range(4)])]
    reduce_scatter x5 -> x3, waiting for transfers between devices: 141 us -> 0.01 us  [owned_sum(): return lax.psum_scatter(partial, 'shard', scatter_dimension=0, tiled=True)]
    ppermute x0 -> x97, starting transfers between devices: none -> 111 us  [the longest x91 105 us: swap(): return lax.ppermute(values, 'dp', [(i, i ^ bit) for i in range(4)])]
    all_to_all x21 -> x0, starting transfers between devices: 96.1 us -> none  [trade(): return lax.all_to_all(pieces, 'dp', 0, 0)]
    reshape x41 -> x3, local copies, waits for them, and re-layouts: 58.1 us -> 1.21 us  [the longest x1 0.67 us: shards(): grad_query.reshape(buffer_rows, model_width)]
    all_to_all x4 -> x0, blocking collectives: 54.7 us -> none  [trade(): return lax.all_to_all(pieces, 'dp', 0, 0)]
    pallas_call x2 -> x31, Pallas kernels: 87 us -> 135 us  [the longest x1 65.1 us: scan_backward(): pl.pallas_call(back_kernel, grid_spec=pltpu.PrefetchScalarGridSpec(num_sc...]
  transfers between devices with their start and end apart: 34 -> 108, of which waited for: 18 -> 49; matrix products, arithmetic and copies ran while one was open for 37% -> 36% of each run, Pallas kernels for 7% -> 16%
where the time goes in v2:
time: 805 us; the launch traced here: 795 us
  matrix products  187 us (23%)
  waiting for transfers between devices  172 us (21%)
  Pallas kernels  135 us (17%)
  starting transfers between devices  111 us (14%)
  local copies, waits for them, and re-layouts  86.8 us (11%)
  other arithmetic  84.7 us (11%)
  between operations  17.5 us (2%)
    ppermute x91, waiting for transfers between devices, swap(): return lax.ppermute(values, 'dp', [(i, i ^ bit) for i in range(4)])  157 us
    ppermute x91, starting transfers between devices, swap(): return lax.ppermute(values, 'dp', [(i, i ^ bit) for i in range(4)])  105 us
    pallas_call x1, Pallas kernels, scan_backward(): pl.pallas_call(back_kernel, grid_spec=pltpu.PrefetchScalarGridSpec(num_sc...  65.1 us
    dot_general x7, matrix products, product_nt(): lax.dot_general(left, right, (((1,), (1,)), ((), ())), preferred_element_...  59.4 us
    dot_general x8, matrix products, product(): return jnp.dot(left, right, preferred_element_type=jnp.float32)  59.2 us
    dot_general x7, matrix products, product_tn(): lax.dot_general(left, right, (((0,), (0,)), ((), ())), preferred_element_...  46 us
    unnamed x308, local copies, waits for them, and re-layouts  45.3 us
    pallas_call x1, Pallas kernels, scan_forward(): pl.pallas_call(scan_kernel, grid_spec=pltpu.PrefetchScalarGridSpec(num_sc...  34.4 us
  transfers between devices with their start and end apart: 108, of which 49 were waited for; matrix products, arithmetic and copies ran while one was open for 36% of the time, Pallas kernels for 16%

profile of v2, /device:TPU:0, one launch (start us, length us, event | category | flops | bytes accessed | tf_op | source)
XLA Modules:
  0.0 795.3 jit_solution(931943441773982518)
XLA Ops:
  41.5 15.6 %collective-permute-done.6 = bf16[256,1600]{0,1:T(8,128)(2,1)S(1)} collective-permute-done((bf16[256,1600]{0,1:T(8,128)(2,1)S(1)}, bf16[256,1600]{0,1:T(8,128)(2,1)S(1)}, u32[]{:S(2)}, u32[]{:S(2)}) %collective-permute-start.6) | collective-permute-done | bytes 819232 | tf_op jit(solution)/shard_map/ppermute | solution.py:558
  73.3 9.6 %collective-permute-done.12.refs_3_ = bf16[100,400]{1,0:T(8,128)(2,1)S(1)} collective-permute-done((bf16[100,400]{1,0:T(8,128)(2,1)S(1)}, bf16[100,400]{1,0:T(8,128)(2,1)S(1)}, u32[]{:S(2)}, u32[]{:S(2)}) %collective-permute-start.12) | collective-permute-done | bytes 80032 | tf_op jit(solution)/shard_map/ppermute | solution.py:558
  95.5 12.2 %fusion.4 = f32[1024,1792]{1,0:T(8,128)} fusion(bf16[1024,1600]{0,1:T(8,128)(2,1)} %constant_dynamic-update-slice_fusion, bf16[1600,2048]{1,0:T(8,128)(2,1)} %all-gather.6.cloned.1.call-done), kind=kOutput, calls=%fused_computation.19 | convolution fusion | flops 5872025600 | bytes 16351232 | tf_op jit(solution)/shard_map/dot_general | solution.py:32
  126.1 9.3 %fusion.89 = (f32[1024,896]{1,0:T(8,128)}, bf16[1024,896]{1,0:T(8,128)(2,1)S(1)}, f32[1024,896]{1,0:T(8,128)}) fusion(f32[1024]{0:T(1024)S(1)} %bitcast.197, f32[1021,896]{1,0:T(8,128)} %slice.568, f32[896]{0:T(1024)S(1)} %get-tuple-element.291, f32[1024]{0:T(1024)S(1)} %bitcast.194, f32[1022,896]{1,0:T(8,128)} %slice.566, f32[896]{0:T(1024)S(1)} %get-tuple-element.292, ...), kind=kLoop, calls=%fused_computation.300 | loop fusion | flops 15597568 | bytes 23867904 | tf_op jit(solution)/shard_map/convert_element_type | solution.py:837
  165.0 34.4 %state_scan.1 = (f32[1024,896]{1,0:T(8,128)S(1)}, f32[8,16,896]{2,1,0:T(8,128)S(1)}, f32[1024,16,128]{2,1,0:T(8,128)S(1)}, f32[1024,16,128]{2,1,0:T(8,128)S(1)}) custom-call(f32[8]{0:T(128)S(1)} %sub.151.keep_ref, f32[1024,896]{1,0:T(8,128)S(1)} %get-tuple-element.401.step_ref, f32[1024,896]{1,0:T(8,128)S(1)} %copy-done, ...), custom_call_target="tpu_custom_call" | custom-call | flops 440401920 | bytes 128450560 | tf_op jit(solution)/shard_map/state_scan/pallas_call | solution.py:168
  234.7 6.1 convolution_convert_fusion.5
  246.9 8.0 %multiply_reduce_fusion.13 = (f32[256]{0:T(256)S(1)}, f32[256,1600]{0,1:T(8,128)S(1)}) fusion(bf16[256,1600]{0,1:T(8,128)(2,1)S(1)} %bitcast.171, bf16[1600,2160]{1,0:T(8,128)(2,1)} %all-gather.8.cloned.1.call-done), kind=kOutput, calls=%fused_computation.108 | convolution fusion | flops 1311538944 | bytes 7783424 | tf_op jit(solution)/shard_map/dot_general | solution.py:32
  269.9 14.8 %collective-permute-done.38 = bf16[256,1600]{0,1:T(8,128)(2,1)S(1)} collective-permute-done((bf16[256,1600]{0,1:T(8,128)(2,1)S(1)}, bf16[256,1600]{0,1:T(8,128)(2,1)S(1)}, u32[]{:S(2)}, u32[]{:S(2)}) %collective-permute-start.38) | collective-permute-done | bytes 819232 | tf_op jit(solution)/shard_map/ppermute | solution.py:558
  287.3 6.6 collective-permute-done.40
  303.7 17.5 %fusion.105 = f32[1024,2816]{1,0:T(8,128)} fusion(bf16[1024,1600]{0,1:T(8,128)(2,1)} %copy-done.100, bf16[1600,2816]{1,0:T(8,128)(2,1)} %all-gather.12.cloned.1.call-done), kind=kOutput, calls=%fused_computation.316 | convolution fusion | flops 9227468800 | bytes 23822336 | tf_op jit(solution)/shard_map/dot_general | solution.py:32
  321.1 8.9 %collective-permute-done.43 = bf16[256,1600]{0,1:T(8,128)(2,1)} collective-permute-done((bf16[256,1600]{0,1:T(8,128)(2,1)}, bf16[256,1600]{0,1:T(8,128)(2,1)}, u32[]{:S(2)}, u32[]{:S(2)}) %collective-permute-start.43) | collective-permute-done | bytes 819232 | tf_op jit(solution)/shard_map/ppermute | solution.py:558
  344.7 14.1 %multiply_convert_fusion.2 = (bf16[1024,1408]{1,0:T(8,128)(2,1)S(1)}, bf16[1024,1408]{1,0:T(8,128)(2,1)S(1)}, bf16[1024,1408]{1,0:T(8,128)(2,1)}) fusion(f32[1024,2816]{1,0:T(8,128)} %fusion.105, bf16[1024,1600]{0,1:T(8,128)(2,1)} %constant_dynamic-update-slice_fusion.10, bf16[1408,1600]{1,0:T(8,128)(2,1)} %all-gather.14.cloned.1.call-done), kind=kOutput, calls=%fused_computation.16 | convolution fusion | flops 4635361280 | bytes 27967488 | tf_op jit(solution)/shard_map/dot_general | solution.py:42
  358.8 13.3 %convolution_convert_fusion.4 = bf16[1024,1600]{0,1:T(8,128)(2,1)} fusion(bf16[1600,2816]{1,0:T(8,128)(2,1)} %all-gather.12.cloned.1.call-done, bf16[1024,1408]{1,0:T(8,128)(2,1)S(1)} %get-tuple-element.320, bf16[1024,1408]{1,0:T(8,128)(2,1)S(1)} %get-tuple-element.319), kind=kOutput, calls=%fused_computation.27 | convolution fusion | flops 9240641536 | bytes 18055168 | tf_op jit(solution)/shard_map/dot_general | solution.py:42
  372.1 11.9 %convolution_convert_fusion = bf16[1600,2816]{1,0:T(8,128)(2,1)} fusion(bf16[1024,1600]{0,1:T(8,128)(2,1)S(1)} %copy-done.101, bf16[1024,1408]{1,0:T(8,128)(2,1)S(1)} %get-tuple-element.320, bf16[1024,1408]{1,0:T(8,128)(2,1)S(1)} %get-tuple-element.319), kind=kOutput, calls=%fused_computation | convolution fusion | flops 9243508736 | bytes 18055168 | tf_op jit(solution)/shard_map/dot_general | solution.py:36
  391.0 9.6 %convolution_convert_fusion.1 = bf16[1408,1600]{1,0:T(8,128)(2,1)} fusion(bf16[1024,1408]{1,0:T(8,128)(2,1)S(1)} %copy-done.135, bf16[1024,1600]{0,1:T(8,128)(2,1)} %constant_dynamic-update-slice_fusion.10), kind=kOutput, calls=%fused_computation.1 | convolution fusion | flops 4615987200 | bytes 10665984 | tf_op jit(solution)/shard_map/dot_general | solution.py:36
  409.8 7.7 collective-permute-done.47
  458.6 7.1 convolution_convert_fusion.7
  466.6 12.5 %multiply_convert_fusion.3 = (bf16[1024,896]{1,0:T(8,128)(2,1)S(1)}, f32[1024,896]{1,0:T(8,128)}) fusion(f32[1024,1792]{1,0:T(8,128)} %fusion.4, f32[1024,896]{1,0:T(8,128)} %copy-done.8, bf16[1024,896]{1,0:T(8,128)(2,1)} %copy-done.51, f32[896]{0:T(1024)S(1)} %copy-done.116, bf16[1024,1600]{0,1:T(8,128)(2,1)} %constant_dynamic-update-slice_fusion.14, ...), kind=kOutput, calls=%fused_computation.52 | convolution fusion | flops 2949775360 | bytes 20827648 | tf_op jit(solution)/shard_map/dot_general | solution.py:42
  510.7 9.2 %pad_maximum_fusion = bf16[1600,2160]{1,0:T(8,128)(2,1)} fusion(bf16[1600,1600]{1,0:T(8,128)(2,1)} %convolution_convert_fusion.2, bf16[1600,560]{1,0:T(8,128)(2,1)} %copy.136), kind=kLoop, calls=%fused_computation.3 | loop fusion | flops 13824000 | bytes 13824000 | tf_op jit(solution)/shard_map/concatenate | solution.py:965
  521.0 8.6 %convolution_convert_fusion.3 = bf16[1024,1600]{0,1:T(8,128)(2,1)S(1)} fusion(bf16[1024,1408]{1,0:T(8,128)(2,1)} %get-tuple-element.193, bf16[1408,1600]{1,0:T(8,128)(2,1)} %all-gather.14.cloned.1.call-done), kind=kOutput, calls=%fused_computation.26 | convolution fusion | flops 4615372800 | bytes 10665984 | tf_op jit(solution)/shard_map/dot_general | solution.py:32
  540.8 65.1 %state_back.1 = (f32[1024,896]{1,0:T(8,128)S(1)}, f32[1024,896]{1,0:T(8,128)S(1)}, f32[16,1024]{1,0:T(8,128)S(1)}, f32[16,1024]{1,0:T(8,128)S(1)}, f32[16,896]{1,0:T(8,128)S(1)}) custom-call(f32[8]{0:T(128)S(1)} %copy-done.46, f32[1024,896]{1,0:T(8,128)S(1)} %copy-done.2, f32[1024,896]{1,0:T(8,128)} %get-tuple-element.316.conv_ref, ...), custom_call_target="tpu_custom_call" | custom-call | flops 880803840 | bytes 238551040 | tf_op jit(solution)/shard_map/state_back/pallas_call | solution.py:319
  636.4 11.8 %fusion.86 = (bf16[896]{0:T(1024)(128)(2,1)S(1)}, bf16[896]{0:T(1024)(128)(2,1)S(1)}, bf16[896]{0:T(1024)(128)(2,1)S(1)}, bf16[896]{0:T(1024)(128)(2,1)S(1)}, bf...) fusion(f32[1024]{0:T(1024)S(1)} %bitcast.199, f32[1021,896]{1,0:T(8,128)} %slice.568, f32[1024]{0:T(1024)S(1)} %bitcast.196, ...), kind=kLoop, calls=%fused_computation.297 | loop fusion | flops 19263104 | bytes 25693952 | tf_op jit(solution)/shard_map/reduce_sum | solution.py:1014
  667.2 6.6 fusion.16
  683.5 8.2 %collective-permute-done.69 = bf16[128,1600]{0,1:T(8,128)(2,1)S(1)} collective-permute-done((bf16[128,1600]{0,1:T(8,128)(2,1)S(1)}, bf16[128,1600]{0,1:T(8,128)(2,1)S(1)}, u32[]{:S(2)}, u32[]{:S(2)}) %collective-permute-start.69) | collective-permute-done | bytes 409632 | tf_op jit(solution)/shard_map/ppermute | solution.py:558
  (761 shorter events, 449.1 us)
Async XLA Ops:
  7.2 87.0 %all-gather.6.cloned.1.call-start = ((), (), s32[]{:S(2)}) async-start(), calls=%async_computation.6 | async-start | bytes 7372800 | tf_op jit(solution)/shard_map/all_gather | solution.py:731
  24.3 185.3 %all-gather.8.cloned.1.call-start = ((), (), s32[]{:S(2)}) async-start(), calls=%async_computation.7 | async-start | bytes 7833600 | tf_op jit(solution)/shard_map/all_gather | solution.py:731
  38.0 25.1 %collective-permute-start.19 = (bf16[200,400]{1,0:T(8,128)(2,1)S(1)}, bf16[200,400]{1,0:T(8,128)(2,1)S(1)}, u32[]{:S(2)}, u32[]{:S(2)}) collective-permute-start(bf16[200,400]{1,0:T(8,128)(2,1)S(1)} %copy-done.29), channel_id=1, source_target_pairs={{0,8},{8,0},{16,24},{24,16},{1,9},{9,1},{17,25},{25,17},{2,10},{10... | collective-permute-start | bytes 480008 | tf_op jit(solution)/shard_map/ppermute | solution.py:558
  39.5 23.8 %collective-permute-start.20 = (bf16[200,400]{1,0:T(8,128)(2,1)S(1)}, bf16[200,400]{1,0:T(8,128)(2,1)S(1)}, u32[]{:S(2)}, u32[]{:S(2)}) collective-permute-start(bf16[200,400]{1,0:T(8,128)(2,1)S(1)} %copy-done.29), channel_id=1, source_target_pairs={{0,16},{8,24},{16,0},{24,8},{1,17},{9,25},{17,1},{25,9},{2,18},{10... | collective-permute-start | bytes 480008 | tf_op jit(solution)/shard_map/ppermute | solution.py:558
  40.0 25.4 %collective-permute-start.21 = (bf16[200,400]{1,0:T(8,128)(2,1)S(1)}, bf16[200,400]{1,0:T(8,128)(2,1)S(1)}, u32[]{:S(2)}, u32[]{:S(2)}) collective-permute-start(bf16[200,400]{1,0:T(8,128)(2,1)S(1)} %copy-done.29), channel_id=1, source_target_pairs={{0,24},{8,16},{16,8},{24,0},{1,25},{9,17},{17,9},{25,1},{2,26},{10... | collective-permute-start | bytes 480008 | tf_op jit(solution)/shard_map/ppermute | solution.py:558
  95.5 139.2 %all-gather.10.cloned.1.call-start = ((), (), s32[]{:S(2)}) async-start(), calls=%async_computation.8 | async-start | bytes 3354624 | tf_op jit(solution)/shard_map/all_gather | solution.py:731
  107.7 195.9 %all-gather.12.cloned.1.call-start = ((), (), s32[]{:S(2)}) async-start(), calls=%async_computation.9 | async-start | bytes 10137600 | tf_op jit(solution)/shard_map/all_gather | solution.py:731
  108.3 236.4 %all-gather.14.cloned.1.call-start = ((), (), s32[]{:S(2)}) async-start(), calls=%async_computation.10 | async-start | bytes 5271552 | tf_op jit(solution)/shard_map/all_gather | solution.py:731
  155.2 64.1 %collective-permute-start.29 = (bf16[172,400]{1,0:T(8,128)(2,1)S(1)}, bf16[172,400]{1,0:T(8,128)(2,1)S(1)}, u32[]{:S(2)}, u32[]{:S(2)}) collective-permute-start(bf16[172,400]{1,0:T(8,128)(2,1)S(1)} %get-tuple-element.176), channel_id=1, source_target_pairs={{0,8},{8,0},{16,24},{24,16},{1,9},{9,1},{17,25},{25,17},{2,10},{10... | collective-permute-start | bytes 412808 | tf_op jit(solution)/shard_map/ppermute | solution.py:558
  157.7 66.8 %collective-permute-start.30 = (bf16[172,400]{1,0:T(8,128)(2,1)S(1)}, bf16[172,400]{1,0:T(8,128)(2,1)S(1)}, u32[]{:S(2)}, u32[]{:S(2)}) collective-permute-start(bf16[172,400]{1,0:T(8,128)(2,1)S(1)} %get-tuple-element.177), channel_id=1, source_target_pairs={{0,16},{8,24},{16,0},{24,8},{1,17},{9,25},{17,1},{25,9},{2,18},{10... | collective-permute-start | bytes 412808 | tf_op jit(solution)/shard_map/ppermute | solution.py:558
  158.7 65.9 %collective-permute-start.31 = (bf16[172,400]{1,0:T(8,128)(2,1)S(1)}, bf16[172,400]{1,0:T(8,128)(2,1)S(1)}, u32[]{:S(2)}, u32[]{:S(2)}) collective-permute-start(bf16[172,400]{1,0:T(8,128)(2,1)S(1)} %get-tuple-element.178), channel_id=1, source_target_pairs={{0,24},{8,16},{16,8},{24,0},{1,25},{9,17},{17,9},{25,1},{2,26},{10... | collective-permute-start | bytes 412808 | tf_op jit(solution)/shard_map/ppermute | solution.py:558
  225.6 385.3 %reduce-scatter.13.cloned.1.call-start = ((), (), s32[]{:S(2)}) async-start(), calls=%async_computation.11 | async-start | bytes 10137600 | tf_op jit(solution)/shard_map/reduce_scatter | solution.py:735
  300.2 29.9 %collective-permute-start.43 = (bf16[256,1600]{0,1:T(8,128)(2,1)}, bf16[256,1600]{0,1:T(8,128)(2,1)}, u32[]{:S(2)}, u32[]{:S(2)}) collective-permute-start(bf16[256,1600]{0,1:T(8,128)(2,1)} %fusion.37), channel_id=1, source_target_pairs={{0,16},{8,24},{16,0},{24,8},{1,17},{9,25},{17,1},{25,9},{2,18},{10... | collective-permute-start | bytes 2457608 | tf_op jit(solution)/shard_map/ppermute | solution.py:558
  301.7 28.4 %collective-permute-start.44 = (bf16[256,1600]{0,1:T(8,128)(2,1)}, bf16[256,1600]{0,1:T(8,128)(2,1)}, u32[]{:S(2)}, u32[]{:S(2)}) collective-permute-start(bf16[256,1600]{0,1:T(8,128)(2,1)} %fusion.37), channel_id=1, source_target_pairs={{0,24},{8,16},{16,8},{24,0},{1,25},{9,17},{17,9},{25,1},{2,26},{10... | collective-permute-start | bytes 2457608 | tf_op jit(solution)/shard_map/ppermute | solution.py:558
  384.1 252.3 %reduce-scatter.17.cloned.1.call-start = ((), (), s32[]{:S(2)}) async-start(), calls=%async_computation.13 | async-start | bytes 3354624 | tf_op jit(solution)/shard_map/reduce_scatter | solution.py:735
  465.8 170.7 %reduce-scatter.15.cloned.1.call-start = ((), (), s32[]{:S(2)}) async-start(), calls=%async_computation.12 | async-start | bytes 5271552 | tf_op jit(solution)/shard_map/reduce_scatter | solution.py:735
  466.5 197.9 %reduce-scatter.19.cloned.1.call-start = ((), (), s32[]{:S(2)}) async-start(), calls=%async_computation.14 | async-start | bytes 3225600
  485.2 227.3 %reduce-scatter.21.cloned.1.call-start = ((), (), s32[]{:S(2)}) async-start(), calls=%async_computation.15 | async-start | bytes 7833600
  519.9 246.4 %reduce-scatter.23.cloned.1.call-start = ((), (), s32[]{:S(2)}) async-start(), calls=%async_computation.16 | async-start | bytes 4147200
  530.8 79.1 %collective-permute-start.58 = (bf16[128,1600]{0,1:T(8,128)(2,1)S(1)}, bf16[128,1600]{0,1:T(8,128)(2,1)S(1)}, u32[]{:S(2)}, u32[]{:S(2)}) collective-permute-start(bf16[128,1600]{0,1:T(8,128)(2,1)S(1)} %get-tuple-element.361), channel_id=1, source_target_pairs={{0,8},{8,0},{16,24},{24,16},{1,9},{9,1},{17,25},{25,17},{2,10},{10... | collective-permute-start | bytes 1228808 | tf_op jit(solution)/shard_map/ppermute | solution.py:558
  531.5 78.5 %collective-permute-start.59 = (bf16[128,1600]{0,1:T(8,128)(2,1)S(1)}, bf16[128,1600]{0,1:T(8,128)(2,1)S(1)}, u32[]{:S(2)}, u32[]{:S(2)}) collective-permute-start(bf16[128,1600]{0,1:T(8,128)(2,1)S(1)} %get-tuple-element.360), channel_id=1, source_target_pairs={{0,16},{8,24},{16,0},{24,8},{1,17},{9,25},{17,1},{25,9},{2,18},{10... | collective-permute-start | bytes 1228808 | tf_op jit(solution)/shard_map/ppermute | solution.py:558
  532.6 77.5 %collective-permute-start.60 = (bf16[128,1600]{0,1:T(8,128)(2,1)S(1)}, bf16[128,1600]{0,1:T(8,128)(2,1)S(1)}, u32[]{:S(2)}, u32[]{:S(2)}) collective-permute-start(bf16[128,1600]{0,1:T(8,128)(2,1)S(1)} %slice.517), channel_id=1, source_target_pairs={{0,8},{8,0},{16,24},{24,16},{1,9},{9,1},{17,25},{25,17},{2,10},{10... | collective-permute-start | bytes 1228808 | tf_op jit(solution)/shard_map/ppermute | solution.py:558
  534.1 76.7 %collective-permute-start.61 = (bf16[128,1600]{0,1:T(8,128)(2,1)S(1)}, bf16[128,1600]{0,1:T(8,128)(2,1)}, u32[]{:S(2)}, u32[]{:S(2)}) collective-permute-start(bf16[128,1600]{0,1:T(8,128)(2,1)S(1)} %slice.518), channel_id=1, source_target_pairs={{0,16},{8,24},{16,0},{24,8},{1,17},{9,25},{17,1},{25,9},{2,18},{10... | collective-permute-start | bytes 1228808 | tf_op jit(solution)/shard_map/ppermute | solution.py:558
  665.6 42.9 %collective-permute-start.67 = (bf16[128,1600]{0,1:T(8,128)(2,1)S(1)}, bf16[128,1600]{0,1:T(8,128)(2,1)S(1)}, u32[]{:S(2)}, u32[]{:S(2)}) collective-permute-start(bf16[128,1600]{0,1:T(8,128)(2,1)S(1)} %add_convert_fusion.4), channel_id=1, source_target_pairs={{0,8},{8,0},{16,24},{24,16},{1,9},{9,1},{17,25},{25,17},{2,10},{10... | collective-permute-start | bytes 1228808 | tf_op jit(solution)/shard_map/ppermute | solution.py:558
  (229 other events, 2501.0 us)
Sparse Core Ops, SparseCore 0:
  24.5 67.2 all-gather.5
  95.6 70.9 all-gather.7
  168.8 35.5 all-gather.9
  206.5 86.1 all-gather.11
  294.7 49.9 all-gather.13
  384.2 94.5 reduce-scatter.12
  481.2 37.4 reduce-scatter.16
  521.1 54.3 reduce-scatter.14
  577.8 39.8 reduce-scatter.18
  619.8 76.8 reduce-scatter.20
  699.1 43.4 reduce-scatter.22

commit v3 on v2

--- a/solution.py
+++ b/solution.py
@@ -115,7 +115,10 @@
     inject_ref,
     read_ref,
     rates_ref,
+    gate_ref,
+    channel_ref,
     out_ref,
+    gated_ref,
     start_ref,
     inject_wide_ref,
     read_wide_ref,
@@ -157,9 +160,12 @@
     state = lax.fori_loop(0, BLOCK // 8, group, tuple(state_ref[:, tile] for tile in tiles))
     for k, tile in enumerate(tiles):
         state_ref[:, tile] = state[k]
-
-
-def scan_forward(keep, step, conv, inject, read, rates):
+        scanned = out_ref[:, tile] + channel_ref[CONV + 2 : CONV + 3, tile] * conv_ref[:, tile]
+        out_ref[:, tile] = scanned
+        gated_ref[:, tile] = (scanned * silu_act(gate_ref[:, tile])).astype(jnp.bfloat16)
+
+
+def scan_forward(keep, step, conv, inject, read, rates, mixed, channels):
     rows, width = step.shape
     blocks = rows // BLOCK
     row_spec = pl.BlockSpec((BLOCK, width), lambda i, *_: (i, 0))
@@ -176,8 +182,11 @@
                 state_spec,
                 state_spec,
                 pl.BlockSpec((STATE, width), lambda i, *_: (0, 0)),
+                pl.BlockSpec((BLOCK, width), lambda i, *_: (i, 1)),
+                pl.BlockSpec((8, width), lambda i, *_: (0, 0)),
             ],
             out_specs=[
+                row_spec,
                 row_spec,
                 pl.BlockSpec((1, STATE, width), lambda i, *_: (i, 0, 0)),
                 wide_spec,
@@ -187,6 +196,7 @@
         ),
         out_shape=[
             jax.ShapeDtypeStruct((rows, width), jnp.float32),
+            jax.ShapeDtypeStruct((rows, width), jnp.bfloat16),
             jax.ShapeDtypeStruct((blocks, STATE, width), jnp.float32),
         ]
         + [jax.ShapeDtypeStruct((rows, STATE, LANES), jnp.float32)] * 2,
@@ -197,7 +207,7 @@
         ),
         compiler_params=pltpu.CompilerParams(vmem_limit_bytes=24 * 2**20),
         name="state_scan",
-    )(keep, step, conv, inject, read, rates)
+    )(keep, step, conv, inject, read, rates, mixed, channels)
 
 
 def back_kernel(
@@ -207,17 +217,24 @@
     inject_ref,
     read_ref,
     rates_ref,
+    gated_ref,
+    gate_ref,
+    scanned_ref,
+    pre_ref,
+    start_ref,
     grad_ref,
-    start_ref,
-    gstep_ref,
+    ggate_ref,
+    gpre_ref,
     gconv_ref,
     ginject_ref,
     gread_ref,
     grate_ref,
+    gsums_ref,
     later_ref,
     history_ref,
     decay_ref,
     sums_ref,
+    gstep_ref,
 ):
     tiles = lane_tiles(step_ref.shape[1])
     at = pl.num_programs(0) - 1 - pl.program_id(0)
@@ -226,6 +243,16 @@
     def _():
         later_ref[...] = jnp.zeros_like(later_ref)
         grate_ref[...] = jnp.zeros_like(grate_ref)
+        gsums_ref[...] = jnp.zeros_like(gsums_ref)
+
+    for tile in tiles:
+        gate, incoming = gate_ref[:, tile], gated_ref[:, tile]
+        opened = sigmoid(gate)
+        grad = incoming * (gate * opened)
+        grad_ref[:, tile] = grad
+        slope = opened * (1.0 + gate * (1.0 - opened))
+        ggate_ref[:, tile] = (incoming * scanned_ref[:, tile] * slope).astype(jnp.bfloat16)
+        gsums_ref[0:1, tile] += jnp.sum(grad * conv_ref[:, tile], axis=0, keepdims=True)
 
     def forward(turn, state):
         base = pl.multiple_of(turn * 8, 8)
@@ -284,6 +311,10 @@
     later = lax.fori_loop(
         0, BLOCK // 8, backward, tuple(later_ref[:, tile] for tile in tiles)
     )
+    for tile in tiles:
+        grad = gstep_ref[:, tile] * sigmoid(pre_ref[:, tile])
+        gpre_ref[:, tile] = grad.astype(jnp.bfloat16)
+        gsums_ref[1:2, tile] += jnp.sum(grad, axis=0, keepdims=True)
     ones = jnp.ones((LANES, LANES), jnp.bfloat16)
     lane = lax.broadcasted_iota(jnp.int32, (STATE, BLOCK), 1)
     ginject_ref[...] = jnp.zeros_like(ginject_ref)
@@ -309,7 +340,7 @@
         later_ref[:, tile] = later[k] * keep_ref[at]
 
 
-def scan_backward(keep, step, conv, inject, read, rates, grad, starts):
+def scan_backward(keep, step, conv, inject, read, rates, grad_gated, mixed, scanned, pre, starts):
     rows, width = step.shape
     blocks = rows // BLOCK
     row_spec = pl.BlockSpec((BLOCK, width), lambda i, *_: (blocks - 1 - i, 0))
@@ -328,27 +359,104 @@
                 wide_spec,
                 all_spec,
                 row_spec,
+                pl.BlockSpec((BLOCK, width), lambda i, *_: (blocks - 1 - i, 1)),
+                row_spec,
+                row_spec,
                 pl.BlockSpec((1, STATE, width), lambda i, *_: (blocks - 1 - i, 0, 0)),
             ],
-            out_specs=[row_spec, row_spec, flat_spec, flat_spec, all_spec],
+            out_specs=[row_spec] * 4
+            + [flat_spec, flat_spec, all_spec, pl.BlockSpec((8, width), lambda i, *_: (0, 0))],
             scratch_shapes=[
                 pltpu.VMEM((STATE, width), jnp.float32),
                 pltpu.VMEM((BLOCK + 1, STATE, width), jnp.float32),
                 pltpu.VMEM((BLOCK, STATE, width), jnp.float32),
                 pltpu.VMEM((2, BLOCK, STATE, LANES), jnp.float32),
+                pltpu.VMEM((BLOCK, width), jnp.float32),
             ],
         ),
-        out_shape=[jax.ShapeDtypeStruct((rows, width), jnp.float32)] * 2
+        out_shape=[
+            jax.ShapeDtypeStruct((rows, width), kind)
+            for kind in (jnp.float32, jnp.bfloat16, jnp.bfloat16, jnp.float32)
+        ]
         + [jax.ShapeDtypeStruct((STATE, rows), jnp.float32)] * 2
-        + [jax.ShapeDtypeStruct((STATE, width), jnp.float32)],
+        + [jax.ShapeDtypeStruct((n, width), jnp.float32) for n in (STATE, 8)],
         cost_estimate=pl.CostEstimate(
             flops=60 * rows * STATE * width,
             bytes_accessed=260 * rows * width,
             transcendentals=rows * STATE * width,
         ),
-        compiler_params=pltpu.CompilerParams(vmem_limit_bytes=40 * 2**20),
+        compiler_params=pltpu.CompilerParams(vmem_limit_bytes=48 * 2**20),
         name="state_back",
-    )(keep, step, conv, inject, read, rates, grad, starts)
+    )(keep, step, conv, inject, read, rates, grad_gated, mixed, scanned, pre, starts)
+
+
+def conv_kernel(mixed_ref, place_ref, channel_ref, pre_ref, out_ref, low_ref):
+    inputs, place = mixed_ref[...], place_ref[...]
+    total = channel_ref[CONV : CONV + 1] + channel_ref[0:1] * inputs
+    for lag in range(1, CONV):
+        tap = jnp.where(place >= lag, pltpu.roll(inputs, lag, 0), 0.0)
+        total = total + channel_ref[lag : lag + 1] * tap
+    pre_ref[...] = total
+    low = silu_act(total).astype(jnp.bfloat16)
+    low_ref[...] = low
+    out_ref[...] = low.astype(jnp.float32)
+
+
+def conv_forward(mixed, place, channels):
+    rows, width = mixed.shape[0], channels.shape[1]
+    spec = pl.BlockSpec((rows, LANES), lambda i: (0, i))
+    return pl.pallas_call(
+        conv_kernel,
+        grid=(width // LANES,),
+        in_specs=[
+            spec,
+            pl.BlockSpec((rows, LANES), lambda i: (0, 0)),
+            pl.BlockSpec((8, LANES), lambda i: (0, i)),
+        ],
+        out_specs=[spec] * 3,
+        out_shape=[
+            jax.ShapeDtypeStruct((rows, width), kind)
+            for kind in (jnp.float32, jnp.float32, jnp.bfloat16)
+        ],
+        compiler_params=pltpu.CompilerParams(vmem_limit_bytes=24 * 2**20),
+        name="conv_forward",
+    )(mixed, place, channels)
+
+
+def conv_back_kernel(
+    part_ref, scan_ref, grad_ref, pre_ref, mixed_ref, place_ref, channel_ref, low_ref, sums_ref
+):
+    pre, inputs, place = pre_ref[...], mixed_ref[...], place_ref[...]
+    rows = pre.shape[0]
+    grad = part_ref[...] + scan_ref[...] + channel_ref[CONV + 2 : CONV + 3] * grad_ref[...]
+    grad = grad * silu_slope(pre)
+    sums_ref[CONV : CONV + 1] = jnp.sum(grad, axis=0, keepdims=True)
+    sums_ref[0:1] = jnp.sum(grad * inputs, axis=0, keepdims=True)
+    total = channel_ref[0:1] * grad
+    for lag in range(1, CONV):
+        kept = jnp.where(place >= lag, grad, 0.0)
+        sums_ref[lag : lag + 1] = jnp.sum(kept * pltpu.roll(inputs, lag, 0), axis=0, keepdims=True)
+        total = total + pltpu.roll(channel_ref[lag : lag + 1] * kept, rows - lag, 0)
+    sums_ref[CONV + 1 :] = jnp.zeros((7 - CONV, LANES), jnp.float32)
+    low_ref[...] = total.astype(jnp.bfloat16)
+
+
+def conv_backward(part, scan, grad, pre, mixed, place, channels):
+    rows, width = pre.shape
+    spec = pl.BlockSpec((rows, LANES), lambda i: (0, i))
+    few = pl.BlockSpec((8, LANES), lambda i: (0, i))
+    return pl.pallas_call(
+        conv_back_kernel,
+        grid=(width // LANES,),
+        in_specs=[spec] * 5 + [pl.BlockSpec((rows, LANES), lambda i: (0, 0)), few],
+        out_specs=[spec, few],
+        out_shape=[
+            jax.ShapeDtypeStruct((rows, width), jnp.bfloat16),
+            jax.ShapeDtypeStruct((8, width), jnp.float32),
+        ],
+        compiler_params=pltpu.CompilerParams(vmem_limit_bytes=24 * 2**20),
+        name="conv_backward",
+    )(part, scan, grad, pre, mixed, place, channels)
 
 
 def adam_kernel(
@@ -790,7 +898,8 @@
     )
     gain_cols = whole_small(norm_gains.astype(jnp.float32).T, ranks)
     mixer_pack = jnp.concatenate(
-        [deal_columns(mixer_in, here, groups, part_inner, wide_inner), table_part], axis=1
+        [deal_columns(mixer_in, here, groups, part_inner, wide_inner), table_part, qkv_weight],
+        axis=1,
     )
     mixer_early = whole(mixer_pack)
     lengths_all = jnp.concatenate(spread_direct(lengths, groups), axis=0)
@@ -809,43 +918,60 @@
     scale_in = rms_scale(inputs)
     normed = (inputs * scale_in * gain_cols[0]).astype(low)
     normed_all, near_rows = spread(after(normed, mixer_pack), groups)
-    attn_rows = beside(spread_direct(attn_weight, groups), here)
-    dealt_mix = deal_rows(after(mixer_out, near_rows), here, groups, wide_inner)
     dealt_up = deal_columns(after(ffn_in, near_rows), here, groups, part_hidden, wide_hidden)
-    mixer_full = after(mixer_early, normed_all, dealt_mix, dealt_up)
+    dealt_rows = jnp.concatenate(
+        [
+            beside(spread_direct(attn_weight, groups), here),
+            deal_rows(after(mixer_out, near_rows), here, groups, wide_inner),
+            deal_rows(after(ffn_out, near_rows), here, groups, wide_hidden),
+        ],
+        axis=0,
+    )
+    mixer_full, normed_all, dealt_up, dealt_rows = lax.optimization_barrier(
+        (mixer_early, normed_all, dealt_up, dealt_rows)
+    )
     weight_in = mixer_full[:, : 2 * inner]
-    table_low = mixer_full[:, 2 * inner :].reshape(ranks, part_model, 2 * LANES)[:, :part_inner]
+    weight_qkv = mixer_full[:, 2 * inner + 2 * LANES :]
+    table_low = mixer_full[:, 2 * inner : 2 * inner + 2 * LANES].reshape(ranks, part_model, 2 * LANES)[:, :part_inner]
     table_low = jnp.pad(
         table_low[:, :, :table_width], ((0, 0), (0, wide_inner - part_inner), (0, 0))
     ).reshape(inner, table_width)
 
-    heads_full = whole(jnp.concatenate([after(qkv_weight, mixer_full), attn_rows], axis=1))
-    weight_qkv, weight_attn = heads_full[:, :qkv_width], heads_full[:, qkv_width:]
+    rows_full = whole(dealt_rows).reshape(ranks, -1, model_width)
+    mix_end = part_model + wide_inner
+    weight_attn = rows_full[:, :part_model].reshape(model_width, model_width)
+    weight_mix = rows_full[:, part_model:mix_end].reshape(inner, model_width)
+    weight_down = rows_full[:, mix_end:].reshape(hidden_units, model_width)
     grad_out = cotangent.astype(jnp.float32) * live_rows[:, None]
 
     mixed = product(normed_all, weight_in)
-    weight_mix, weight_up = whole(after(dealt_mix, mixed)), whole(after(dealt_up, mixed))
-    xin = mixed[:, :inner]
-    gate_z = mixed[:, inner:]
+    mixed, dealt_up = lax.optimization_barrier((mixed, dealt_up))
+    weight_up = whole(dealt_up)
     table = table_low.astype(jnp.float32)
-    tap_masks = [(offset_all >= lag).astype(jnp.float32)[:, None] for lag in range(CONV)]
-    taps = [shift_rows(xin, lag) * tap_masks[lag] for lag in range(CONV)]
-    conv_pre = table[:, CONV]
-    for lag in range(CONV):
-        conv_pre = conv_pre + table[:, lag] * taps[lag]
-    conv_low = silu_act(conv_pre).astype(low)
-    conv_out = conv_low.astype(jnp.float32)
+    channels = jnp.pad(table[:, : CONV + 3].T, ((0, 5 - CONV), (0, 0)))
+    place = jnp.broadcast_to(offset_all[:, None], (offset_all.shape[0], LANES))
+    conv_pre, conv_out, conv_low = conv_forward(mixed, place, channels)
     proj_start = CONV + 3 + STATE
     input_proj = table_low[:, proj_start : proj_start + RANK + 2 * STATE]
     step_proj = table_low[:, proj_start + RANK + 2 * STATE :]
     double_part = product_tt(input_proj, conv_low)
     double = everywhere(double_part, groups)
-    dealt_down = deal_rows(after(ffn_out, double), here, groups, wide_hidden)
-    weight_down = whole(dealt_down)
 
     heads_part = product(after(normed_all, double_part), weight_qkv).astype(low)
     heads_part = after(heads_part, double)
     heads_low = beside(exchange(row_pieces(heads_part, groups)), here)
+    rank_part = double[:RANK].astype(low)
+    inject = double[RANK : RANK + STATE]
+    readout = double[RANK + STATE :]
+    dt_pre = product_tt(rank_part, step_proj) + table[:, CONV + 1]
+    step_size = jnp.log1p(jnp.exp(dt_pre))
+    rates = -jnp.exp(table[:, CONV + 3 : CONV + 3 + STATE]).T
+    scanned, gated_low, block_begins, inject_wide, readout_wide = scan_forward(
+        block_keep, step_size, conv_out, inject, readout, rates, mixed, channels
+    )
+    gated_low, heads_low, grad_ffn_pieces = lax.optimization_barrier(
+        (gated_low, heads_low, spread_direct(after(grad_out.astype(low), double), groups))
+    )
     kv_width = KV * HEAD
     query = heads_low[:, :model_width].reshape(buffer_rows, KV, GROUP, HEAD)
     key_rows = heads_low[:, model_width : model_width + kv_width].reshape(buffer_rows, KV, HEAD)
@@ -871,20 +997,6 @@
     attn_raw = product(context, weight_attn)
     scale_attn = rms_scale(attn_raw)
 
-    rank_part = double[:RANK].astype(low)
-    inject = double[RANK : RANK + STATE]
-    readout = double[RANK + STATE :]
-    dt_pre = product_tt(rank_part, step_proj) + table[:, CONV + 1]
-    step_size = jnp.log1p(jnp.exp(dt_pre))
-    rates = -jnp.exp(table[:, CONV + 3 : CONV + 3 + STATE]).T
-    states_out, block_begins, inject_wide, readout_wide = scan_forward(
-        block_keep, step_size, conv_out, inject, readout, rates
-    )
-    skip_weight = table[:, CONV + 2]
-    scanned = states_out + skip_weight * conv_out
-    silu_z = silu_act(gate_z)
-    gated_low = (scanned * silu_z).astype(low)
-    gated_low = after(gated_low, heads_low, dealt_down)
     mamba_raw = collect(row_pieces(product(gated_low, weight_mix).astype(low), groups))
     mamba_raw = after(mamba_raw, attn_raw)
     scale_mamba = rms_scale(mamba_raw)
@@ -895,9 +1007,7 @@
     normed_two = (hidden * scale_hidden * gain_cols[3]).astype(low)
 
     normed_two_all, _ = spread(normed_two, groups)
-    grad_ffn_pieces = spread_direct(after(grad_out.astype(low), normed_two_all), groups)
     both = product(normed_two_all, weight_up)
-    both, grad_ffn_pieces = lax.optimization_barrier((both, grad_ffn_pieces))
     grad_ffn_all = jnp.concatenate(grad_ffn_pieces, axis=0)
     gate_ffn = both[:, :hidden_units]
     up_ffn = both[:, hidden_units:]
@@ -917,7 +1027,7 @@
     half_grad = 0.5 * grad_hidden
     grad_mamba_full, gain_two = rms_back(mamba_raw, scale_mamba, gain_cols[2], half_grad)
     grad_mamba_all, _ = spread(grad_mamba_full.astype(low), groups)
-    up_own, down_own = owned_sum(grad_up_w), owned_sum(grad_down_w)
+    up_own = owned_sum(grad_up_w)
 
     grad_attn_full, gain_one = rms_back(attn_raw, scale_attn, gain_cols[1], half_grad)
     grad_attn_low = grad_attn_full.astype(low)
@@ -953,43 +1063,47 @@
         ],
         axis=1,
     ).astype(low)
-    grad_heads_part = jnp.concatenate(exchange(apart(grad_heads, here, groups)), axis=0)
-
-    grad_mamba_all = after(grad_mamba_all, grad_heads)
+    head_pieces = exchange(apart(grad_heads, here, groups))
+
+    grad_attn_w = product_tn(context, grad_attn_low).astype(low)
+    grad_mamba_all, grad_heads, grad_attn_w = lax.optimization_barrier(
+        (grad_mamba_all, grad_heads, grad_attn_w)
+    )
+    down_own, attn_own = owned_sum(grad_down_w), owned_sum(grad_attn_w)
     grad_gated = product_nt(grad_mamba_all, weight_mix)
-    grad_scanned = grad_gated * silu_z
-    grad_gate_low = (grad_gated * scanned * silu_slope(gate_z)).astype(low)
     grad_mix_w = product_tn(gated_low, grad_mamba_all).astype(low)
-    grad_gate_w = product_tn(normed_all, grad_gate_low).astype(low)
-    mix_own, gate_own = owned_sum(grad_mix_w), owned_sum(grad_gate_w)
-    heads_pack = jnp.concatenate(
-        [
-            product_tn(normed_all, grad_heads_part).astype(low),
-            product_tn(context, grad_attn_low).astype(low),
-        ],
-        axis=1,
-    )
-    heads_own = owned_sum(heads_pack)
-    raw_pieces = row_pieces(product(after(act_low, grad_gate_w), weight_down).astype(low), groups)
-    grad_scanned, raw_pieces = after(
-        (grad_scanned, raw_pieces), grad_mix_w, grad_gate_w, heads_pack
-    )
+    raw_pieces = row_pieces(product(after(act_low, grad_gated), weight_down).astype(low), groups)
+    grad_gated, raw_pieces, grad_mix_w = lax.optimization_barrier(
+        (grad_gated, raw_pieces, grad_mix_w)
+    )
+    mix_own = owned_sum(grad_mix_w)
     raw_hops = first_hop(raw_pieces)
-    grad_skip = jnp.sum(grad_scanned * conv_out, axis=0)
-    grad_step, grad_conv_scan, grad_inject, grad_readout, grad_rates = scan_backward(
+    (
+        grad_scanned,
+        grad_gate_low,
+        grad_pre_low,
+        grad_conv_scan,
+        grad_inject,
+        grad_readout,
+        grad_rates,
+        scan_sums,
+    ) = scan_backward(
         block_keep,
         step_size,
         conv_out,
         inject_wide,
         readout_wide,
         rates,
-        grad_scanned,
+        grad_gated,
+        mixed,
+        scanned,
+        dt_pre,
         block_begins,
     )
-    grad_step = after(grad_step, up_own, raw_hops)
-    grad_pre = grad_step * sigmoid(dt_pre)
-    grad_step_bias = jnp.sum(grad_pre, axis=0)
-    grad_pre_low = grad_pre.astype(low)
+    grad_pre_low, raw_hops, head_pieces = lax.optimization_barrier(
+        (grad_pre_low, raw_hops, head_pieces)
+    )
+    grad_heads_part = jnp.concatenate(head_pieces, axis=0)
     grad_rank = product_tt(step_proj, grad_pre_low)
     grad_double = everywhere(
         jnp.concatenate([grad_rank, grad_inject, grad_readout], axis=0), groups
@@ -998,21 +1112,27 @@
     raw_hops = after(raw_hops, grad_double)
     ffn_raw = second_hop(raw_pieces, raw_hops)
     output = (live_rows[:, None] * (hidden + ffn_raw)).astype(low)
-    grad_conv_out = (
-        product_tt(grad_double, input_proj) + grad_conv_scan + skip_weight * grad_scanned
-    )
-    grad_conv_out = after(grad_conv_out, down_own, mix_own)
-    grad_conv = grad_conv_out * silu_slope(conv_pre)
-    grad_xin = unshift_rows(grad_conv * tap_masks[0] * table[:, 0], 0)
-    for lag in range(1, CONV):
-        grad_xin = grad_xin + unshift_rows(grad_conv * tap_masks[lag] * table[:, lag], lag)
-    grad_xin_low = grad_xin.astype(low)
+    side_pack = jnp.concatenate(
+        [
+            product_tn(normed_all, grad_heads_part).astype(low),
+            product_tn(normed_all, grad_gate_low).astype(low),
+        ],
+        axis=1,
+    )
+    side_pack, grad_double = lax.optimization_barrier((side_pack, grad_double))
+    side_own = owned_sum(side_pack)
+    conv_part = product_tt(grad_double, input_proj)
+    conv_part, up_own, down_own, attn_own = lax.optimization_barrier(
+        (conv_part, up_own, down_own, attn_own)
+    )
+    grad_xin_low, conv_sums = conv_backward(
+        conv_part, grad_conv_scan, grad_scanned, conv_pre, mixed, place, channels
+    )
     grad_table = jnp.concatenate(
         [
-            jnp.stack(
-                [jnp.sum(grad_conv * taps[lag], axis=0) for lag in range(CONV)]
-                + [jnp.sum(grad_conv, axis=0), grad_step_bias, grad_skip]
-            ),
+            conv_sums[: CONV + 1],
+            scan_sums[1:2],
+            scan_sums[0:1],
             grad_rates * rates,
             product(grad_double, conv_low),
             product(rank_part, grad_pre_low),
@@ -1027,15 +1147,25 @@
     xin_pack = jnp.concatenate(
         [product_tn(normed_all, grad_xin_low).astype(low), grad_table], axis=1
     )
-    xin_pack = after(xin_pack, gate_own)
+    xin_pack, mix_own = lax.optimization_barrier((xin_pack, mix_own))
     last_own = owned_sum(xin_pack)
     normed_part = (
         product_nt(grad_heads_part, weight_qkv)
         + product_nt(grad_gate_low, weight_in[:, inner:])
         + product_nt(after(grad_xin_low, xin_pack), weight_in[:, :inner])
-    ).astype(low)
+    )
+    gain_zero = jnp.sum(normed_part * normed_all.astype(jnp.float32), axis=0) / gain_cols[0]
+    normed_part, up_own = lax.optimization_barrier((normed_part.astype(low), up_own))
+    if groups == 4:
+        runs = 2 * ranks // groups
+        starts = lambda i: [(i * runs + r) * wide_hidden for r in range(runs)]
+        up_pieces = exchange(split_columns(up_own, here, starts, part_hidden))
+    else:
+        up_pieces = return_columns(up_own, here, groups, part_hidden, wide_hidden)
+    up_done = join_back(up_pieces, here, part_hidden) if groups == 4 else up_pieces
     grad_normed = collect(row_pieces(normed_part, groups))
-    back_inputs, gain_zero = rms_back(inputs, scale_in, gain_cols[0], grad_normed)
+    grad_normed, side_own = lax.optimization_barrier((grad_normed, side_own))
+    back_inputs, _ = rms_back(inputs, scale_in, gain_cols[0], grad_normed)
     grad_tokens = grad_hidden + back_inputs
     grad_gains = everyone(jnp.stack([gain_zero, gain_one, gain_two, gain_three], axis=0), groups, ranks)
     grad_gains_done = lax.dynamic_slice_in_dim(
@@ -1043,9 +1173,9 @@
     ).T
 
     last_own = lax.optimization_barrier(last_own)
-    heads_own = lax.optimization_barrier(heads_own)
+    side_own = lax.optimization_barrier(side_own)
     grad_in_done = return_columns(
-        jnp.concatenate([last_own[:, :inner], gate_own], axis=1),
+        jnp.concatenate([last_own[:, :inner], side_own[:, qkv_width:]], axis=1),
         here,
         groups,
         part_inner,
@@ -1056,14 +1186,14 @@
         grad_table_done = join_rows(table_pieces, here)[:, :table_width]
     else:
         grad_table_done = jnp.concatenate(table_pieces, axis=0)[:, :table_width]
-    grad_qkv_done = heads_own[:, :qkv_width]
+    grad_qkv_done = side_own[:, :qkv_width]
     grad_attn_done = sum(
         piece.astype(jnp.float32)
-        for piece in exchange(apart(heads_own[:, qkv_width:], here, groups))
+        for piece in exchange(apart(attn_own, here, groups))
     )
     grad_mix_done = return_rows(after(mix_own, normed_part), here, groups, part_inner)
     ffn_done = (
-        return_columns(after(up_own, normed_part), here, groups, part_hidden, wide_hidden),
+        up_done,
         return_rows(after(down_own, normed_part), here, groups, part_hidden),
     )
 

time: 805 us -> 803 us (level)
  other arithmetic: 84.7 us -> 55.9 us
  Pallas kernels: 135 us -> 157 us
  local copies, waits for them, and re-layouts: 86.8 us -> 108 us
  waiting for transfers between devices: 172 us -> 159 us
    ppermute x91, waiting for transfers between devices: 157 us -> 132 us  [swap(): return lax.ppermute(values, 'dp', [(i, i ^ bit) for i in range(4)])]
    convert_element_type x3 -> x0, other arithmetic: 15.4 us -> none  [the longest x1 9.33 us: shards(): conv_out = conv_low.astype(jnp.float32)]
    reduce_sum x3 -> x1, other arithmetic: 16.5 us -> 1.75 us  [rms_back(): inner_mean = jnp.mean(weighted * values, axis=-1, keepdims=True)]
    unnamed x308 -> x325, local copies, waits for them, and re-layouts: 45.3 us -> 59.9 us
    pallas_call x0 -> x2, Pallas kernels: none -> 13.9 us  [the longest x1 9.3 us: conv_backward(): pl.pallas_call(conv_back_kernel, grid=(width // LANES,), in_specs=[spec]...]
    all_gather x5 -> x3, waiting for transfers between devices: 5.86 us -> 15 us  [whole(): return lax.all_gather(shard, 'shard', axis=0, tiled=True)]
  transfers between devices with their start and end apart: 108 -> 106, of which waited for: 49 -> 42; matrix products, arithmetic and copies ran while one was open for 36% -> 30% of each run, Pallas kernels for 16% -> 19%
where the time goes in v3:
time: 803 us; the launch traced here: 792 us
  matrix products  182 us (23%)
  waiting for transfers between devices  159 us (20%)
  Pallas kernels  157 us (20%)
  starting transfers between devices  113 us (14%)
  local copies, waits for them, and re-layouts  108 us (13%)
  other arithmetic  55.9 us (7%)
  between operations  17.5 us (2%)
    ppermute x91, waiting for transfers between devices, swap(): return lax.ppermute(values, 'dp', [(i, i ^ bit) for i in range(4)])  132 us
    ppermute x91, starting transfers between devices, swap(): return lax.ppermute(values, 'dp', [(i, i ^ bit) for i in range(4)])  106 us
    pallas_call x1, Pallas kernels, scan_backward(): pl.pallas_call(back_kernel, grid_spec=pltpu.PrefetchScalarGridSpec(num_sc...  69.9 us
    unnamed x325, local copies, waits for them, and re-layouts  59.9 us
    dot_general x7, matrix products, product_nt(): lax.dot_general(left, right, (((1,), (1,)), ((), ())), preferred_element_...  58.5 us
    dot_general x8, matrix products, product(): return jnp.dot(left, right, preferred_element_type=jnp.float32)  51.9 us
    dot_general x7, matrix products, product_tn(): lax.dot_general(left, right, (((0,), (0,)), ((), ())), preferred_element_...  49.8 us
    pallas_call x1, Pallas kernels, scan_forward(): pl.pallas_call(scan_kernel, grid_spec=pltpu.PrefetchScalarGridSpec(num_sc...  37 us
  transfers between devices with their start and end apart: 106, of which 42 were waited for; matrix products, arithmetic and copies ran while one was open for 30% of the time, Pallas kernels for 19%

profile of v3, /device:TPU:0, one launch (start us, length us, event | category | flops | bytes accessed | tf_op | source)
XLA Modules:
  0.0 792.2 jit_solution(3642104659718662526)
XLA Ops:
  42.7 20.5 %collective-permute-done.18.refs_3_ = bf16[200,400]{1,0:T(8,128)(2,1)S(1)} collective-permute-done((bf16[200,400]{1,0:T(8,128)(2,1)S(1)}, bf16[200,400]{1,0:T(8,128)(2,1)S(1)}, u32[]{:S(2)}, u32[]{:S(2)}) %collective-permute-start.18) | collective-permute-done | bytes 160032 | tf_op jit(solution)/shard_map/ppermute | solution.py:666
  93.2 10.1 %collective-permute-done.14.refs_2_ = bf16[200,688]{1,0:T(8,128)(2,1)S(1)} collective-permute-done((bf16[200,688]{1,0:T(8,128)(2,1)}, bf16[200,688]{1,0:T(8,128)(2,1)S(1)}, u32[]{:S(2)}, u32[]{:S(2)}) %collective-permute-start.14) | collective-permute-done | bytes 275232 | tf_op jit(solution)/shard_map/ppermute | solution.py:666
  115.9 12.9 %fusion.4.mixed_ref.gate_ref = f32[1024,1792]{1,0:T(8,128)} fusion(bf16[1024,1600]{0,1:T(8,128)(2,1)} %constant_dynamic-update-slice_fusion, bf16[1600,2608]{1,0:T(8,128)(2,1)} %all-gather.4.cloned.1.call-done), kind=kOutput, calls=%fused_computation.19 | convolution fusion | flops 5872025600 | bytes 16351232 | tf_op jit(solution)/shard_map/dot_general | solution.py:32
  176.7 37.0 %state_scan.1 = (f32[1024,896]{1,0:T(8,128)S(1)}, bf16[1024,896]{1,0:T(8,128)(2,1)S(1)}, f32[8,16,896]{2,1,0:T(8,128)S(1)}, f32[1024,16,128]{2,1,0:T(8,128)S(1)}, f32[1024,16,128]{2,1,0:T(8,128)}) custom-call(f32[8]{0:T(128)S(1)} %sub.133.keep_ref, f32[1024,896]{1,0:T(8,128)S(1)} %get-tuple-element.438.step_ref, ...), custom_call_target="tpu_custom_call" | custom-call | flops 440401920 | bytes 128450560 | tf_op jit(solution)/shard_map/state_scan/pallas_call | solution.py:174
  248.7 9.5 %collective-permute-done.39 = bf16[128,1600]{0,1:T(8,128)(2,1)S(1)} collective-permute-done((bf16[128,1600]{0,1:T(8,128)(2,1)S(1)}, bf16[128,1600]{0,1:T(8,128)(2,1)S(1)}, u32[]{:S(2)}, u32[]{:S(2)}) %collective-permute-start.39) | collective-permute-done | bytes 409632 | tf_op jit(solution)/shard_map/ppermute | solution.py:666
  287.7 5.9 collective-permute-done.42
  305.3 13.0 %all-gather.8.cloned.1.call-done = bf16[1600,2816]{1,0:T(8,128)(2,1)} async-done(((bf16[200,2816]{1,0:T(8,128)(2,1)}), bf16[1600,2816]{1,0:T(8,128)(2,1)}) %all-gather.8.cloned.1.call-update) | async-done | bytes 9011216 | tf_op jit(solution)/shard_map/all_gather | solution.py:839
  318.3 17.8 %fusion.90 = f32[1024,2816]{1,0:T(8,128)} fusion(bf16[1024,1600]{0,1:T(8,128)(2,1)} %constant_dynamic-update-slice_fusion.9, bf16[1600,2816]{1,0:T(8,128)(2,1)} %all-gather.8.cloned.1.call-done), kind=kOutput, calls=%fused_computation.276 | convolution fusion | flops 9227468800 | bytes 23822336 | tf_op jit(solution)/shard_map/dot_general | solution.py:32
  336.1 14.4 %multiply_convert_fusion.2 = (bf16[1024,1408]{1,0:T(8,128)(2,1)S(1)}, bf16[1024,1408]{1,0:T(8,128)(2,1)}, bf16[1024,1408]{1,0:T(8,128)(2,1)}) fusion(f32[1024,2816]{1,0:T(8,128)} %fusion.90, bf16[1024,1600]{0,1:T(8,128)(2,1)} %constant_dynamic-update-slice_fusion.5, bf16[1408,1600]{1,0:T(8,128)(2,1)} %bitcast.175), kind=kOutput, calls=%fused_computation.16 | convolution fusion | flops 4635361280 | bytes 27967488 | tf_op jit(solution)/shard_map/dot_general | solution.py:42
  350.5 11.9 %convolution_convert_fusion.4 = bf16[1024,1600]{0,1:T(8,128)(2,1)S(1)} fusion(bf16[1600,2816]{1,0:T(8,128)(2,1)S(1)} %bitcast.197, bf16[1024,1408]{1,0:T(8,128)(2,1)} %get-tuple-element.360, bf16[1024,1408]{1,0:T(8,128)(2,1)S(1)} %get-tuple-element.359), kind=kOutput, calls=%fused_computation.24 | convolution fusion | flops 9240641536 | bytes 18055168 | tf_op jit(solution)/shard_map/dot_general | solution.py:42
  366.3 14.5 %convolution_convert_fusion = bf16[1600,2816]{1,0:T(8,128)(2,1)} fusion(bf16[1024,1600]{0,1:T(8,128)(2,1)} %constant_dynamic-update-slice_fusion.9, bf16[1024,1408]{1,0:T(8,128)(2,1)S(1)} %copy-done.146, bf16[1024,1408]{1,0:T(8,128)(2,1)S(1)} %get-tuple-element.359), kind=kOutput, calls=%fused_computation | convolution fusion | flops 9243508736 | bytes 18055168 | tf_op jit(solution)/shard_map/dot_general | solution.py:36
  383.8 10.3 %convolution_convert_fusion.1 = bf16[1408,1600]{1,0:T(8,128)(2,1)} fusion(bf16[1024,1408]{1,0:T(8,128)(2,1)} %get-tuple-element.227, bf16[1024,1600]{0,1:T(8,128)(2,1)} %constant_dynamic-update-slice_fusion.5), kind=kOutput, calls=%fused_computation.1 | convolution fusion | flops 4615987200 | bytes 10665984 | tf_op jit(solution)/shard_map/dot_general | solution.py:36
  401.4 5.6 collective-permute-done.45
  407.4 7.1 collective-permute-done.47
  442.1 5.4 convolution_convert_fusion.2
  462.1 8.7 %fusion.91.gated_ref = f32[1024,896]{1,0:T(8,128)} fusion(bf16[1024,1600]{0,1:T(8,128)(2,1)} %constant_dynamic-update-slice_fusion.14, bf16[896,1600]{1,0:T(8,128)(2,1)} %bitcast.180), kind=kOutput, calls=%fused_computation.277 | convolution fusion | flops 2936012800 | bytes 9814016 | tf_op jit(solution)/shard_map/dot_general | solution.py:42
  470.9 7.9 convolution_convert_fusion.3
  497.0 69.9 %state_back.1 = (f32[1024,896]{1,0:T(8,128)}, bf16[1024,896]{1,0:T(8,128)(2,1)S(1)}, bf16[1024,896]{1,0:T(8,128)(2,1)S(1)}, f32[1024,896]{1,0:T(8,128)}, f32[16,...) custom-call(f32[8]{0:T(128)S(1)} %copy-done.58, ...), custom_call_target="tpu_custom_call" | custom-call | flops 880803840 | bytes 238551040 | tf_op jit(solution)/shard_map/state_back/pallas_call | solution.py:350
  607.7 8.9 %fusion.10 = f32[1024,1600]{0,1:T(8,128)} fusion(bf16[1024,896]{1,0:T(8,128)(2,1)} %copy-done.59, bf16[1600,2608]{1,0:T(8,128)(2,1)} %all-gather.4.cloned.1.call-done), kind=kOutput, calls=%fused_computation.42 | convolution fusion | flops 2936012800 | bytes 11255808 | tf_op jit(solution)/shard_map/dot_general | solution.py:42
  633.1 9.3 %conv_backward.1 = (bf16[1024,896]{1,0:T(8,128)(2,1)S(1)}, f32[8,896]{1,0:T(8,128)S(1)}) custom-call(f32[1024,896]{1,0:T(8,128)S(1)} %copy-done.3, f32[1024,896]{1,0:T(8,128)S(1)} %copy-done.16, f32[1024,896]{1,0:T(8,128)S(1)} %copy-done.15, f32[1024,896]{1,0:T(8,128)S(1)} %copy-done.14, f32[1024,1792]{1,0:T(8,128)S(1)} %copy-done.1, ...), custom_call_target="tpu_custom_call" | custom-call | tf_op jit(solution)/shard_map/conv_backward/pallas_call | solution.py:448
  646.9 5.8 convolution_convert_fusion.6
  657.6 5.6 fusion.8
  663.3 7.3 multiply_reduce_fusion
  715.8 6.9 collective-permute-done.96.refs_3_
  (763 shorter events, 448.5 us)
Async XLA Ops:
  7.2 102.5 %all-gather.4.cloned.1.call-start = ((), (), s32[]{:S(2)}) async-start(), calls=%async_computation.6 | async-start | bytes 9676800 | tf_op jit(solution)/shard_map/all_gather | solution.py:839
  25.5 207.7 %all-gather.6.cloned.1.call-start = ((), (), s32[]{:S(2)}) async-start(), calls=%async_computation.7 | async-start | bytes 14616576 | tf_op jit(solution)/shard_map/all_gather | solution.py:839
  37.1 29.5 %collective-permute-start.10 = (bf16[256,1600]{0,1:T(8,128)(2,1)S(1)}, bf16[256,1600]{0,1:T(8,128)(2,1)S(1)}, u32[]{:S(2)}, u32[]{:S(2)}) collective-permute-start(bf16[256,1600]{0,1:T(8,128)(2,1)S(1)} %fusion.19), channel_id=1, source_target_pairs={{0,16},{8,24},{16,0},{24,8},{1,17},{9,25},{17,1},{25,9},{2,18},{10... | collective-permute-start | bytes 2457608 | tf_op jit(solution)/shard_map/ppermute | solution.py:666
  109.8 208.5 %all-gather.8.cloned.1.call-start = ((), (), s32[]{:S(2)}) async-start(), calls=%async_computation.8 | async-start | bytes 10137600 | tf_op jit(solution)/shard_map/all_gather | solution.py:839
  128.9 492.7 %reduce-scatter.13.cloned.1.call-start = ((), (), s32[]{:S(2)}) async-start(), calls=%async_computation.10 | async-start | bytes 5271552 | tf_op jit(solution)/shard_map/reduce_scatter | solution.py:843
  161.8 58.4 %collective-permute-start.34 = (bf16[256,1600]{0,1:T(8,128)(2,1)}, bf16[256,1600]{0,1:T(8,128)(2,1)S(1)}, u32[]{:S(2)}, u32[]{:S(2)}) collective-permute-start(bf16[256,1600]{0,1:T(8,128)(2,1)} %fusion.26), channel_id=1, source_target_pairs={{0,24},{8,16},{16,8},{24,0},{1,25},{9,17},{17,9},{25,1},{2,26},{10... | collective-permute-start | bytes 2457608 | tf_op jit(solution)/shard_map/ppermute | solution.py:666
  163.3 57.8 %collective-permute-start.33 = (bf16[256,1600]{0,1:T(8,128)(2,1)}, bf16[256,1600]{0,1:T(8,128)(2,1)S(1)}, u32[]{:S(2)}, u32[]{:S(2)}) collective-permute-start(bf16[256,1600]{0,1:T(8,128)(2,1)} %fusion.26), channel_id=1, source_target_pairs={{0,16},{8,24},{16,0},{24,8},{1,17},{9,25},{17,1},{25,9},{2,18},{10... | collective-permute-start | bytes 2457608 | tf_op jit(solution)/shard_map/ppermute | solution.py:666
  165.8 56.2 %collective-permute-start.32 = (bf16[256,1600]{0,1:T(8,128)(2,1)}, bf16[256,1600]{0,1:T(8,128)(2,1)S(1)}, u32[]{:S(2)}, u32[]{:S(2)}) collective-permute-start(bf16[256,1600]{0,1:T(8,128)(2,1)} %fusion.26), channel_id=1, source_target_pairs={{0,8},{8,0},{16,24},{24,16},{1,9},{9,1},{17,25},{25,17},{2,10},{10... | collective-permute-start | bytes 2457608 | tf_op jit(solution)/shard_map/ppermute | solution.py:666
  165.9 53.2 %collective-permute-start.30 = (bf16[256,560]{1,0:T(8,128)(2,1)S(1)}, bf16[256,560]{1,0:T(8,128)(2,1)S(1)}, u32[]{:S(2)}, u32[]{:S(2)}) collective-permute-start(bf16[256,560]{1,0:T(8,128)(2,1)S(1)} %get-tuple-element.395), channel_id=1, source_target_pairs={{0,16},{8,24},{16,0},{24,8},{1,17},{9,25},{17,1},{25,9},{2,18},{10... | collective-permute-start | bytes 860168 | tf_op jit(solution)/shard_map/ppermute | solution.py:666
  171.9 47.1 %collective-permute-start.29 = (bf16[256,560]{1,0:T(8,128)(2,1)S(1)}, bf16[256,560]{1,0:T(8,128)(2,1)S(1)}, u32[]{:S(2)}, u32[]{:S(2)}) collective-permute-start(bf16[256,560]{1,0:T(8,128)(2,1)S(1)} %get-tuple-element.396), channel_id=1, source_target_pairs={{0,8},{8,0},{16,24},{24,16},{1,9},{9,1},{17,25},{25,17},{2,10},{10... | collective-permute-start | bytes 860168 | tf_op jit(solution)/shard_map/ppermute | solution.py:666
  394.1 227.4 %reduce-scatter.19.cloned.1.call-start = ((), (), s32[]{:S(2)}) async-start(), calls=%async_computation.13 | async-start | bytes 5990400
  461.5 160.1 %reduce-scatter.11.cloned.1.call-start = ((), (), s32[]{:S(2)}) async-start(), calls=%async_computation.9 | async-start | bytes 10137600 | tf_op jit(solution)/shard_map/reduce_scatter | solution.py:843
  462.1 195.5 %reduce-scatter.15.cloned.1.call-start = ((), (), s32[]{:S(2)}) async-start(), calls=%async_computation.11 | async-start | bytes 3354624 | tf_op jit(solution)/shard_map/reduce_scatter | solution.py:843
  487.9 272.4 %reduce-scatter.17.cloned.1.call-start = ((), (), s32[]{:S(2)}) async-start(), calls=%async_computation.12 | async-start | bytes 5529600 | tf_op jit(solution)/shard_map/reduce_scatter | solution.py:843
  488.9 78.1 %collective-permute-start.59 = (bf16[256,560]{1,0:T(8,128)(2,1)S(1)}, bf16[256,560]{1,0:T(8,128)(2,1)S(1)}, u32[]{:S(2)}, u32[]{:S(2)}) collective-permute-start(bf16[256,560]{1,0:T(8,128)(2,1)S(1)} %get-tuple-element.239), channel_id=1, source_target_pairs={{0,8},{8,0},{16,24},{24,16},{1,9},{9,1},{17,25},{25,17},{2,10},{10... | collective-permute-start | bytes 860168 | tf_op jit(solution)/shard_map/ppermute | solution.py:666
  489.9 77.7 %collective-permute-start.60 = (bf16[256,560]{1,0:T(8,128)(2,1)S(1)}, bf16[256,560]{1,0:T(8,128)(2,1)S(1)}, u32[]{:S(2)}, u32[]{:S(2)}) collective-permute-start(bf16[256,560]{1,0:T(8,128)(2,1)S(1)} %get-tuple-element.240), channel_id=1, source_target_pairs={{0,16},{8,24},{16,0},{24,8},{1,17},{9,25},{17,1},{25,9},{2,18},{10... | collective-permute-start | bytes 860168 | tf_op jit(solution)/shard_map/ppermute | solution.py:666
  491.4 82.2 %collective-permute-start.61 = (bf16[256,560]{1,0:T(8,128)(2,1)S(1)}, bf16[256,560]{1,0:T(8,128)(2,1)S(1)}, u32[]{:S(2)}, u32[]{:S(2)}) collective-permute-start(bf16[256,560]{1,0:T(8,128)(2,1)S(1)} %get-tuple-element.241), channel_id=1, source_target_pairs={{0,24},{8,16},{16,8},{24,0},{1,25},{9,17},{17,9},{25,1},{2,26},{10... | collective-permute-start | bytes 860168 | tf_op jit(solution)/shard_map/ppermute | solution.py:666
  494.5 79.0 %collective-permute-start.58 = (bf16[128,1600]{0,1:T(8,128)(2,1)S(1)}, bf16[128,1600]{0,1:T(8,128)(2,1)S(1)}, u32[]{:S(2)}, u32[]{:S(2)}) collective-permute-start(bf16[128,1600]{0,1:T(8,128)(2,1)S(1)} %slice.483), channel_id=1, source_target_pairs={{0,16},{8,24},{16,0},{24,8},{1,17},{9,25},{17,1},{25,9},{2,18},{10... | collective-permute-start | bytes 1228808 | tf_op jit(solution)/shard_map/ppermute | solution.py:666
  495.8 77.8 %collective-permute-start.57 = (bf16[128,1600]{0,1:T(8,128)(2,1)S(1)}, bf16[128,1600]{0,1:T(8,128)(2,1)S(1)}, u32[]{:S(2)}, u32[]{:S(2)}) collective-permute-start(bf16[128,1600]{0,1:T(8,128)(2,1)S(1)} %slice.482), channel_id=1, source_target_pairs={{0,8},{8,0},{16,24},{24,16},{1,9},{9,1},{17,25},{25,17},{2,10},{10... | collective-permute-start | bytes 1228808 | tf_op jit(solution)/shard_map/ppermute | solution.py:666
  603.2 160.2 %reduce-scatter.21.cloned.1.call-start = ((), (), s32[]{:S(2)}) async-start(), calls=%async_computation.14 | async-start | bytes 4147200
  723.5 33.8 %collective-permute-start.68 = (bf16[128,1600]{0,1:T(8,128)(2,1)}, bf16[128,1600]{0,1:T(8,128)(2,1)}, u32[]{:S(2)}, u32[]{:S(2)}) collective-permute-start(bf16[128,1600]{0,1:T(8,128)(2,1)} %get-tuple-element.364), channel_id=1, source_target_pairs={{0,8},{8,0},{16,24},{24,16},{1,9},{9,1},{17,25},{25,17},{2,10},{10... | collective-permute-start | bytes 1228808 | tf_op jit(solution)/shard_map/ppermute | solution.py:666
  725.5 31.8 %collective-permute-start.71 = (bf16[128,1600]{0,1:T(8,128)(2,1)}, bf16[128,1600]{0,1:T(8,128)(2,1)}, u32[]{:S(2)}, u32[]{:S(2)}) collective-permute-start(bf16[128,1600]{0,1:T(8,128)(2,1)} %get-tuple-element.366), channel_id=1, source_target_pairs={{0,16},{8,24},{16,0},{24,8},{1,17},{9,25},{17,1},{25,9},{2,18},{10... | collective-permute-start | bytes 1228808 | tf_op jit(solution)/shard_map/ppermute | solution.py:666
  726.9 30.5 %collective-permute-start.70 = (bf16[128,1600]{0,1:T(8,128)(2,1)}, bf16[128,1600]{0,1:T(8,128)(2,1)}, u32[]{:S(2)}, u32[]{:S(2)}) collective-permute-start(bf16[128,1600]{0,1:T(8,128)(2,1)} %get-tuple-element.368), channel_id=1, source_target_pairs={{0,16},{8,24},{16,0},{24,8},{1,17},{9,25},{17,1},{25,9},{2,18},{10... | collective-permute-start | bytes 1228808 | tf_op jit(solution)/shard_map/ppermute | solution.py:666
  728.6 28.7 %collective-permute-start.73 = (bf16[128,1600]{0,1:T(8,128)(2,1)}, bf16[128,1600]{0,1:T(8,128)(2,1)}, u32[]{:S(2)}, u32[]{:S(2)}) collective-permute-start(bf16[128,1600]{0,1:T(8,128)(2,1)} %get-tuple-element.369), channel_id=1, source_target_pairs={{0,8},{8,0},{16,24},{24,16},{1,9},{9,1},{17,25},{25,17},{2,10},{10... | collective-permute-start | bytes 1228808 | tf_op jit(solution)/shard_map/ppermute | solution.py:666
  (237 other events, 2869.9 us)
Sparse Core Ops, SparseCore 0:
  25.6 84.1 all-gather.3
  112.0 118.5 all-gather.5
  232.8 85.4 all-gather.7
  394.3 51.5 reduce-scatter.12
  461.6 59.1 reduce-scatter.18
  522.9 94.6 reduce-scatter.10
  620.1 37.4 reduce-scatter.14
  659.9 57.4 reduce-scatter.16
  719.7 43.6 reduce-scatter.20
